TPU v7x, 32 devices: a whole 2x2x4 slice. The times are simulated.
32 devices in a mesh: wide: 16 (over z, y, core), narrow: 2 (over x).
Axes of the slice: x: 2, y: 2, z: 4, core: 2. Of those that a mesh axis runs over, the one named last changes fastest.
Arguments:
- hidden: bfloat16 [16384, 768], P('wide'), may hold values from -6 to 6
- encoded: bfloat16 [24576, 768], P('wide'), may hold values from -6 to 6
- retrieved: int32 [128, 8], P('wide'), may hold values from 0 to 191, as said below
- self_query: bfloat16 [768, 768], P(None, 'narrow'), may hold values from -0.21875 to 0.21875
- self_key: bfloat16 [768, 768], P(None, 'narrow'), may hold values from -0.21875 to 0.21875
- self_value: bfloat16 [768, 768], P(None, 'narrow'), may hold values from -0.21875 to 0.21875
- self_out: bfloat16 [768, 768], P('narrow'), may hold values from -1.25 to 1.25
- cross_query: bfloat16 [768, 768], P(None, 'narrow'), may hold values from -0.21875 to 0.21875
- cross_key: bfloat16 [768, 768], P(None, 'narrow'), may hold values from -0.21875 to 0.21875
- cross_value: bfloat16 [768, 768], P(None, 'narrow'), may hold values from -0.21875 to 0.21875
- cross_out: bfloat16 [768, 768], P('narrow'), may hold values from -1.75 to 1.75
- expand_weight: bfloat16 [768, 3072], P(None, 'narrow'), may hold values from -0.21875 to 0.21875
- reduce_weight: bfloat16 [3072, 768], P('narrow'), may hold values from -0.109375 to 0.109375
- first_gain: float32 [768], replicated, may hold values from 0.5 to 1.5
- first_shift: float32 [768], replicated, may hold values from -1.5 to 1.5
- second_gain: float32 [768], replicated, may hold values from 0.5 to 1.5
- second_shift: float32 [768], replicated, may hold values from -1.5 to 1.5
- third_gain: float32 [768], replicated, may hold values from 0.5 to 1.5
- third_shift: float32 [768], replicated, may hold values from -1.5 to 1.5
- cotangent: bfloat16 [16384, 768], P('wide'), may hold values from -6 to 6
Outputs:
- output: bfloat16 [16384, 768], P('wide')
- hidden_grad: float32 [16384, 768], P('wide')
- self_query_grad: float32 [768, 768], P(None, 'narrow')
- self_key_grad: float32 [768, 768], P(None, 'narrow')
- self_value_grad: float32 [768, 768], P(None, 'narrow')
- self_out_grad: float32 [768, 768], P('narrow')
- cross_query_grad: float32 [768, 768], P(None, 'narrow')
- cross_key_grad: float32 [768, 768], P(None, 'narrow')
- cross_value_grad: float32 [768, 768], P(None, 'narrow')
- cross_out_grad: float32 [768, 768], P('narrow')
- expand_grad: float32 [768, 3072], P(None, 'narrow')
- reduce_grad: float32 [3072, 768], P('narrow')
- first_gain_grad: float32 [768], replicated
- first_shift_grad: float32 [768], replicated
- second_gain_grad: float32 [768], replicated
- second_shift_grad: float32 [768], replicated
- third_gain_grad: float32 [768], replicated
- third_shift_grad: float32 [768], replicated
Inputs may be any that keep to these rules, and one draw needn't show every extreme that they name: `retrieved`: each row names 8 different encoder blocks. Encoder block e belongs to index e // 12 of wide. The rows of one index of wide name at most 8 blocks of any one index, and in every draw some index of wide has exactly 8 of its blocks named by the rows of every index.
All inputs are finite; a program needn't handle non-finite values.
Results may differ from a plain program's by a relative error of at most 0.025.
Values may be sent and summed in bfloat16 or wider, within the bound.
A program may use at most 320 MiB of HBM per device.

v0:
```python
import jax
import jax.numpy as jnp
from jax import lax
from jax.sharding import PartitionSpec as P

HEAD_DIM = 64
BLOCK_ROWS = 128
RET_BLOCKS = 8


epsilon = 1e-05


def norm_forward(summed, norm_gain, norm_shift):
    average = jnp.mean(summed, axis=-1, keepdims=True)
    centred = summed - average
    inverse = lax.rsqrt(jnp.mean(centred * centred, axis=-1, keepdims=True) + epsilon)
    normal = centred * inverse
    return (normal * norm_gain + norm_shift, normal, inverse)


def norm_backward(grad_out, normal, inverse, norm_gain):
    scaled = grad_out * norm_gain
    grad_in = inverse * (
        scaled
        - jnp.mean(scaled, axis=-1, keepdims=True)
        - normal * jnp.mean(scaled * normal, axis=-1, keepdims=True)
    )
    return (grad_in, jnp.sum(grad_out * normal, axis=0), jnp.sum(grad_out, axis=0))


def gelu_slope(pre_act):
    return (
        0.5 * (1.0 + lax.erf(pre_act * 0.7071067811865476))
        + pre_act * jnp.exp(-0.5 * pre_act * pre_act) * 0.3989422804014327
    )


def attend(queries, key_rows, value_rows, allowed):
    factor = HEAD_DIM ** (-0.5)
    scores = (
        jnp.einsum("bqhd,bkhd->bhqk", queries, key_rows, preferred_element_type=jnp.float32)
        * factor
    )
    scores = jnp.where(allowed, scores, -1e30)
    row_max = jnp.max(scores, axis=-1, keepdims=True)
    raised = jnp.exp(scores - row_max)
    row_sum = jnp.sum(raised, axis=-1, keepdims=True)
    chances = raised / row_sum
    blended = jnp.einsum(
        "bhqk,bkhd->bqhd",
        chances.astype(jnp.bfloat16),
        value_rows,
        preferred_element_type=jnp.float32,
    )
    return (blended.astype(jnp.bfloat16), row_max + jnp.log(row_sum))


def attend_back(queries, key_rows, value_rows, allowed, log_total, grad_blend):
    factor = HEAD_DIM ** (-0.5)
    scores = (
        jnp.einsum("bqhd,bkhd->bhqk", queries, key_rows, preferred_element_type=jnp.float32)
        * factor
    )
    scores = jnp.where(allowed, scores, -1e30)
    chances = jnp.exp(scores - log_total)
    grad_values = jnp.einsum(
        "bhqk,bqhd->bkhd",
        chances.astype(jnp.bfloat16),
        grad_blend,
        preferred_element_type=jnp.float32,
    )
    grad_chance = jnp.einsum(
        "bqhd,bkhd->bhqk", grad_blend, value_rows, preferred_element_type=jnp.float32
    )
    centre = jnp.sum(grad_chance * chances, axis=-1, keepdims=True)
    grad_scores = (chances * (grad_chance - centre)).astype(jnp.bfloat16)
    grad_queries = (
        jnp.einsum("bhqk,bkhd->bqhd", grad_scores, key_rows, preferred_element_type=jnp.float32)
        * factor
    )
    grad_keys = (
        jnp.einsum("bhqk,bqhd->bkhd", grad_scores, queries, preferred_element_type=jnp.float32)
        * factor
    )
    return (grad_queries, grad_keys, grad_values)


def project(rows_in, weight):
    return jnp.dot(rows_in, weight, preferred_element_type=jnp.float32)


def grad_weight(left, right):
    return jnp.einsum("ti,to->io", left, right, preferred_element_type=jnp.float32)


def grad_input(grad_rows, weight):
    return jnp.einsum("to,io->ti", grad_rows, weight, preferred_element_type=jnp.float32)


def split_weight(rows_low, grads_float):
    upper = grads_float.astype(jnp.bfloat16)
    lower = (grads_float - upper.astype(jnp.float32)).astype(jnp.bfloat16)
    return grad_weight(rows_low, upper) + grad_weight(rows_low, lower)


def narrow_sum(partial_value):
    return lax.psum(partial_value, "narrow")


def narrow_back(partial_value):
    return lax.psum(partial_value.astype(jnp.bfloat16), "narrow").astype(jnp.float32)


def local(
    hidden,
    encoded,
    retrieved,
    self_query,
    self_key,
    self_value,
    self_out,
    cross_query,
    cross_key,
    cross_value,
    cross_out,
    expand_weight,
    reduce_weight,
    first_gain,
    first_shift,
    second_gain,
    second_shift,
    third_gain,
    third_shift,
    cotangent,
):
    tok_rows = hidden.shape[0]
    width = self_query.shape[1]
    local_heads = width // HEAD_DIM
    hidden_float = hidden.astype(jnp.float32)

    def split_heads(flat, leading):
        return flat.reshape(leading, -1, local_heads, HEAD_DIM)

    query_self = project(hidden, self_query).astype(jnp.bfloat16)
    key_self = project(hidden, self_key).astype(jnp.bfloat16)
    value_self = project(hidden, self_value).astype(jnp.bfloat16)
    row_index = lax.broadcasted_iota(jnp.int32, (tok_rows, tok_rows), 0)
    col_index = lax.broadcasted_iota(jnp.int32, (tok_rows, tok_rows), 1)
    causal = (col_index <= row_index)[None, None]
    blend_self, log_self = attend(
        split_heads(query_self, 1), split_heads(key_self, 1), split_heads(value_self, 1), causal
    )
    blend_self = blend_self.reshape(tok_rows, width)
    self_result = narrow_sum(project(blend_self, self_out))
    first, first_normal, first_inverse = norm_forward(
        hidden_float + self_result, first_gain, first_shift
    )
    first_low = first.astype(jnp.bfloat16)
    query_cross = project(first_low, cross_query).astype(jnp.bfloat16)
    wanted_flat = retrieved.reshape(-1)
    live = wanted_flat.shape[0]
    query_blocks = live // RET_BLOCKS
    blocks_dev = encoded.shape[0] // BLOCK_ROWS
    peers = lax.axis_size("wide")
    capacity = max(2, 2 * live // peers)
    owners = wanted_flat // blocks_dev
    local_block = wanted_flat % blocks_dev
    order = jnp.arange(live, dtype=jnp.int32)
    earlier = jnp.sum(
        ((owners[None, :] == owners[:, None]) & (order[None, :] < order[:, None])).astype(
            jnp.int32
        ),
        axis=1,
    )
    slot_of = owners * capacity + earlier
    slot_ids = jnp.arange(peers * capacity, dtype=jnp.int32)
    table = (
        jnp.sum(
            jnp.where(slot_ids[None, :] == slot_of[:, None], local_block[:, None] + 1, 0), axis=0
        )
        - 1
    )
    requests = lax.all_to_all(
        table.reshape(peers, capacity), "wide", split_axis=0, concat_axis=0, tiled=True
    )
    present = (requests >= 0)[:, :, None, None]
    fetch_ids = jnp.maximum(requests, 0).reshape(-1)
    key_enc = project(encoded, cross_key).astype(jnp.bfloat16)
    value_enc = project(encoded, cross_value).astype(jnp.bfloat16)
    stacked = jnp.concatenate([key_enc, value_enc], 1).reshape(blocks_dev, BLOCK_ROWS, 2 * width)
    outgoing = jnp.where(
        present,
        jnp.take(stacked, fetch_ids, axis=0).reshape(peers, capacity, BLOCK_ROWS, 2 * width),
        jnp.zeros((), jnp.bfloat16),
    )
    arrived = lax.all_to_all(outgoing, "wide", split_axis=0, concat_axis=0, tiled=True)
    fetched = jnp.take(arrived.reshape(peers * capacity, BLOCK_ROWS, 2 * width), slot_of, axis=0)
    fetched = fetched.reshape(live * BLOCK_ROWS, 2 * width)
    key_cross = fetched[:, :width]
    value_cross = fetched[:, width:]
    heads_query = split_heads(query_cross, query_blocks)
    heads_key = split_heads(key_cross, query_blocks)
    heads_value = split_heads(value_cross, query_blocks)
    blend_cross, log_cross = attend(heads_query, heads_key, heads_value, True)
    blend_cross = blend_cross.reshape(tok_rows, width)
    cross_result = narrow_sum(project(blend_cross, cross_out))
    second, second_normal, second_inverse = norm_forward(
        first + cross_result, second_gain, second_shift
    )
    second_low = second.astype(jnp.bfloat16)
    pre_act = project(second_low, expand_weight)
    activated = jax.nn.gelu(pre_act, approximate=False).astype(jnp.bfloat16)
    ffn_result = narrow_sum(project(activated, reduce_weight))
    final, third_normal, third_inverse = norm_forward(second + ffn_result, third_gain, third_shift)
    output = final.astype(jnp.bfloat16)
    grad_final = cotangent.astype(jnp.float32)
    grad_third, third_gain_grad, third_shift_grad = norm_backward(
        grad_final, third_normal, third_inverse, third_gain
    )
    grad_ffn = grad_third.astype(jnp.bfloat16)
    reduce_grad = grad_weight(activated, grad_ffn)
    grad_pre = (grad_input(grad_ffn, reduce_weight) * gelu_slope(pre_act)).astype(jnp.bfloat16)
    expand_grad = grad_weight(second_low, grad_pre)
    grad_second = grad_third + narrow_back(grad_input(grad_pre, expand_weight))
    grad_second_in, second_gain_grad, second_shift_grad = norm_backward(
        grad_second, second_normal, second_inverse, second_gain
    )
    grad_cross = grad_second_in.astype(jnp.bfloat16)
    cross_out_grad = grad_weight(blend_cross, grad_cross)
    grad_blend_cross = grad_input(grad_cross, cross_out).astype(jnp.bfloat16)
    grad_query_cross, grad_key_cross, grad_value_cross = attend_back(
        heads_query,
        heads_key,
        heads_value,
        True,
        log_cross,
        split_heads(grad_blend_cross, query_blocks),
    )
    grad_query_cross = grad_query_cross.reshape(tok_rows, width).astype(jnp.bfloat16)
    cross_query_grad = grad_weight(first_low, grad_query_cross)
    grad_key_flat = grad_key_cross.reshape(live * BLOCK_ROWS, width)
    grad_value_flat = grad_value_cross.reshape(live * BLOCK_ROWS, width)
    slot_grads = jnp.concatenate([grad_key_flat, grad_value_flat], 1).reshape(
        live, BLOCK_ROWS, 2 * width
    )
    grad_slots = (
        jnp.zeros((peers * capacity, BLOCK_ROWS, 2 * width), jnp.float32)
        .at[slot_of]
        .set(slot_grads)
    )
    returned = lax.all_to_all(
        grad_slots.reshape(peers, capacity, BLOCK_ROWS, 2 * width).astype(jnp.bfloat16),
        "wide",
        split_axis=0,
        concat_axis=0,
        tiled=True,
    ).astype(jnp.float32)
    pick_table = (
        requests.reshape(-1)[:, None] == jnp.arange(blocks_dev, dtype=jnp.int32)[None, :]
    ).astype(jnp.bfloat16)
    block_grads = split_weight(pick_table, returned.reshape(peers * capacity, -1))
    block_grads = block_grads.reshape(blocks_dev * BLOCK_ROWS, 2 * width)
    cross_key_grad = split_weight(encoded, block_grads[:, :width])
    cross_value_grad = split_weight(encoded, block_grads[:, width:])
    grad_first = grad_second_in + narrow_back(grad_input(grad_query_cross, cross_query))
    grad_first_in, first_gain_grad, first_shift_grad = norm_backward(
        grad_first, first_normal, first_inverse, first_gain
    )
    grad_self = grad_first_in.astype(jnp.bfloat16)
    self_out_grad = grad_weight(blend_self, grad_self)
    grad_blend_self = grad_input(grad_self, self_out).astype(jnp.bfloat16)
    grad_query_self, grad_key_self, grad_value_self = attend_back(
        split_heads(query_self, 1),
        split_heads(key_self, 1),
        split_heads(value_self, 1),
        causal,
        log_self,
        split_heads(grad_blend_self, 1),
    )
    grad_key_self = grad_key_self.reshape(tok_rows, width).astype(jnp.bfloat16)
    grad_value_self = grad_value_self.reshape(tok_rows, width).astype(jnp.bfloat16)
    grad_query_self = grad_query_self.reshape(tok_rows, width).astype(jnp.bfloat16)
    self_query_grad = grad_weight(hidden, grad_query_self)
    self_key_grad = grad_weight(hidden, grad_key_self)
    self_value_grad = grad_weight(hidden, grad_value_self)
    grad_hidden = grad_first_in + narrow_back(
        grad_input(grad_query_self, self_query)
        + grad_input(grad_key_self, self_key)
        + grad_input(grad_value_self, self_value)
    )
    summed_grads = lax.psum(
        (
            self_query_grad,
            self_key_grad,
            self_value_grad,
            self_out_grad,
            cross_query_grad,
            cross_key_grad,
            cross_value_grad,
            cross_out_grad,
            expand_grad,
            reduce_grad,
            first_gain_grad,
            first_shift_grad,
            second_gain_grad,
            second_shift_grad,
            third_gain_grad,
            third_shift_grad,
        ),
        "wide",
    )
    return (output, grad_hidden) + tuple(summed_grads)


def solution(mesh):
    return jax.shard_map(
        local,
        mesh=mesh,
        in_specs=(
            P("wide", None),
            P("wide", None),
            P("wide", None),
            P(None, "narrow"),
            P(None, "narrow"),
            P(None, "narrow"),
            P("narrow", None),
            P(None, "narrow"),
            P(None, "narrow"),
            P(None, "narrow"),
            P("narrow", None),
            P(None, "narrow"),
            P("narrow", None),
            P(),
            P(),
            P(),
            P(),
            P(),
            P(),
            P("wide", None),
        ),
        out_specs=(
            P("wide", None),
            P("wide", None),
            P(None, "narrow"),
            P(None, "narrow"),
            P(None, "narrow"),
            P("narrow", None),
            P(None, "narrow"),
            P(None, "narrow"),
            P(None, "narrow"),
            P("narrow", None),
            P(None, "narrow"),
            P("narrow", None),
            P(),
            P(),
            P(),
            P(),
            P(),
            P(),
        ),
        check_vma=False,
    )
```

profile of v0, /device:TPU:0, one launch (start us, length us, event | category | flops | bytes accessed | tf_op | source)
XLA Modules:
  0.0 2237.9 jit_solution(17378687458921364556)
XLA Ops:
  40.4 21.8 select_select_fusion
  109.3 86.2 %all-reduce.10.cloned.1.call-done = f32[1024,768]{1,0:T(8,128)} async-done(((f32[1024,768]{1,0:T(8,128)}), f32[1024,768]{1,0:T(8,128)}) %all-reduce.10.cloned.1.call-update) | async-done | bytes 3145744 | tf_op jit(solution)/shard_map/psum | solution.py:108
  204.5 306.7 %all-to-all-done.1 = bf16[16,8,128,768]{3,2,1,0:T(8,128)(2,1)} async-done(((bf16[16,8,128,768]{3,2,1,0:T(8,128)(2,1)}), bf16[16,8,128,768]{3,2,1,0:T(8,128)(2,1)}, u32[]{:S(2)}, u32[]{:S(2)}) %all-to-all-start.1) | async-done | bytes 25165856 | tf_op jit(solution)/shard_map/all_to_all | solution.py:197
  526.8 15.9 copy.154
  592.8 17.5 fusion.61
  614.5 185.1 %all-reduce.12.cloned.1.call-done = f32[1024,768]{1,0:T(8,128)} async-done(((f32[1024,768]{1,0:T(8,128)}), f32[1024,768]{1,0:T(8,128)}) %all-reduce.12.cloned.1.call-update) | async-done | bytes 3145744 | tf_op jit(solution)/shard_map/psum | solution.py:108
  804.2 17.3 fusion.15
  827.4 85.9 %all-reduce.14.cloned.1.call-done = f32[1024,768]{1,0:T(8,128)} async-done(((f32[1024,768]{1,0:T(8,128)}), f32[1024,768]{1,0:T(8,128)}) %all-reduce.14.cloned.1.call-update) | async-done | bytes 3145744 | tf_op jit(solution)/shard_map/psum | solution.py:108
  933.5 51.6 %all-reduce.16.cloned.1.call-done = bf16[1024,768]{1,0:T(8,128)(2,1)} async-done(((bf16[1024,768]{1,0:T(8,128)(2,1)}), bf16[1024,768]{1,0:T(8,128)(2,1)}) %all-reduce.16.cloned.1.call-update) | async-done | bytes 1572880 | tf_op jit(solution)/shard_map/psum | solution.py:112
  1008.5 26.6 %multiply_reduce_fusion.1 = (f32[8,6,128]{2,1,0:T(8,128)S(1)}, f32[8,6,128,1024]{3,2,1,0:T(8,128)}) fusion(f32[8,6,128,1024]{3,2,1,0:T(8,128)} %get-tuple-element.159, f32[8,6,128]{2,1,0:T(8,128)S(1)} %log_add_fusion.1, bf16[8,1024,6,64]{1,0,3,2:T(8,128)(2,1)} %bitcast.180, bf16[8,128,6,64]{1,0,3,2:T(8,128)(2,1)S(1)} %bitcast.184), kind=kOutput, calls=%fused_computation.10 | convolution fusion | flops 830466048 | bytes 57458688 | tf_op jit(solution)/shard_map/bqhd,bkhd->bhqk/dot_general | solution.py:73
  1035.1 16.5 copy.171
  1065.2 16.7 multiply_convert_fusion.1
  1092.3 16.5 copy.169
  1122.4 18.5 pad_maximum_fusion
  1140.9 24.8 %copy.172 = f32[64,128,768]{2,1,0:T(8,128)} copy(f32[64,128,768]{1,0,2:T(8,128)} %pad_maximum_fusion) | data formatting | bytes 50331648 | tf_op jit(solution)/shard_map/concatenate | solution.py:244
  1165.7 16.3 broadcast_in_dim.120
  1182.0 51.3 %scatter_fusion = f32[128,128,768]{2,1,0:T(8,128)} fusion(f32[128,128,768]{2,1,0:T(8,128)} %broadcast_in_dim.120, s32[64]{0:T(128)S(1)} %copy-done.78, f32[64,128,768]{2,1,0:T(8,128)} %copy.172), kind=kCustom, calls=%fused_computation.2 | custom fusion | bytes 75497728 | tf_op jit(solution)/shard_map/scatter | solution.py:250
  1233.3 25.9 %convert_element_type.238 = bf16[128,128,768]{2,1,0:T(8,128)(2,1)} convert(f32[128,128,768]{2,1,0:T(8,128)} %scatter_fusion) | non-fusion elementwise | flops 12582912 | bytes 75497472 | tf_op jit(solution)/shard_map/convert_element_type | solution.py:253
  1300.9 35.3 %all-reduce.18.cloned.1.call-done = bf16[1024,768]{1,0:T(8,128)(2,1)} async-done(((bf16[1024,768]{1,0:T(8,128)(2,1)}), bf16[1024,768]{1,0:T(8,128)(2,1)}) %all-reduce.18.cloned.1.call-update) | async-done | bytes 1572880 | tf_op jit(solution)/shard_map/psum | solution.py:112
  1361.4 17.1 multiply_convert_fusion
  1422.3 285.4 %all-to-all-done.2 = bf16[16,8,128,768]{3,2,1,0:T(8,128)(2,1)} async-done(((bf16[16,8,128,768]{3,2,1,0:T(8,128)(2,1)}), bf16[16,8,128,768]{3,2,1,0:T(8,128)(2,1)}, u32[]{:S(2)}, u32[]{:S(2)}) %all-to-all-start.2) | async-done | bytes 25165856 | tf_op jit(solution)/shard_map/all_to_all | solution.py:252
  1707.8 26.2 %copy.188 = bf16[16,8,128,768]{3,1,2,0:T(8,128)(2,1)} copy(bf16[16,8,128,768]{3,2,1,0:T(8,128)(2,1)} %all-to-all-done.2) | data formatting | bytes 50331648
  1776.0 164.0 %all-reduce = (f32[768]{0:T(1024)}, f32[768]{0:T(1024)}, f32[768]{0:T(1024)}, f32[768]{0:T(1024)}, f32[768]{0:T(1024)}, /*index=5*/f32[768]{0:T(1024)}) all-reduce(f32[768]{0:T(1024)S(1)} %get-tuple-element.110, f32[768]{0:T(1024)S(1)} %get-tuple-element.117, ...), channel_id=1, replica_groups=mesh['wide'=16,'narrow'=2] {'wide'}, use_global_device_ids=true, to_apply=%region_38.39 | all-reduce | flops 4608 | bytes 36864 | tf_op jit(solution)/shard_map/psum | solution.py:292
  1944.7 265.8 %all-reduce.22.cloned.1.call-done = (f32[768,384]{0,1:T(8,128)}, f32[768,384]{0,1:T(8,128)}, f32[768,384]{0,1:T(8,128)}, f32[384,768]{1,0:T(8,128)}, f32[768,384...) async-done(((f32[768,384]{0,1:T(8,128)}, f32[768,384]{0,1:T(8,128)}, ...) | async-done | bytes 18874384 | tf_op jit(solution)/shard_map/psum | solution.py:292
  (334 shorter events, 427.6 us)
Async XLA Ops:
  7.2 796.8 %copy-start = (bf16[768,1536]{1,0:T(8,128)(2,1)S(1)}, bf16[768,1536]{1,0:T(8,128)(2,1)}, u32[]{:S(2)}) copy-start(bf16[768,1536]{1,0:T(8,128)(2,1)} %param.31) | copy-start | bytes 7077892
  10.1 17.5 all-to-all-start
  62.2 449.0 %all-to-all-start.1 = ((bf16[16,8,128,768]{3,2,1,0:T(8,128)(2,1)}), bf16[16,8,128,768]{3,2,1,0:T(8,128)(2,1)}, u32[]{:S(2)}, u32[]{:S(2)}) async-start(bf16[16,8,128,768]{3,2,1,0:T(8,128)(2,1)} %select_select_fusion), calls=%async_computation.1 | async-start | bytes 50331648 | tf_op jit(solution)/shard_map/all_to_all | solution.py:197
  68.4 127.1 %all-reduce.10.cloned.1.call-start = ((), (), s32[]{:S(2)}) async-start(), calls=%async_computation.3 | async-start | bytes 6291456 | tf_op jit(solution)/shard_map/psum | solution.py:108
  73.1 20.9 copy-start.46
  108.2 691.4 %all-reduce.12.cloned.1.call-start = ((), (), s32[]{:S(2)}) async-start(), calls=%async_computation.4 | async-start | bytes 6291456 | tf_op jit(solution)/shard_map/psum | solution.py:108
  198.3 601.3 %copy-start.55 = (f32[1024]{0:T(1024)}, f32[1024]{0:T(1024)S(1)}, u32[]{:S(2)}) copy-start(f32[1024]{0:T(1024)S(1)} %broadcast_multiply_fusion.8) | copy-start | bytes 12292
  199.0 600.6 %copy-start.59 = (f32[1024]{0:T(1024)}, f32[1024]{0:T(1024)S(1)}, u32[]{:S(2)}) copy-start(f32[1024]{0:T(1024)S(1)} %add_rsqrt_fusion.2) | copy-start | bytes 12292
  204.5 363.0 %copy-start.22 = (bf16[48,8,8,128]{3,2,1,0:T(8,128)(2,1)}, bf16[48,8,8,128]{3,2,1,0:T(8,128)(2,1)S(1)}, u32[]{:S(2)}) copy-start(bf16[48,8,8,128]{3,2,1,0:T(8,128)(2,1)S(1)} %copy.183) | copy-start | bytes 2359300
  592.8 19.0 copy-start.33
  614.4 298.8 %all-reduce.14.cloned.1.call-start = ((), (), s32[]{:S(2)}) async-start(), calls=%async_computation.5 | async-start | bytes 6291456 | tf_op jit(solution)/shard_map/psum | solution.py:108
  803.4 18.1 copy-start.9
  803.4 186.6 %copy-start.61 = (f32[1024]{0:T(1024)}, f32[1024]{0:T(1024)S(1)}, u32[]{:S(2)}) copy-start(f32[1024]{0:T(1024)S(1)} %broadcast_multiply_fusion.7) | copy-start | bytes 12292
  804.2 185.8 %copy-start.67 = (f32[1024]{0:T(1024)}, f32[1024]{0:T(1024)S(1)}, u32[]{:S(2)}) copy-start(f32[1024]{0:T(1024)S(1)} %add_rsqrt_fusion.1) | copy-start | bytes 12292
  804.2 18.9 copy-start.82
  827.3 157.8 %all-reduce.16.cloned.1.call-start = ((), (), s32[]{:S(2)}) async-start(), calls=%async_computation.6 | async-start | bytes 3145728 | tf_op jit(solution)/shard_map/psum | solution.py:112
  1065.2 21.2 copy-start.23
  1259.2 448.5 %all-to-all-start.2 = ((bf16[16,8,128,768]{3,2,1,0:T(8,128)(2,1)}), bf16[16,8,128,768]{3,2,1,0:T(8,128)(2,1)}, u32[]{:S(2)}, u32[]{:S(2)}) async-start(bf16[16,8,128,768]{3,2,1,0:T(8,128)(2,1)} %bitcast.173), calls=%async_computation.2 | async-start | bytes 50331648 | tf_op jit(solution)/shard_map/all_to_all | solution.py:252
  1265.0 71.3 %all-reduce.18.cloned.1.call-start = ((), (), s32[]{:S(2)}) async-start(), calls=%async_computation.7 | async-start | bytes 3145728 | tf_op jit(solution)/shard_map/psum | solution.py:112
  1284.3 655.7 %all-reduce.20.cloned.1.call-start = ((), (), s32[]{:S(2)}) async-start(), calls=%async_computation.8 | async-start | bytes 3145728 | tf_op jit(solution)/shard_map/psum | solution.py:112
  1299.0 37.2 %copy-start.56 = (f32[1024]{0:T(1024)S(1)}, f32[1024]{0:T(1024)}, u32[]{:S(2)}) copy-start(f32[1024]{0:T(1024)} %copy-done.55) | copy-start | bytes 12292
  1299.0 37.2 %copy-start.60 = (f32[1024]{0:T(1024)S(1)}, f32[1024]{0:T(1024)}, u32[]{:S(2)}) copy-start(f32[1024]{0:T(1024)} %copy-done.59) | copy-start | bytes 12292
  1299.1 37.2 %copy-start.66 = (f32[768]{0:T(1024)S(1)}, f32[768]{0:T(1024)}, u32[]{:S(2)}) copy-start(f32[768]{0:T(1024)} %param.33) | copy-start | bytes 9220
  1412.6 797.8 %all-reduce.22.cloned.1.call-start = ((), (), s32[]{:S(2)}) async-start(), calls=%async_computation.9 | async-start | bytes 37748736 | tf_op jit(solution)/shard_map/psum | solution.py:292
  (80 other events, 406.4 us)
Sparse Core Ops, SparseCore 0:
  108.4 87.0 all-reduce.9
  614.6 184.9 all-reduce.11
  827.5 85.7 all-reduce.13
  933.6 51.4 all-reduce.15
  1284.4 51.8 all-reduce.17
  1412.7 51.4 all-reduce.19
  1775.4 434.9 all-reduce.21
where the time goes:
time: 2250 us; the launch traced here: 2240 us
  waiting for transfers between devices  1300 us (58%)
  local copies, waits for them, and re-layouts  300 us (13%)
  matrix products  270 us (12%)
  other arithmetic  166 us (7%)
  blocking collectives  164 us (7%)
    psum x3, waiting for transfers between devices, narrow_sum(): return lax.psum(partial_value, 'narrow')  357 us
    all_to_all x1, waiting for transfers between devices, local(): lax.all_to_all(outgoing, 'wide', split_axis=0, concat_axis=0, tiled=True)  307 us
    all_to_all x1, waiting for transfers between devices, local(): lax.all_to_all(grad_slots.reshape(peers, capacity, BLOCK_ROWS, 2 * width)...  285 us
    psum x1, waiting for transfers between devices, local(): lax.psum((self_query_grad, self_key_grad, self_value_grad, self_out_grad,...  266 us
    psum x1, blocking collectives, local(): lax.psum((self_query_grad, self_key_grad, self_value_grad, self_out_grad,...  164 us
    unnamed x203, local copies, waits for them, and re-layouts  88.4 us
    psum x3, waiting for transfers between devices, narrow_back(): lax.psum(partial_value.astype(jnp.bfloat16), 'narrow').astype(jnp.float32)  87 us
    dot_general x14, matrix products, grad_weight(): jnp.einsum('ti,to->io', left, right, preferred_element_type=jnp.float32)  61.2 us
  transfers between devices with their start and end apart: 10, of which 8 were waited for; matrix products, arithmetic and copies ran while one was open for 11% of the time, Pallas kernels for 0%

commit v1 on v0

v1 whole, which is shorter than its diff:
```python
import functools

import jax
import jax.numpy as jnp
from jax import lax
from jax.experimental import pallas as pl
from jax.experimental.pallas import tpu as pltpu
from jax.sharding import PartitionSpec as P

HEAD_DIM = 64
BLOCK_ROWS = 128
RET_BLOCKS = 8
PAIR = 2 * HEAD_DIM
VMEM_LIMIT = 56 << 20

epsilon = 1e-05
bf16 = jnp.bfloat16
f32 = jnp.float32
MESH = pl.DeviceIdType.MESH


def norm_forward(summed, norm_gain, norm_shift):
    average = jnp.mean(summed, axis=-1, keepdims=True)
    centred = summed - average
    inverse = lax.rsqrt(jnp.mean(centred * centred, axis=-1, keepdims=True) + epsilon)
    normal = centred * inverse
    return (normal * norm_gain + norm_shift, normal, inverse)


def norm_backward(grad_out, normal, inverse, norm_gain):
    scaled = grad_out * norm_gain
    grad_in = inverse * (
        scaled
        - jnp.mean(scaled, axis=-1, keepdims=True)
        - normal * jnp.mean(scaled * normal, axis=-1, keepdims=True)
    )
    return (grad_in, jnp.sum(grad_out * normal, axis=0), jnp.sum(grad_out, axis=0))


def gelu_slope(pre_act):
    return (
        0.5 * (1.0 + lax.erf(pre_act * 0.7071067811865476))
        + pre_act * jnp.exp(-0.5 * pre_act * pre_act) * 0.3989422804014327
    )


def project(rows_in, weight):
    return jnp.dot(rows_in, weight, preferred_element_type=f32)


def grad_weight(left, right):
    return jnp.einsum("ti,to->io", left, right, preferred_element_type=f32)


def grad_input(grad_rows, weight):
    return jnp.einsum("to,io->ti", grad_rows, weight, preferred_element_type=f32)


def dot_nt(left, right):
    return lax.dot_general(left, right, (((1,), (1,)), ((), ())), preferred_element_type=f32)


def dot_tn(left, right):
    return lax.dot_general(left, right, (((0,), (0,)), ((), ())), preferred_element_type=f32)


def dot_nn(left, right):
    return lax.dot_general(left, right, (((1,), (0,)), ((), ())), preferred_element_type=f32)


def stack_heads(pair_rows):
    lane = lax.broadcasted_iota(jnp.int32, pair_rows.shape, 1)
    wide_rows = pair_rows.astype(f32)
    zero = jnp.zeros_like(wide_rows)
    return jnp.concatenate(
        [
            jnp.where(lane < HEAD_DIM, wide_rows, zero).astype(bf16),
            jnp.where(lane < HEAD_DIM, zero, wide_rows).astype(bf16),
        ],
        axis=0,
    )


def merge_heads(both):
    rows = both.shape[1] // 2
    sublane = lax.broadcasted_iota(jnp.int32, (PAIR, rows), 0)
    return jnp.transpose(jnp.where(sublane < HEAD_DIM, both[:, :rows], both[:, rows:]))


def causal_edge(rows):
    key = lax.broadcasted_iota(jnp.int32, (rows, 2 * rows), 0)
    query = lax.broadcasted_iota(jnp.int32, (rows, 2 * rows), 1)
    return key <= jnp.where(query >= rows, query - rows, query)


def scaled_heads(pair_rows):
    return stack_heads(pair_rows.astype(f32) * HEAD_DIM**-0.5)


def pair_forward(queries, keys, values, edge):
    stacked = scaled_heads(queries)
    scores = dot_nt(keys, stacked)
    if edge is not None:
        split = keys.shape[0] - edge.shape[0]
        last = jnp.where(edge, scores[split:], -1e30)
        scores = jnp.concatenate([scores[:split], last], axis=0) if split else last
    top = jnp.max(scores, axis=0, keepdims=True)
    raised = jnp.exp(scores - top)
    total = jnp.sum(raised, axis=0, keepdims=True)
    blended = dot_tn(values, raised.astype(bf16)) / total
    return merge_heads(blended).astype(bf16), top + jnp.log(total)


def pair_backward(queries, keys, values, edge, log_total, blended, grad_blend):
    rows = queries.shape[0]
    stacked = scaled_heads(queries)
    grads = stack_heads(grad_blend)
    scores = dot_nt(keys, stacked)
    if edge is not None:
        split = keys.shape[0] - edge.shape[0]
        last = jnp.where(edge, scores[split:], -1e30)
        scores = jnp.concatenate([scores[:split], last], axis=0) if split else last
    chances = jnp.exp(scores - log_total)
    weighed = jnp.transpose(blended.astype(f32) * grad_blend.astype(f32))
    centre = jnp.concatenate(
        [
            jnp.sum(weighed[:HEAD_DIM], axis=0, keepdims=True),
            jnp.sum(weighed[HEAD_DIM:], axis=0, keepdims=True),
        ],
        axis=1,
    )
    grad_scores = (chances * (dot_nt(values, grads) - centre)).astype(bf16)
    grad_values = dot_nn(chances.astype(bf16), grads)
    grad_keys = dot_nn(grad_scores, stacked)
    grad_queries = merge_heads(dot_tn(keys, grad_scores)) * HEAD_DIM**-0.5
    return grad_queries, grad_keys, grad_values


def self_variants(narrow, at):
    for n in range(narrow):
        yield 0, n + 1, at == n
        yield 1, 2 * narrow - n, at == n


def self_forward_kernel(narrow, at_ref, q_ref, k_ref, v_ref, o_ref, log_ref):
    rows = q_ref.shape[0] // 2
    for chunk, seen, taken in self_variants(narrow, at_ref[0]):

        @pl.when(taken)
        def _():
            mine = pl.ds(chunk * rows, rows)
            keys = pl.ds(0, seen * rows)
            blended, log_total = pair_forward(
                q_ref[mine], k_ref[keys], v_ref[keys], causal_edge(rows)
            )
            o_ref[mine] = blended
            log_ref[0, pl.ds(chunk, 1)] = log_total


def self_forward(narrow, at, queries, keys, values):
    rows, width = queries.shape
    total_rows = keys.shape[0]
    pairs = width // PAIR
    pair = lambda count: pl.BlockSpec((count, PAIR), lambda g, at: (0, g))
    return pl.pallas_call(
        functools.partial(self_forward_kernel, narrow),
        grid_spec=pltpu.PrefetchScalarGridSpec(
            num_scalar_prefetch=1,
            grid=(pairs,),
            in_specs=[pair(rows), pair(total_rows), pair(total_rows)],
            out_specs=[pair(rows), pl.BlockSpec((1, 2, rows), lambda g, at: (g, 0, 0))],
        ),
        out_shape=[
            jax.ShapeDtypeStruct((rows, width), bf16),
            jax.ShapeDtypeStruct((pairs, 2, rows), f32),
        ],
        compiler_params=pltpu.CompilerParams(vmem_limit_bytes=VMEM_LIMIT),
        name="self_forward",
    )(at, queries, keys, values)


def self_backward_kernel(
    narrow, at_ref, q_ref, k_ref, v_ref, log_ref, o_ref, g_ref, dq_ref, dk_ref, dv_ref, dk_sum, dv_sum
):
    rows = q_ref.shape[0] // 2
    dk_sum[...] = jnp.zeros_like(dk_sum)
    dv_sum[...] = jnp.zeros_like(dv_sum)
    for chunk, seen, taken in self_variants(narrow, at_ref[0]):

        @pl.when(taken)
        def _():
            mine = pl.ds(chunk * rows, rows)
            keys = pl.ds(0, seen * rows)
            grad_q, grad_k, grad_v = pair_backward(
                q_ref[mine],
                k_ref[keys],
                v_ref[keys],
                causal_edge(rows),
                log_ref[0, pl.ds(chunk, 1)],
                o_ref[mine],
                g_ref[mine],
            )
            dq_ref[mine] = grad_q.astype(bf16)
            dk_sum[keys] += grad_k
            dv_sum[keys] += grad_v

    dk_ref[...] = dk_sum[...].astype(bf16)
    dv_ref[...] = dv_sum[...].astype(bf16)


def self_backward(narrow, at, queries, keys, values, logs, blended, grads):
    rows, width = queries.shape
    total_rows = keys.shape[0]
    pairs = width // PAIR
    pair = lambda count: pl.BlockSpec((count, PAIR), lambda g, at: (0, g))
    return pl.pallas_call(
        functools.partial(self_backward_kernel, narrow),
        grid_spec=pltpu.PrefetchScalarGridSpec(
            num_scalar_prefetch=1,
            grid=(pairs,),
            in_specs=[
                pair(rows),
                pair(total_rows),
                pair(total_rows),
                pl.BlockSpec((1, 2, rows), lambda g, at: (g, 0, 0)),
                pair(rows),
                pair(rows),
            ],
            out_specs=[pair(rows), pair(total_rows), pair(total_rows)],
            scratch_shapes=[pltpu.VMEM((total_rows, PAIR), f32)] * 2,
        ),
        out_shape=[
            jax.ShapeDtypeStruct((rows, width), bf16),
            jax.ShapeDtypeStruct((total_rows, width), bf16),
            jax.ShapeDtypeStruct((total_rows, width), bf16),
        ],
        compiler_params=pltpu.CompilerParams(vmem_limit_bytes=VMEM_LIMIT),
        name="self_backward",
    )(at, queries, keys, values, logs, blended, grads)


def cross_forward_kernel(picked_ref, *refs):
    blocks = refs[:RET_BLOCKS]
    wk_ref, wv_ref, q_ref, o_ref, log_ref, k_ref, v_ref, rows_in = refs[RET_BLOCKS:]
    for j in range(RET_BLOCKS):
        rows_in[pl.ds(j * BLOCK_ROWS, BLOCK_ROWS)] = blocks[j][...]
    k_ref[...] = dot_nn(rows_in[...], wk_ref[...]).astype(bf16)
    v_ref[...] = dot_nn(rows_in[...], wv_ref[...]).astype(bf16)
    for g in range(q_ref.shape[1] // PAIR):
        lanes = pl.ds(g * PAIR, PAIR)
        blended, log_total = pair_forward(q_ref[:, lanes], k_ref[:, lanes], v_ref[:, lanes], None)
        o_ref[:, lanes] = blended
        log_ref[0, pl.ds(g, 1)] = log_total


def block_specs(width):
    def spec(j):
        return pl.BlockSpec((BLOCK_ROWS, width), lambda b, picked: (picked[b * RET_BLOCKS + j], 0))

    return [spec(j) for j in range(RET_BLOCKS)]


def cross_forward(picked, everything, cross_key, cross_value, queries):
    rows, width = queries.shape
    count = rows // BLOCK_ROWS
    pairs = width // PAIR
    keys = RET_BLOCKS * BLOCK_ROWS
    whole = pl.BlockSpec((width, width), lambda b, picked: (0, 0))
    by_block = pl.BlockSpec((BLOCK_ROWS, width), lambda b, picked: (b, 0))
    by_keys = pl.BlockSpec((keys, width), lambda b, picked: (b, 0))
    return pl.pallas_call(
        cross_forward_kernel,
        grid_spec=pltpu.PrefetchScalarGridSpec(
            num_scalar_prefetch=1,
            grid=(count,),
            in_specs=block_specs(width) + [whole, whole, by_block],
            out_specs=[
                by_block,
                pl.BlockSpec((1, pairs, 2 * BLOCK_ROWS), lambda b, picked: (b, 0, 0)),
                by_keys,
                by_keys,
            ],
            scratch_shapes=[pltpu.VMEM((keys, width), bf16)],
        ),
        out_shape=[
            jax.ShapeDtypeStruct((rows, width), bf16),
            jax.ShapeDtypeStruct((count, pairs, 2 * BLOCK_ROWS), f32),
            jax.ShapeDtypeStruct((count * keys, width), bf16),
            jax.ShapeDtypeStruct((count * keys, width), bf16),
        ],
        compiler_params=pltpu.CompilerParams(vmem_limit_bytes=VMEM_LIMIT),
        name="cross_forward",
    )(picked, *([everything] * RET_BLOCKS), cross_key, cross_value, queries)


def cross_backward_kernel(picked_ref, *refs):
    blocks = refs[:RET_BLOCKS]
    (k_ref, v_ref, q_ref, log_ref, o_ref, g_ref, dq_ref, dwk_ref, dwv_ref, rows_in, both, sums) = refs[
        RET_BLOCKS:
    ]
    width = q_ref.shape[1]
    step = pl.program_id(0)

    @pl.when(step == 0)
    def _():
        sums[...] = jnp.zeros_like(sums)

    for j in range(RET_BLOCKS):
        rows_in[pl.ds(j * BLOCK_ROWS, BLOCK_ROWS)] = blocks[j][...]
    for g in range(width // PAIR):
        lanes = pl.ds(g * PAIR, PAIR)
        grad_q, grad_k, grad_v = pair_backward(
            q_ref[:, lanes],
            k_ref[:, lanes],
            v_ref[:, lanes],
            None,
            log_ref[0, pl.ds(g, 1)],
            o_ref[:, lanes],
            g_ref[:, lanes],
        )
        dq_ref[:, lanes] = grad_q.astype(bf16)
        both[:, lanes] = grad_k.astype(bf16)
        both[:, pl.ds(width + g * PAIR, PAIR)] = grad_v.astype(bf16)
    sums[...] += dot_tn(rows_in[...], both[...])

    @pl.when(step == pl.num_programs(0) - 1)
    def _():
        dwk_ref[...] = sums[:, :width].astype(bf16)
        dwv_ref[...] = sums[:, width:].astype(bf16)


def cross_backward(picked, everything, keys_in, values_in, queries, logs, blended, grads):
    rows, width = queries.shape
    count = rows // BLOCK_ROWS
    pairs = width // PAIR
    keys = RET_BLOCKS * BLOCK_ROWS
    whole = pl.BlockSpec((width, width), lambda b, picked: (0, 0))
    by_block = pl.BlockSpec((BLOCK_ROWS, width), lambda b, picked: (b, 0))
    by_keys = pl.BlockSpec((keys, width), lambda b, picked: (b, 0))
    return pl.pallas_call(
        cross_backward_kernel,
        grid_spec=pltpu.PrefetchScalarGridSpec(
            num_scalar_prefetch=1,
            grid=(count,),
            in_specs=block_specs(width)
            + [
                by_keys,
                by_keys,
                by_block,
                pl.BlockSpec((1, pairs, 2 * BLOCK_ROWS), lambda b, picked: (b, 0, 0)),
                by_block,
                by_block,
            ],
            out_specs=[by_block, whole, whole],
            scratch_shapes=[
                pltpu.VMEM((keys, width), bf16),
                pltpu.VMEM((keys, 2 * width), bf16),
                pltpu.VMEM((width, 2 * width), f32),
            ],
        ),
        out_shape=[
            jax.ShapeDtypeStruct((rows, width), bf16),
            jax.ShapeDtypeStruct((width, width), bf16),
            jax.ShapeDtypeStruct((width, width), bf16),
        ],
        compiler_params=pltpu.CompilerParams(vmem_limit_bytes=VMEM_LIMIT),
        name="cross_backward",
    )(
        picked,
        *([everything] * RET_BLOCKS),
        keys_in,
        values_in,
        queries,
        logs,
        blended,
        grads,
    )


COLUMNS = (0, 1, 2, 4, 5, 6, 8)


LINE = 4


class Place:
    def __init__(self):
        wide = lax.axis_index("wide")
        self.x = lax.axis_index("narrow")
        self.core = lax.rem(wide, 2)
        self.y = lax.rem(lax.div(wide, 2), 2)
        self.z = lax.div(wide, 4)
        self.wide = wide

    def at(self, z=None, y=None, core=None, x=None):
        z, y = (self.z if z is None else z), (self.y if y is None else y)
        core = self.core if core is None else core
        return (z * 4 + y * 2 + core, self.x if x is None else x)

    def greet(self):
        barrier = pltpu.get_barrier_semaphore()
        targets = [self.at(core=1 - self.core), self.at(y=1 - self.y), self.at(x=1 - self.x)]
        targets += [self.at(z=lax.rem(self.z + step, LINE)) for step in range(1, LINE)]
        for target in targets:
            pl.semaphore_signal(barrier, inc=1, device_id=target, device_id_type=MESH)
        pl.semaphore_wait(barrier, len(targets))


def gather_kernel(a_rows, b_rows, *refs):
    encoded, weights = refs[0], refs[1:11]
    everything, full = refs[11], refs[12:22]
    (own_sem, half_sem, flow_send, flow_recv, weight_send, weight_recv) = refs[22:]
    me = Place()
    rows = encoded.shape[0]
    x, y, z, core = me.x, me.y, me.z, me.core
    low, high = z > 0, z < LINE - 1
    UP_A, DOWN_A, Y_A, UP_B, DOWN_B, Y_B, X_B, CORE_A, CORE_B = range(9)

    own = pltpu.make_async_copy(
        encoded, everything.at[pl.ds(pl.multiple_of(me.wide * rows, 128), rows)], own_sem
    )
    own.start()

    def region(i, ref, plane, part):
        if i in COLUMNS:
            count, columns = ref.shape[0], ref.shape[1] // 2
            start = pl.multiple_of(plane * columns, 128)
            if part is None:
                return ref.at[:, pl.ds(start, columns)]
            first = pl.multiple_of(part * (count // 2), 16)
            return ref.at[pl.ds(first, count // 2), pl.ds(start, columns)]
        count = ref.shape[0] // 2
        if part is None:
            return ref.at[pl.ds(pl.multiple_of(plane * count, 16), count)]
        first = pl.multiple_of(plane * count + part * (count // 2), 16)
        return ref.at[pl.ds(first, count // 2)]

    halves = []
    for i in range(10):
        halves.append(
            pltpu.make_async_copy(weights[i], region(i, full[i], x, None), half_sem.at[i])
        )
        halves[-1].start()

    me.greet()
    own.wait()

    def flow(kind, owner_z, owner_y, plane, target, from_core=None):
        owner = owner_z * 2 + owner_y
        start = owner * (2 * rows) + (core if from_core is None else from_core) * rows
        if plane is None:
            size, slot = a_rows, owner
        else:
            start = start + a_rows + plane * b_rows
            size, slot = b_rows, owner + (plane * 8 if kind == CORE_B else 0)
        piece = everything.at[pl.ds(pl.multiple_of(start, 16), size)]
        return pltpu.make_async_remote_copy(
            src_ref=piece,
            dst_ref=piece,
            send_sem=flow_send.at[kind, slot],
            recv_sem=flow_recv.at[kind, slot],
            device_id=target,
            device_id_type=MESH,
        )

    sibling = me.at(core=1 - core)
    beside = me.at(y=1 - y)
    across = me.at(x=1 - x)
    above, below = me.at(z=z + 1), me.at(z=z - 1)

    def up_a(oz):
        return flow(UP_A, oz, y, None, above)

    def down_a(oz):
        return flow(DOWN_A, oz, y, None, below)

    def up_b(oz, oy):
        return flow(UP_B, oz, oy, x, above)

    def down_b(oz, oy):
        return flow(DOWN_B, oz, oy, x, below)

    def y_a(oz, oy):
        return flow(Y_A, oz, oy, None, beside)

    def y_b(oy):
        return flow(Y_B, z, oy, x, beside)

    def x_b(oz, oy, plane):
        return flow(X_B, oz, oy, plane, across)

    def core_a(oz, oy, from_core=None):
        return flow(CORE_A, oz, oy, None, sibling, from_core)

    def core_b(oz, oy, plane, from_core=None):
        return flow(CORE_B, oz, oy, plane, sibling, from_core)

    def weight(way, i, plane, part):
        piece = region(i, full[i], plane, part)
        if way == 0:
            piece_in = weights[i]
            count = piece_in.shape[0] // 2
            piece_in = piece_in.at[pl.ds(pl.multiple_of(part * count, 16), count)]
        else:
            piece_in = piece
        return pltpu.make_async_remote_copy(
            src_ref=piece_in,
            dst_ref=piece,
            send_sem=weight_send.at[way, i],
            recv_sem=weight_recv.at[way, i],
            device_id=across if way == 0 else sibling,
            device_id_type=MESH,
        )

    y_b(y).start()
    y_a(z, y).start()
    pl.when(high)(lambda: up_a(z).start())
    pl.when(low)(lambda: down_a(z).start())
    core_a(z, y).start()
    core_b(z, y, 0).start()
    core_b(z, y, 1).start()
    for i in range(10):
        weight(0, i, x, core).start()

    y_b(1 - y).wait_recv()
    core_b(z, 1 - y, x).start()
    x_b(z, 1 - y, x).start()

    def beside_arrives(oz):
        y_a(oz, 1 - y).wait_recv()
        core_a(oz, 1 - y).start()

    def pass_a(oz, arrived, onward, further):
        arrived(oz).wait_recv()
        pl.when(onward)(lambda: further(oz).start())
        y_a(oz, y).start()
        core_a(oz, y).start()

    def pass_b(oz, arrived, onward, further):
        for oy in (y, 1 - y):
            arrived(oz, oy).wait_recv()
            pl.when(onward)(lambda: further(oz, oy).start())
            x_b(oz, oy, x).start()
            core_b(oz, oy, x).start()

    for step in range(LINE):
        for kind, back in ((0, 1), (1, 0)):
            under, over = z - back - step, z + back + step
            if kind == 0 and step < LINE - 1:
                pl.when(under >= 0)(lambda: pass_a(under, up_a, high, up_a))
                pl.when(over < LINE)(lambda: pass_a(over, down_a, low, down_a))
            if kind == 1 and step == 0:
                for oy in (y, 1 - y):
                    pl.when(high)(lambda oy=oy: up_b(z, oy).start())
                    pl.when(low)(lambda oy=oy: down_b(z, oy).start())
            if kind == 1 and step > 0:
                pl.when(under >= 0)(lambda: pass_b(under, up_b, high, up_b))
                pl.when(over < LINE)(lambda: pass_b(over, down_b, low, down_b))
    for i in range(10):
        weight(0, i, 1 - x, core).wait_recv()
        weight(1, i, 1 - x, core).start()
    beside_arrives(z)
    for step in range(1, LINE):
        pl.when(z - step >= 0)(lambda: beside_arrives(z - step))
        pl.when(z + step < LINE)(lambda: beside_arrives(z + step))

    def across_arrives(oz, oy):
        x_b(oz, oy, 1 - x).wait_recv()
        core_b(oz, oy, 1 - x).start()

    across_arrives(z, 1 - y)
    for step in range(LINE - 1):
        under, over = z - 1 - step, z + 1 + step
        for oy in (y, 1 - y):
            pl.when(under >= 0)(lambda: across_arrives(under, oy))
            pl.when(over < LINE)(lambda: across_arrives(over, oy))

    y_b(y).wait_send()
    x_b(z, 1 - y, x).wait_send()
    for oz in range(LINE):
        y_a(oz, y).wait_send()
        for oy in range(2):
            core_a(oz, oy).wait_send()
            core_a(oz, oy, 1 - core).wait_recv()
            for plane in range(2):
                core_b(oz, oy, plane).wait_send()
                core_b(oz, oy, plane, 1 - core).wait_recv()
        away = oz != z

        @pl.when(away)
        def _():
            for oy in range(2):
                x_b(oz, oy, x).wait_send()

        @pl.when(jnp.logical_and(high, oz <= z))
        def _():
            up_a(oz).wait_send()
            for oy in range(2):
                up_b(oz, oy).wait_send()

        @pl.when(jnp.logical_and(low, oz >= z))
        def _():
            down_a(oz).wait_send()
            for oy in range(2):
                down_b(oz, oy).wait_send()

    for i in range(10):
        halves[i].wait()
        weight(0, i, x, core).wait_send()
        weight(1, i, 1 - x, core).wait_send()
        weight(1, i, 1 - x, 1 - core).wait_recv()


def gather_by_kernel(encoded, weights):
    rows, width = encoded.shape
    a_rows = rows * 17 // 24 // 16 * 16
    b_rows = (rows - a_rows) // 2
    shapes = [jax.ShapeDtypeStruct((16 * rows, width), bf16)]
    for i, w in enumerate(weights):
        doubled = (w.shape[0], 2 * w.shape[1]) if i in COLUMNS else (2 * w.shape[0], w.shape[1])
        shapes.append(jax.ShapeDtypeStruct(doubled, bf16))
    dma = pltpu.SemaphoreType.DMA
    out = pl.pallas_call(
        functools.partial(gather_kernel, a_rows, b_rows),
        out_shape=shapes,
        in_specs=[pl.BlockSpec(memory_space=pl.ANY)] * 11,
        out_specs=[pl.BlockSpec(memory_space=pl.ANY)] * 11,
        scratch_shapes=[dma, dma((10,)), dma((9, 16)), dma((9, 16)), dma((2, 10)), dma((2, 10))],
        compiler_params=pltpu.CompilerParams(
            collective_id=0, has_side_effects=True, vmem_limit_bytes=4 << 20
        ),
        name="gather",
    )(encoded, *weights)
    return out[0], tuple(out[1:])


TILE = 384
UNITS = 16


def share_of(refs, unit, core, plane):
    narrow_units = (0, 1, 2, 4, 5, 6)
    if unit < 6:
        ref, row, column = refs[narrow_units[unit]], core * TILE, plane * TILE
    elif unit < 8:
        ref, row, column = refs[(3, 7)[unit - 6]], plane * TILE, core * TILE
    elif unit < 12:
        ref, row, column = refs[8], core * TILE, plane * 4 * TILE + (unit - 8) * TILE
    else:
        ref, row, column = refs[9], plane * 4 * TILE + (unit - 12) * TILE, core * TILE
    return ref.at[
        pl.ds(pl.multiple_of(row, 128), TILE), pl.ds(pl.multiple_of(column, 128), TILE)
    ]


def reduce_kernel(*refs):
    grads = refs[:10]
    theirs, mine, made, norms = refs[10:14]
    sums_out, mine_out, theirs_out, made_out, norms_out = refs[14:19]
    (
        own, from_core, from_x, from_y, from_z, total, rows_in, rows_got, norm_all, norm_in,
        own_sem, core_send, core_recv, x_send, x_recv, y_send, y_recv, z_send, z_recv,
        gz_send, gz_recv, gy_send, gy_recv, gc_send, gc_recv, out_sem,
        extra_send, extra_recv, norm_send, norm_recv,
    ) = refs[19:]
    me = Place()
    x, y, z, core = me.x, me.y, me.z, me.core
    half, part = TILE // 2, TILE // 2 // LINE
    sibling, beside, across = me.at(core=1 - core), me.at(y=1 - y), me.at(x=1 - x)

    def remote(src, dst, send, recv, target):
        return pltpu.make_async_remote_copy(
            src_ref=src, dst_ref=dst, send_sem=send, recv_sem=recv,
            device_id=target, device_id_type=MESH,
        )

    def own_copy(unit, plane):
        return pltpu.make_async_copy(
            share_of(grads, unit, core, plane), own.at[unit, plane], own_sem.at[unit, plane]
        )

    def to_core(unit, plane):
        return remote(
            share_of(grads, unit, 1 - core, plane), from_core.at[unit, plane],
            core_send.at[unit, plane], core_recv.at[unit, plane], sibling,
        )

    def to_x(u):
        return remote(own.at[u, 1 - x], from_x.at[u], x_send.at[u], x_recv.at[u], across)

    def to_y(u):
        rows = pl.ds(pl.multiple_of((1 - y) * half, 16), half)
        return remote(own.at[u, x, rows], from_y.at[u], y_send.at[u], y_recv.at[u], beside)

    def to_z(u, d):
        other = lax.rem(z + d, LINE)
        rows = pl.ds(pl.multiple_of(y * half + other * part, 16), part)
        return remote(
            own.at[u, x, rows], from_z.at[u, d - 1], z_send.at[u, d - 1], z_recv.at[u, d - 1],
            me.at(z=other),
        )

    def gather_z(u, d):
        rows = pl.ds(pl.multiple_of(y * half + z * part, 16), part)
        piece = total.at[u, core, rows]
        return remote(
            piece, piece, gz_send.at[u, d - 1], gz_recv.at[u, d - 1],
            me.at(z=lax.rem(z + d, LINE)),
        )

    def gathered_z(u, d):
        rows = pl.ds(pl.multiple_of(y * half + lax.rem(z + LINE - d, LINE) * part, 16), part)
        piece = total.at[u, core, rows]
        return remote(piece, piece, gz_send.at[u, d - 1], gz_recv.at[u, d - 1], beside)

    def gather_y(u, at_y):
        piece = total.at[u, core, pl.ds(pl.multiple_of(at_y * half, 16), half)]
        return remote(piece, piece, gy_send.at[u], gy_recv.at[u], beside)

    def gather_core(u, at_core):
        piece = total.at[u, at_core]
        return remote(piece, piece, gc_send.at[u], gc_recv.at[u], sibling)

    def put_out(u):
        return pltpu.make_async_copy(total.at[u], sums_out.at[u], out_sem.at[u])

    rows_copy = remote(theirs, rows_in, extra_send.at[0], extra_recv.at[0], across)
    made_copy = remote(made, made_out, extra_send.at[1], extra_recv.at[1], across)
    got_copy = remote(rows_got, theirs_out, extra_send.at[2], extra_recv.at[2], across)

    for unit in range(UNITS):
        for plane in range(2):
            own_copy(unit, plane).start()
    me.greet()
    rows_copy.start()
    for unit in range(UNITS):
        for plane in range(2):
            to_core(unit, plane).start()

    norm_all[...] = norms[...]
    along_z = tuple(me.at(z=lax.rem(z + d, LINE)) for d in range(1, LINE))
    slot = 0
    for targets in ((sibling,), (across,), (beside,), along_z):
        copies = []
        for target in targets:
            copies.append(
                remote(norm_all, norm_in.at[slot], norm_send.at[slot], norm_recv.at[slot], target)
            )
            copies[-1].start()
            slot += 1
        for copy in copies:
            copy.wait()
        for k in range(slot - len(copies), slot):
            norm_all[...] += norm_in[k]
    norms_out[...] = norm_all[...]

    for unit in range(UNITS):
        for plane in range(2):
            own_copy(unit, plane).wait()

    def plus(a, b):
        return (a.astype(f32) + b.astype(f32)).astype(bf16)

    def step(t, carry):
        def at(lag):
            u = t - lag
            return u, jnp.logical_and(u >= 0, u < UNITS)

        u0, on0 = at(0)

        @pl.when(on0)
        def _():
            for plane in range(2):
                to_core_wait(u0, plane)
            own[u0] = plus(own[u0], from_core[u0])
            to_x(u0).start()

        u1, on1 = at(2)

        @pl.when(on1)
        def _():
            to_x(u1).wait()
            own[u1, x] = plus(own[u1, x], from_x[u1])
            to_y(u1).start()

        u2, on2 = at(3)

        @pl.when(on2)
        def _():
            to_y(u2).wait()
            rows = pl.ds(pl.multiple_of(y * half, 16), half)
            own[u2, x, rows] = plus(own[u2, x, rows], from_y[u2])
            for d in range(1, LINE):
                to_z(u2, d).start()

        u3, on3 = at(4)

        @pl.when(on3)
        def _():
            for d in range(1, LINE):
                to_z(u3, d).wait()
            rows = pl.ds(pl.multiple_of(y * half + z * part, 16), part)
            summed = own[u3, x, rows].astype(f32)
            for d in range(1, LINE):
                summed += from_z[u3, d - 1].astype(f32)
            total[u3, core, rows] = summed.astype(bf16)
            for d in range(1, LINE):
                gather_z(u3, d).start()

        u4, on4 = at(5)

        @pl.when(on4)
        def _():
            for d in range(1, LINE):
                gathered_z(u4, d).wait_recv()
                gather_z(u4, d).wait_send()
            gather_y(u4, y).start()

        u5, on5 = at(6)

        @pl.when(on5)
        def _():
            gather_y(u5, 1 - y).wait_recv()
            gather_y(u5, y).wait_send()
            gather_core(u5, core).start()

        u6, on6 = at(7)

        @pl.when(on6)
        def _():
            gather_core(u6, 1 - core).wait_recv()
            gather_core(u6, core).wait_send()
            put_out(u6).start()

        @pl.when(t == UNITS)
        def _():
            rows_copy.wait()
            summed = mine[...] + rows_in[...].astype(f32)
            mine_out[...] = summed
            rows_got[...] = summed.astype(bf16)
            got_copy.start()
            made_copy.start()

        return carry

    def to_core_wait(u, plane):
        piece = remote(
            own.at[u, plane], from_core.at[u, plane], core_send.at[u, plane],
            core_recv.at[u, plane], sibling,
        )
        piece.wait_recv()

    lax.fori_loop(0, UNITS + 7, step, 0)
    got_copy.wait()
    made_copy.wait()
    for unit in range(UNITS):
        put_out(unit).wait()
        for plane in range(2):
            to_core(unit, plane).wait_send()


def reduce_by_kernel(grads, theirs, mine, made, norms):
    rows, width = mine.shape
    anywhere = pl.BlockSpec(memory_space=pl.ANY)
    vmem = pl.BlockSpec(memory_space=pltpu.VMEM)
    dma = pltpu.SemaphoreType.DMA
    U, T = UNITS, TILE
    z_only = LINE - 1
    return pl.pallas_call(
        reduce_kernel,
        out_shape=[
            jax.ShapeDtypeStruct((U, 2, T, T), bf16),
            jax.ShapeDtypeStruct((rows, width), f32),
            jax.ShapeDtypeStruct((rows, width), bf16),
            jax.ShapeDtypeStruct((rows, width), bf16),
            jax.ShapeDtypeStruct(norms.shape, f32),
        ],
        in_specs=[anywhere] * 10 + [anywhere, vmem, anywhere, vmem],
        out_specs=[anywhere, vmem, anywhere, anywhere, vmem],
        scratch_shapes=[
            pltpu.VMEM((U, 2, T, T), bf16),
            pltpu.VMEM((U, 2, T, T), bf16),
            pltpu.VMEM((U, T, T), bf16),
            pltpu.VMEM((U, T // 2, T), bf16),
            pltpu.VMEM((U, z_only, T // 2 // LINE, T), bf16),
            pltpu.VMEM((U, 2, T, T), bf16),
            pltpu.VMEM((rows, width), bf16),
            pltpu.VMEM((rows, width), bf16),
            pltpu.VMEM(norms.shape, f32),
            pltpu.VMEM((6,) + norms.shape, f32),
            dma((U, 2)), dma((U, 2)), dma((U, 2)), dma((U,)), dma((U,)), dma((U,)), dma((U,)),
            dma((U, z_only)), dma((U, z_only)), dma((U, z_only)), dma((U, z_only)),
            dma((U,)), dma((U,)), dma((U,)), dma((U,)), dma((U,)), dma((3,)), dma((3,)),
            dma((6,)), dma((6,)),
        ],
        compiler_params=pltpu.CompilerParams(
            collective_id=1, has_side_effects=True, vmem_limit_bytes=VMEM_LIMIT
        ),
        name="reduce",
    )(*grads, theirs, mine, made, norms)


def weight_outputs(sums):
    narrow_ones = [sums[u].reshape(2 * TILE, TILE) for u in range(6)]
    outs = [jnp.concatenate([sums[u, 0], sums[u, 1]], axis=1) for u in (6, 7)]
    grow = jnp.concatenate([sums[u].reshape(2 * TILE, TILE) for u in range(8, 12)], axis=1)
    shrink = jnp.concatenate(
        [jnp.concatenate([sums[u, 0], sums[u, 1]], axis=1) for u in range(12, 16)], axis=0
    )
    ordered = narrow_ones[:3] + outs[:1] + narrow_ones[3:] + outs[1:] + [grow, shrink]
    return tuple(piece.astype(f32) for piece in ordered)


def by_kernels(narrow):
    return lax.axis_size("wide") == 4 * LINE and narrow == 2


def gather_all(encoded, weights):
    if by_kernels(lax.axis_size("narrow")):
        return gather_by_kernel(encoded, weights)
    everything = lax.all_gather(encoded, "wide", tiled=True)
    full = tuple(
        lax.all_gather(w, "narrow", axis=1 if i in COLUMNS else 0, tiled=True)
        for i, w in enumerate(weights)
    )
    return everything, full


def reduce_all(grads):
    shares = tuple(
        lax.psum_scatter(
            g.astype(bf16), "narrow", scatter_dimension=1 if i in COLUMNS else 0, tiled=True
        )
        for i, g in enumerate(grads)
    )
    return tuple(s.astype(f32) for s in lax.psum(shares, "wide"))


def local(
    hidden,
    encoded,
    retrieved,
    self_query,
    self_key,
    self_value,
    self_out,
    cross_query,
    cross_key,
    cross_value,
    cross_out,
    expand_weight,
    reduce_weight,
    first_gain,
    first_shift,
    second_gain,
    second_shift,
    third_gain,
    third_shift,
    cotangent,
):
    tok_rows, width = hidden.shape
    narrow = lax.axis_size("narrow")
    at = lax.axis_index("narrow").astype(jnp.int32)
    chunk = tok_rows // (2 * narrow)

    def own(rows, size=chunk, at=at):
        low = lax.dynamic_slice_in_dim(rows, at * size, size)
        high = lax.dynamic_slice_in_dim(rows, (2 * narrow - 1 - at) * size, size)
        return jnp.concatenate([low, high], axis=0)

    everything, full = gather_all(
        encoded,
        (
            self_query,
            self_key,
            self_value,
            self_out,
            cross_query,
            cross_key,
            cross_value,
            cross_out,
            expand_weight,
            reduce_weight,
        ),
    )
    (
        self_query,
        self_key,
        self_value,
        self_out,
        cross_query,
        cross_key,
        cross_value,
        cross_out,
        expand_weight,
        reduce_weight,
    ) = full
    where_at = at.reshape(1)
    picked = own(retrieved, chunk // BLOCK_ROWS).reshape(-1)
    mine = own(hidden)
    grad_final = own(cotangent).astype(f32)

    query_self = project(mine, self_query).astype(bf16)
    key_self = project(hidden, self_key).astype(bf16)
    value_self = project(hidden, self_value).astype(bf16)
    blend_self, log_self = self_forward(narrow, where_at, query_self, key_self, value_self)
    first, first_normal, first_inverse = norm_forward(
        mine.astype(f32) + project(blend_self, self_out), first_gain, first_shift
    )
    first_low = first.astype(bf16)
    query_cross = project(first_low, cross_query).astype(bf16)
    blend_cross, log_cross, key_cross, value_cross = cross_forward(
        picked, everything, cross_key, cross_value, query_cross
    )
    second, second_normal, second_inverse = norm_forward(
        first + project(blend_cross, cross_out), second_gain, second_shift
    )
    second_low = second.astype(bf16)
    pre_act = project(second_low, expand_weight)
    activated = jax.nn.gelu(pre_act, approximate=False).astype(bf16)
    final, third_normal, third_inverse = norm_forward(
        second + project(activated, reduce_weight), third_gain, third_shift
    )
    output = final.astype(bf16)

    grad_third, third_gain_grad, third_shift_grad = norm_backward(
        grad_final, third_normal, third_inverse, third_gain
    )
    grad_ffn = grad_third.astype(bf16)
    reduce_grad = grad_weight(activated, grad_ffn)
    grad_pre = (grad_input(grad_ffn, reduce_weight) * gelu_slope(pre_act)).astype(bf16)
    expand_grad = grad_weight(second_low, grad_pre)
    grad_second = grad_third + grad_input(grad_pre, expand_weight)
    grad_second_in, second_gain_grad, second_shift_grad = norm_backward(
        grad_second, second_normal, second_inverse, second_gain
    )
    grad_cross = grad_second_in.astype(bf16)
    cross_out_grad = grad_weight(blend_cross, grad_cross)
    grad_blend_cross = grad_input(grad_cross, cross_out).astype(bf16)
    grad_query_cross, cross_key_grad, cross_value_grad = cross_backward(
        picked,
        everything,
        key_cross,
        value_cross,
        query_cross,
        log_cross,
        blend_cross,
        grad_blend_cross,
    )
    cross_query_grad = grad_weight(first_low, grad_query_cross)
    grad_first = grad_second_in + grad_input(grad_query_cross, cross_query)
    grad_first_in, first_gain_grad, first_shift_grad = norm_backward(
        grad_first, first_normal, first_inverse, first_gain
    )
    grad_self = grad_first_in.astype(bf16)
    self_out_grad = grad_weight(blend_self, grad_self)
    grad_blend_self = grad_input(grad_self, self_out).astype(bf16)
    grad_query_self, grad_key_self, grad_value_self = self_backward(
        narrow, where_at, query_self, key_self, value_self, log_self, blend_self, grad_blend_self
    )
    self_query_grad = grad_weight(mine, grad_query_self)
    self_key_grad = grad_weight(hidden, grad_key_self)
    self_value_grad = grad_weight(hidden, grad_value_self)
    grad_rows = grad_input(grad_key_self, self_key) + grad_input(grad_value_self, self_value)
    grad_own = grad_first_in + grad_input(grad_query_self, self_query)
    weight_grads = (
        self_query_grad,
        self_key_grad,
        self_value_grad,
        self_out_grad,
        cross_query_grad,
        cross_key_grad,
        cross_value_grad,
        cross_out_grad,
        expand_grad,
        reduce_grad,
    )
    norm_grads = (
        first_gain_grad,
        first_shift_grad,
        second_gain_grad,
        second_shift_grad,
        third_gain_grad,
        third_shift_grad,
    )

    if by_kernels(narrow):
        zero = jnp.zeros_like(first_gain_grad)
        theirs = own(grad_rows, at=1 - at).astype(bf16)
        sums, grad_mine, grad_theirs, made_theirs, norm_sums = reduce_by_kernel(
            tuple(g.astype(bf16) for g in weight_grads),
            theirs,
            own(grad_rows) + grad_own,
            output,
            jnp.stack(norm_grads + (zero, zero)),
        )

        def ordered(ours, others):
            a, b = ours[:chunk], ours[chunk:]
            c, d = others[:chunk], others[chunk:]
            first_one = at == 0
            return jnp.concatenate(
                [
                    jnp.where(first_one, a, c),
                    jnp.where(first_one, c, a),
                    jnp.where(first_one, d, b),
                    jnp.where(first_one, b, d),
                ],
                axis=0,
            )

        output = ordered(output, made_theirs)
        grad_hidden = ordered(grad_mine, grad_theirs.astype(f32))
        weight_sums = weight_outputs(sums)
    else:

        def spread(rows):
            empty = jnp.zeros((tok_rows, width), rows.dtype)
            placed = lax.dynamic_update_slice_in_dim(empty, rows[:chunk], at * chunk, 0)
            return lax.dynamic_update_slice_in_dim(
                placed, rows[chunk:], (2 * narrow - 1 - at) * chunk, 0
            )

        grad_hidden = lax.psum((grad_rows + spread(grad_own)).astype(bf16), "narrow").astype(f32)
        output = lax.psum(spread(output), "narrow")
        weight_sums = reduce_all(weight_grads)
        norm_sums = lax.psum(jnp.stack(norm_grads), ("wide", "narrow"))
    return (output, grad_hidden) + weight_sums + tuple(norm_sums[i] for i in range(6))


def solution(mesh):
    rows = P("wide", None)
    columns_split = P(None, "narrow")
    rows_split = P("narrow", None)
    weights = (columns_split,) * 3 + (rows_split,) + (columns_split,) * 3 + (rows_split,)
    weights += (columns_split, rows_split)
    return jax.shard_map(
        local,
        mesh=mesh,
        in_specs=(rows, rows, rows) + weights + (P(),) * 6 + (rows,),
        out_specs=(rows, rows) + weights + (P(),) * 6,
        check_vma=False,
    )
```

time: 2250 us -> 604 us (0.27)
  waiting for transfers between devices: 1300 us -> 0 us
  Pallas kernels: 0 us -> 445 us
  local copies, waits for them, and re-layouts: 300 us -> 34.3 us
  matrix products: 270 us -> 79.8 us
  blocking collectives: 164 us -> 0 us
  other arithmetic: 166 us -> 37.5 us
    psum x7 -> x0, waiting for transfers between devices: 710 us -> none  [the longest x3 357 us: narrow_sum(): return lax.psum(partial_value, 'narrow')]
    all_to_all x3 -> x0, waiting for transfers between devices: 592 us -> none  [the longest x1 307 us: local(): lax.all_to_all(outgoing, 'wide', split_axis=0, concat_axis=0, tiled=True)]
    pallas_call x0 -> x6, Pallas kernels: none -> 445 us  [the longest x1 185 us: gather_by_kernel(): pl.pallas_call(functools.partial(gather_kernel, a_rows, b_rows), out_shap...]
    dot_general x44 -> x24, matrix products: 270 us -> 79.8 us  [the longest x8 31.1 us: project(): return jnp.dot(rows_in, weight, preferred_element_type=f32)]
    psum x1 -> x0, blocking collectives: 164 us -> none  [local(): lax.psum((self_query_grad, self_key_grad, self_value_grad, self_out_grad,...]
    unnamed x203 -> x158, local copies, waits for them, and re-layouts: 88.4 us -> 24.1 us
    concatenate x4 -> x0, local copies, waits for them, and re-layouts: 56.4 us -> none  [the longest x3 52.1 us: local(): jnp.concatenate([grad_key_flat, grad_value_flat], 1)]
    scatter x1 -> x0, local copies, waits for them, and re-layouts: 51.3 us -> none  [local(): grad_slots = jnp.zeros((peers * capacity, BLOCK_ROWS, 2 * width), jnp.flo...]
  transfers between devices with their start and end apart: 10 -> 0, of which waited for: 8 -> 0; matrix products, arithmetic and copies ran while one was open for 11% -> 0% of each run, Pallas kernels for 0% -> 0%
where the time goes in v1:
time: 604 us; the launch traced here: 598 us
  Pallas kernels  445 us (74%)
  matrix products  79.8 us (13%)
  other arithmetic  37.5 us (6%)
  local copies, waits for them, and re-layouts  34.3 us (6%)
    pallas_call x1, Pallas kernels, gather_by_kernel(): pl.pallas_call(functools.partial(gather_kernel, a_rows, b_rows), out_shap...  185 us
    pallas_call x1, Pallas kernels, reduce_by_kernel(): pl.pallas_call(reduce_kernel, out_shape=[jax.ShapeDtypeStruct((U, 2, T, T...  170 us
    pallas_call x1, Pallas kernels, cross_forward(): pl.pallas_call(cross_forward_kernel, grid_spec=pltpu.PrefetchScalarGridSp...  33.6 us
    pallas_call x1, Pallas kernels, cross_backward(): pl.pallas_call(cross_backward_kernel, grid_spec=pltpu.PrefetchScalarGridS...  31.6 us
    dot_general x8, matrix products, project(): return jnp.dot(rows_in, weight, preferred_element_type=f32)  31.1 us
    convert_element_type x10, other arithmetic, weight_outputs(): return tuple((piece.astype(f32) for piece in ordered))  26 us
    dot_general x8, matrix products, grad_weight(): return jnp.einsum('ti,to->io', left, right, preferred_element_type=f32)  24.7 us
    unnamed x158, local copies, waits for them, and re-layouts  24.1 us

profile of v1, /device:TPU:0, one launch (start us, length us, event | category | flops | bytes accessed | tf_op | source)
XLA Modules:
  0.0 598.4 jit_solution(501160737223488600)
XLA Ops:
  0.7 2.5 constant_dynamic-slice_fusion.3
  14.3 185.3 %gather.1 = (bf16[24576,768]{1,0:T(8,128)(2,1)}, bf16[768,768]{1,0:T(8,128)(2,1)S(1)}, bf16[768,768]{1,0:T(8,128)(2,1)S(1)}, bf16[768,768]{1,0:T(8,128)(2,1)S(1)...) custom-call(bf16[1536,768]{1,0:T(8,128)(2,1)S(1)} %copy-done, ...), custom_call_target="tpu_custom_call" | custom-call | tf_op jit(solution)/shard_map/gather/pallas_call | solution.py:623
  207.5 2.5 fusion.23.k_ref
  210.1 2.5 fusion.24.v_ref
  212.6 10.7 %self_forward.1 = (bf16[512,768]{1,0:T(8,128)(2,1)}, f32[6,2,512]{2,1,0:T(2,128)}) custom-call(s32[1]{0:T(128)} %bitcast.at_ref, bf16[512,768]{1,0:T(8,128)(2,1)} %convolution_convert_fusion.13.q_ref, bf16[1024,768]{1,0:T(8,128)(2,1)} %fusion.23.k_ref, bf16[1024,768]{1,0:T(8,128)(2,1)} %fusion.24.v_ref), custom_call_target="tpu_custom_call" | custom-call | tf_op jit(solution)/shard_map/self_forward/pallas_call | solution.py:165
  228.6 33.6 %cross_forward.1 = (bf16[512,768]{1,0:T(8,128)(2,1)}, f32[4,6,256]{2,1,0:T(8,128)}, bf16[4096,768]{1,0:T(8,128)(2,1)}, bf16[4096,768]{1,0:T(8,128)(2,1)}) custom-call(s32[32]{0:T(128)} %reshape.121.picked_ref, bf16[24576,768]{1,0:T(8,128)(2,1)} %get-tuple-element.51.refs_0_.refs_1_.refs_2_.refs_3_.refs_4_.refs_5_.refs_6_.refs_7_, ...), custom_call_target="tpu_custom_call" | custom-call | tf_op jit(solution)/shard_map/cross_forward/pallas_call | solution.py:271
  262.2 2.2 fusion.46
  265.1 15.7 %fusion.2 = (bf16[512,3072]{1,0:T(8,128)(2,1)S(1)}, f32[512,3072]{1,0:T(8,128)S(1)}) fusion(bf16[768,3072]{1,0:T(8,128)(2,1)S(1)} %bitcast.92, f32[512,768]{1,0:T(8,128)S(1)} %get-tuple-element.136, f32[768]{0:T(1024)S(1)} %copy-done.69, f32[768]{0:T(1024)S(1)} %copy-done.63, f32[512]{0:T(512)S(1)} %add_rsqrt_fusion.1, f32[512]{0:T(512)S(1)} %broadcast_multiply_fusion.7), kind=kOutput, calls=%fused_computation.4 | convolution fusion | flops 2520121344 | bytes 15738880 | tf_op jit(solution)/shard_map/dot_general | solution.py:48
  282.5 2.7 fusion.47
  288.1 7.4 %fusion.8 = bf16[512,3072]{1,0:T(8,128)(2,1)S(1)} fusion(f32[512,3072]{1,0:T(8,128)S(1)} %get-tuple-element.138, bf16[3072,768]{1,0:T(8,128)(2,1)S(1)} %bitcast.94, f32[512,768]{1,0:T(8,128)S(1)} %get-tuple-element.140, f32[512]{0:T(512)S(1)} %broadcast_multiply_fusion.4, f32[512]{0:T(512)S(1)} %broadcast_multiply_fusion.5, f32[768]{0:T(1024)S(1)} %copy-done.62, ...), kind=kOutput, calls=%fused_computation.10 | convolution fusion | flops 2436366336 | bytes 16526336 | tf_op jit(solution)/shard_map/to,io->ti/dot_general | solution.py:56
  295.6 3.3 multiply_reduce_fusion
  301.1 31.6 %cross_backward.1 = (bf16[512,768]{1,0:T(8,128)(2,1)}, bf16[768,768]{1,0:T(8,128)(2,1)}, bf16[768,768]{1,0:T(8,128)(2,1)}) custom-call(s32[32]{0:T(128)} %reshape.121.picked_ref, bf16[24576,768]{1,0:T(8,128)(2,1)} %get-tuple-element.51.refs_0_.refs_1_.refs_2_.refs_3_.refs_4_.refs_5_.refs_6_.refs_7_, ...), custom_call_target="tpu_custom_call" | custom-call | tf_op jit(solution)/shard_map/cross_backward/pallas_call | solution.py:340
  332.8 3.4 multiply_reduce_fusion.1
  336.9 2.4 subtract_multiply_fusion
  341.0 14.0 %self_backward.1 = (bf16[512,768]{1,0:T(8,128)(2,1)}, bf16[1024,768]{1,0:T(8,128)(2,1)}, bf16[1024,768]{1,0:T(8,128)(2,1)}) custom-call(s32[1]{0:T(128)} %bitcast.at_ref, bf16[512,768]{1,0:T(8,128)(2,1)} %convolution_convert_fusion.13.q_ref, bf16[1024,768]{1,0:T(8,128)(2,1)} %fusion.23.k_ref, bf16[1024,768]{1,0:T(8,128)(2,1)} %fusion.24.v_ref, ...), custom_call_target="tpu_custom_call" | custom-call | tf_op jit(solution)/shard_map/self_backward/pallas_call | solution.py:216
  355.0 3.0 fusion.48
  367.2 7.1 %convolution_convert_fusion.refs_9_ = bf16[3072,768]{1,0:T(8,128)(2,1)} fusion(bf16[512,3072]{1,0:T(8,128)(2,1)} %copy-done.74, f32[512,768]{1,0:T(8,128)S(1)} %get-tuple-element.140, f32[512]{0:T(512)S(1)} %broadcast_multiply_fusion.4, f32[512]{0:T(512)S(1)} %broadcast_multiply_fusion.5, f32[768]{0:T(1024)S(1)} %copy-done.62, f32[512]{0:T(512)S(1)} %add_rsqrt_fusion, ...), kind=kOutput, calls=%fused_computation.26 | convolution fusion | flops 2422996992 | bytes 10234880 | tf_op jit(solution)/shard_map/ti,to->io/dot_general | solution.py:52
  374.3 4.9 convolution_convert_fusion.1.refs_8_
  387.2 2.5 fusion.25.refs_1_
  389.7 2.5 fusion.26.refs_2_
  392.3 170.1 %reduce.13 = (bf16[16,2,384,384]{3,2,1,0:T(8,128)(2,1)}, f32[512,768]{1,0:T(8,128)}, bf16[512,768]{1,0:T(8,128)(2,1)}, bf16[512,768]{1,0:T(8,128)(2,1)}, f32[8,768]{1,0:T(8,128)}) custom-call(bf16[768,768]{1,0:T(8,128)(2,1)} %convolution_convert_fusion.9.refs_0_, bf16[768,768]{1,0:T(8,128)(2,1)} %fusion.25.refs_1_, bf16[768,768]{1,0:T(8,128)(2,1)} %fusion.26.refs_2_, ...), custom_call_target="tpu_custom_call" | custom-call | tf_op jit(solution)/shard_map/reduce/pallas_call | solution.py:869
  562.4 2.4 slice_bitcast_fusion.7
  564.8 14.1 %maximum_convert_fusion.1 = f32[1536,768]{1,0:T(8,128)} fusion(bf16[384,384]{1,0:T(8,128)(2,1)S(1)} %get-tuple-element.93, bf16[384,384]{1,0:T(8,128)(2,1)S(1)} %get-tuple-element.94, bf16[384,384]{1,0:T(8,128)(2,1)S(1)} %get-tuple-element.95, bf16[384,384]{1,0:T(8,128)(2,1)S(1)} %get-tuple-element.96, bf16[384,384]{1,0:T(8,128)(2,1)S(1)} %get-tuple-element.97, ...), kind=kLoop, calls=%fused_computation.33 | loop fusion | flops 18874368 | bytes 7077888 | tf_op jit(solution)/shard_map/convert_element_type | solution.py:911
  580.6 2.8 maximum_convert_fusion
  (217 shorter events, 67.4 us)
Async XLA Ops:
  3.2 220.1 %copy-start.52 = (bf16[256,768]{1,0:T(8,128)(2,1)}, bf16[256,768]{1,0:T(8,128)(2,1)S(1)}, u32[]{:S(2)}) copy-start(bf16[256,768]{1,0:T(8,128)(2,1)S(1)} %get-tuple-element.143) | copy-start | bytes 1179652
  3.2 220.1 %copy-start.54 = (bf16[256,768]{1,0:T(8,128)(2,1)}, bf16[256,768]{1,0:T(8,128)(2,1)S(1)}, u32[]{:S(2)}) copy-start(bf16[256,768]{1,0:T(8,128)(2,1)S(1)} %get-tuple-element.144) | copy-start | bytes 1179652
  204.0 6.1 %copy-start.19 = (bf16[768,768]{1,0:T(8,128)(2,1)}, bf16[768,768]{1,0:T(8,128)(2,1)S(1)}, u32[]{:S(2)}) copy-start(bf16[768,768]{1,0:T(8,128)(2,1)S(1)} %get-tuple-element.47) | copy-start | bytes 3538948
  204.0 6.1 %copy-start.5 = (bf16[768,768]{1,0:T(8,128)(2,1)}, bf16[768,768]{1,0:T(8,128)(2,1)S(1)}, u32[]{:S(2)}) copy-start(bf16[768,768]{1,0:T(8,128)(2,1)S(1)} %get-tuple-element.48) | copy-start | bytes 3538948
  204.0 19.3 %copy-start.21 = (bf16[768,768]{1,0:T(8,128)(2,1)}, bf16[768,768]{1,0:T(8,128)(2,1)S(1)}, u32[]{:S(2)}) copy-start(bf16[768,768]{1,0:T(8,128)(2,1)S(1)} %get-tuple-element.50) | copy-start | bytes 3538948
  204.0 21.7 %copy-start.23 = (bf16[768,768]{1,0:T(8,128)(2,1)}, bf16[768,768]{1,0:T(8,128)(2,1)S(1)}, u32[]{:S(2)}) copy-start(bf16[768,768]{1,0:T(8,128)(2,1)S(1)} %get-tuple-element.54) | copy-start | bytes 3538948
  225.3 36.8 %copy-start.30 = (f32[512,768]{1,0:T(8,128)}, f32[512,768]{1,0:T(8,128)S(1)}, u32[]{:S(2)}) copy-start(f32[512,768]{1,0:T(8,128)S(1)} %get-tuple-element.134) | copy-start | bytes 4718596
  225.3 36.8 %copy-start.56 = (f32[512]{0:T(512)}, f32[512]{0:T(512)S(1)}, u32[]{:S(2)}) copy-start(f32[512]{0:T(512)S(1)} %broadcast_multiply_fusion.8) | copy-start | bytes 6148
  225.7 36.5 %copy-start.59 = (f32[512]{0:T(512)}, f32[512]{0:T(512)S(1)}, u32[]{:S(2)}) copy-start(f32[512]{0:T(512)S(1)} %add_rsqrt_fusion.2) | copy-start | bytes 6148
  226.1 38.6 %slice-start = ((s8[4718592]{0:T(1024)(128)(4,1)}), s8[524288]{0:T(1024)(128)(4,1)S(1)}, s32[]{:S(2)}) async-start(s8[4718592]{0:T(1024)(128)(4,1)} %bitcast.91), calls=%async_computation | async-start | bytes 1048576
  228.5 36.2 %slice-start.1 = ((s8[4718592]{0:T(1024)(128)(4,1)}), s8[4194304]{0:T(1024)(128)(4,1)S(1)}, s32[]{:S(2)}) async-start(s8[4718592]{0:T(1024)(128)(4,1)} %bitcast.91), calls=%async_computation.1 | async-start | bytes 8388608
  262.2 20.3 %slice-start.2 = ((s8[4718592]{0:T(1024)(128)(4,1)}), s8[4194304]{0:T(1024)(128)(4,1)S(1)}, s32[]{:S(2)}) async-start(s8[4718592]{0:T(1024)(128)(4,1)} %bitcast.93), calls=%async_computation.2 | async-start | bytes 8388608
  264.4 34.5 %copy-start.33 = (f32[512,768]{1,0:T(8,128)}, f32[512,768]{1,0:T(8,128)S(1)}, u32[]{:S(2)}) copy-start(f32[512,768]{1,0:T(8,128)S(1)} %get-tuple-element.136) | copy-start | bytes 4718596
  265.1 17.4 %slice-start.3 = ((s8[4718592]{0:T(1024)(128)(4,1)}), s8[524288]{0:T(1024)(128)(4,1)S(1)}, s32[]{:S(2)}) async-start(s8[4718592]{0:T(1024)(128)(4,1)} %bitcast.93), calls=%async_computation.3 | async-start | bytes 1048576
  299.3 33.4 %copy-start.28 = (f32[512,768]{1,0:T(8,128)}, f32[512,768]{1,0:T(8,128)S(1)}, u32[]{:S(2)}) copy-start(f32[512,768]{1,0:T(8,128)S(1)} %subtract_multiply_fusion.1) | copy-start | bytes 4718596
  301.1 31.7 %copy-start.24 = (bf16[768,768]{1,0:T(8,128)(2,1)S(1)}, bf16[768,768]{1,0:T(8,128)(2,1)}, u32[]{:S(2)}) copy-start(bf16[768,768]{1,0:T(8,128)(2,1)} %copy-done.23) | copy-start | bytes 3538948
  301.1 31.7 %copy-start.31 = (f32[512,768]{1,0:T(8,128)S(1)}, f32[512,768]{1,0:T(8,128)}, u32[]{:S(2)}) copy-start(f32[512,768]{1,0:T(8,128)} %copy-done.30) | copy-start | bytes 4718596
  301.1 31.7 %copy-start.57 = (f32[512]{0:T(512)S(1)}, f32[512]{0:T(512)}, u32[]{:S(2)}) copy-start(f32[512]{0:T(512)} %copy-done.56) | copy-start | bytes 6148
  301.1 31.7 %copy-start.60 = (f32[512]{0:T(512)S(1)}, f32[512]{0:T(512)}, u32[]{:S(2)}) copy-start(f32[512]{0:T(512)} %copy-done.59) | copy-start | bytes 6148
  301.1 31.7 %copy-start.65 = (f32[768]{0:T(1024)S(1)}, f32[768]{0:T(1024)}, u32[]{:S(2)}) copy-start(f32[768]{0:T(1024)} %param.33) | copy-start | bytes 9220
  341.0 14.0 %copy-start.20 = (bf16[768,768]{1,0:T(8,128)(2,1)S(1)}, bf16[768,768]{1,0:T(8,128)(2,1)}, u32[]{:S(2)}) copy-start(bf16[768,768]{1,0:T(8,128)(2,1)} %copy-done.19) | copy-start | bytes 3538948
  367.2 7.2 %copy-start.34 = (f32[512,768]{1,0:T(8,128)S(1)}, f32[512,768]{1,0:T(8,128)}, u32[]{:S(2)}) copy-start(f32[512,768]{1,0:T(8,128)} %copy-done.33) | copy-start | bytes 4718596
  367.2 7.2 %copy-start.73 = (bf16[512,3072]{1,0:T(8,128)(2,1)S(1)}, bf16[512,3072]{1,0:T(8,128)(2,1)}, u32[]{:S(2)}) copy-start(bf16[512,3072]{1,0:T(8,128)(2,1)} %copy-done.72) | copy-start | bytes 9437188
  562.4 16.5 %copy-start.26 = (bf16[16,2,384,384]{3,2,1,0:T(8,128)(2,1)S(1)}, bf16[16,2,384,384]{3,2,1,0:T(8,128)(2,1)}, u32[]{:S(2)}) copy-start(bf16[16,2,384,384]{3,2,1,0:T(8,128)(2,1)} %get-tuple-element.72) | copy-start | bytes 28311556
  (55 other events, 104.2 us)

commit v2 on v1

--- a/solution.py
+++ b/solution.py
@@ -11,7 +11,8 @@
 BLOCK_ROWS = 128
 RET_BLOCKS = 8
 PAIR = 2 * HEAD_DIM
-VMEM_LIMIT = 56 << 20
+VMEM_LIMIT = 60 << 20
+BACKWARD_VMEM = 63 << 20
 
 epsilon = 1e-05
 bf16 = jnp.bfloat16
@@ -136,25 +137,29 @@
     return grad_queries, grad_keys, grad_values
 
 
-def self_variants(narrow, at):
-    for n in range(narrow):
-        yield 0, n + 1, at == n
-        yield 1, 2 * narrow - n, at == n
+def self_blocks(narrow, total_rows, at):
+    chunk = total_rows // (2 * narrow)
+    for block in range(total_rows // BLOCK_ROWS):
+        which, within = divmod(block * BLOCK_ROWS, chunk)
+        if which < narrow:
+            owner, local_row = which, within
+        else:
+            owner, local_row = 2 * narrow - 1 - which, chunk + within
+        yield local_row, (block + 1) * BLOCK_ROWS, at == owner
 
 
 def self_forward_kernel(narrow, at_ref, q_ref, k_ref, v_ref, o_ref, log_ref):
-    rows = q_ref.shape[0] // 2
-    for chunk, seen, taken in self_variants(narrow, at_ref[0]):
+    for local_row, seen, taken in self_blocks(narrow, k_ref.shape[0], at_ref[0]):
 
         @pl.when(taken)
         def _():
-            mine = pl.ds(chunk * rows, rows)
-            keys = pl.ds(0, seen * rows)
+            mine = pl.ds(local_row, BLOCK_ROWS)
+            keys = pl.ds(0, seen)
             blended, log_total = pair_forward(
-                q_ref[mine], k_ref[keys], v_ref[keys], causal_edge(rows)
+                q_ref[mine], k_ref[keys], v_ref[keys], causal_edge(BLOCK_ROWS)
             )
             o_ref[mine] = blended
-            log_ref[0, pl.ds(chunk, 1)] = log_total
+            log_ref[0, pl.ds(local_row // BLOCK_ROWS, 1)] = log_total
 
 
 def self_forward(narrow, at, queries, keys, values):
@@ -168,11 +173,11 @@
             num_scalar_prefetch=1,
             grid=(pairs,),
             in_specs=[pair(rows), pair(total_rows), pair(total_rows)],
-            out_specs=[pair(rows), pl.BlockSpec((1, 2, rows), lambda g, at: (g, 0, 0))],
+            out_specs=[pair(rows), pl.BlockSpec((1, rows // BLOCK_ROWS, 2 * BLOCK_ROWS), lambda g, at: (g, 0, 0))],
         ),
         out_shape=[
             jax.ShapeDtypeStruct((rows, width), bf16),
-            jax.ShapeDtypeStruct((pairs, 2, rows), f32),
+            jax.ShapeDtypeStruct((pairs, rows // BLOCK_ROWS, 2 * BLOCK_ROWS), f32),
         ],
         compiler_params=pltpu.CompilerParams(vmem_limit_bytes=VMEM_LIMIT),
         name="self_forward",
@@ -185,18 +190,18 @@
     rows = q_ref.shape[0] // 2
     dk_sum[...] = jnp.zeros_like(dk_sum)
     dv_sum[...] = jnp.zeros_like(dv_sum)
-    for chunk, seen, taken in self_variants(narrow, at_ref[0]):
+    for local_row, seen, taken in self_blocks(narrow, k_ref.shape[0], at_ref[0]):
 
         @pl.when(taken)
         def _():
-            mine = pl.ds(chunk * rows, rows)
-            keys = pl.ds(0, seen * rows)
+            mine = pl.ds(local_row, BLOCK_ROWS)
+            keys = pl.ds(0, seen)
             grad_q, grad_k, grad_v = pair_backward(
                 q_ref[mine],
                 k_ref[keys],
                 v_ref[keys],
-                causal_edge(rows),
-                log_ref[0, pl.ds(chunk, 1)],
+                causal_edge(BLOCK_ROWS),
+                log_ref[0, pl.ds(local_row // BLOCK_ROWS, 1)],
                 o_ref[mine],
                 g_ref[mine],
             )
@@ -222,7 +227,7 @@
                 pair(rows),
                 pair(total_rows),
                 pair(total_rows),
-                pl.BlockSpec((1, 2, rows), lambda g, at: (g, 0, 0)),
+                pl.BlockSpec((1, rows // BLOCK_ROWS, 2 * BLOCK_ROWS), lambda g, at: (g, 0, 0)),
                 pair(rows),
                 pair(rows),
             ],
@@ -279,12 +284,13 @@
                 pl.BlockSpec((1, pairs, 2 * BLOCK_ROWS), lambda b, picked: (b, 0, 0)),
                 by_keys,
                 by_keys,
+                by_keys,
             ],
-            scratch_shapes=[pltpu.VMEM((keys, width), bf16)],
         ),
         out_shape=[
             jax.ShapeDtypeStruct((rows, width), bf16),
             jax.ShapeDtypeStruct((count, pairs, 2 * BLOCK_ROWS), f32),
+            jax.ShapeDtypeStruct((count * keys, width), bf16),
             jax.ShapeDtypeStruct((count * keys, width), bf16),
             jax.ShapeDtypeStruct((count * keys, width), bf16),
         ],
@@ -407,19 +413,24 @@
 
 
 def gather_kernel(a_rows, b_rows, *refs):
-    encoded, weights = refs[0], refs[1:11]
+    encoded_in, weights_in = refs[0], refs[1:11]
     everything, full = refs[11], refs[12:22]
-    (own_sem, half_sem, flow_send, flow_recv, weight_send, weight_recv) = refs[22:]
+    encoded, weights = refs[22], refs[23:33]
+    load_sem, own_sem, half_sem, flow_send, flow_recv, weight_send, weight_recv = refs[33:]
     me = Place()
     rows = encoded.shape[0]
     x, y, z, core = me.x, me.y, me.z, me.core
     low, high = z > 0, z < LINE - 1
     UP_A, DOWN_A, Y_A, UP_B, DOWN_B, Y_B, X_B, CORE_A, CORE_B = range(9)
 
+    loads = [pltpu.make_async_copy(encoded_in, encoded, load_sem.at[10])]
+    for i in range(10):
+        loads.append(pltpu.make_async_copy(weights_in[i], weights[i], load_sem.at[i]))
+    for load in loads:
+        load.start()
     own = pltpu.make_async_copy(
         encoded, everything.at[pl.ds(pl.multiple_of(me.wide * rows, 128), rows)], own_sem
     )
-    own.start()
 
     def region(i, ref, plane, part):
         if i in COLUMNS:
@@ -440,12 +451,12 @@
         halves.append(
             pltpu.make_async_copy(weights[i], region(i, full[i], x, None), half_sem.at[i])
         )
-        halves[-1].start()
 
     me.greet()
-    own.wait()
-
-    def flow(kind, owner_z, owner_y, plane, target, from_core=None):
+    for load in loads:
+        load.wait()
+
+    def flow(kind, owner_z, owner_y, plane, target, from_core=None, held=False):
         owner = owner_z * 2 + owner_y
         start = owner * (2 * rows) + (core if from_core is None else from_core) * rows
         if plane is None:
@@ -454,8 +465,12 @@
             start = start + a_rows + plane * b_rows
             size, slot = b_rows, owner + (plane * 8 if kind == CORE_B else 0)
         piece = everything.at[pl.ds(pl.multiple_of(start, 16), size)]
+        source = piece
+        if held:
+            first = 0 if plane is None else pl.multiple_of(a_rows + plane * b_rows, 16)
+            source = encoded.at[pl.ds(first, size)]
         return pltpu.make_async_remote_copy(
-            src_ref=piece,
+            src_ref=source,
             dst_ref=piece,
             send_sem=flow_send.at[kind, slot],
             recv_sem=flow_recv.at[kind, slot],
@@ -468,32 +483,32 @@
     across = me.at(x=1 - x)
     above, below = me.at(z=z + 1), me.at(z=z - 1)
 
-    def up_a(oz):
-        return flow(UP_A, oz, y, None, above)
-
-    def down_a(oz):
-        return flow(DOWN_A, oz, y, None, below)
-
-    def up_b(oz, oy):
-        return flow(UP_B, oz, oy, x, above)
-
-    def down_b(oz, oy):
-        return flow(DOWN_B, oz, oy, x, below)
-
-    def y_a(oz, oy):
-        return flow(Y_A, oz, oy, None, beside)
-
-    def y_b(oy):
-        return flow(Y_B, z, oy, x, beside)
+    def up_a(oz, held=False):
+        return flow(UP_A, oz, y, None, above, held=held)
+
+    def down_a(oz, held=False):
+        return flow(DOWN_A, oz, y, None, below, held=held)
+
+    def up_b(oz, oy, held=False):
+        return flow(UP_B, oz, oy, x, above, held=held)
+
+    def down_b(oz, oy, held=False):
+        return flow(DOWN_B, oz, oy, x, below, held=held)
+
+    def y_a(oz, oy, held=False):
+        return flow(Y_A, oz, oy, None, beside, held=held)
+
+    def y_b(oy, held=False):
+        return flow(Y_B, z, oy, x, beside, held=held)
 
     def x_b(oz, oy, plane):
         return flow(X_B, oz, oy, plane, across)
 
-    def core_a(oz, oy, from_core=None):
-        return flow(CORE_A, oz, oy, None, sibling, from_core)
-
-    def core_b(oz, oy, plane, from_core=None):
-        return flow(CORE_B, oz, oy, plane, sibling, from_core)
+    def core_a(oz, oy, from_core=None, held=False):
+        return flow(CORE_A, oz, oy, None, sibling, from_core, held)
+
+    def core_b(oz, oy, plane, from_core=None, held=False):
+        return flow(CORE_B, oz, oy, plane, sibling, from_core, held)
 
     def weight(way, i, plane, part):
         piece = region(i, full[i], plane, part)
@@ -512,15 +527,18 @@
             device_id_type=MESH,
         )
 
-    y_b(y).start()
-    y_a(z, y).start()
-    pl.when(high)(lambda: up_a(z).start())
-    pl.when(low)(lambda: down_a(z).start())
-    core_a(z, y).start()
-    core_b(z, y, 0).start()
-    core_b(z, y, 1).start()
+    y_b(y, True).start()
+    y_a(z, y, True).start()
+    pl.when(high)(lambda: up_a(z, True).start())
+    pl.when(low)(lambda: down_a(z, True).start())
     for i in range(10):
         weight(0, i, x, core).start()
+    core_a(z, y, held=True).start()
+    core_b(z, y, 0, held=True).start()
+    core_b(z, y, 1, held=True).start()
+    own.start()
+    for i in range(10):
+        halves[i].start()
 
     y_b(1 - y).wait_recv()
     core_b(z, 1 - y, x).start()
@@ -550,9 +568,9 @@
                 pl.when(under >= 0)(lambda: pass_a(under, up_a, high, up_a))
                 pl.when(over < LINE)(lambda: pass_a(over, down_a, low, down_a))
             if kind == 1 and step == 0:
-                for oy in (y, 1 - y):
-                    pl.when(high)(lambda oy=oy: up_b(z, oy).start())
-                    pl.when(low)(lambda oy=oy: down_b(z, oy).start())
+                for oy, held in ((y, True), (1 - y, False)):
+                    pl.when(high)(lambda oy=oy, held=held: up_b(z, oy, held).start())
+                    pl.when(low)(lambda oy=oy, held=held: down_b(z, oy, held).start())
             if kind == 1 and step > 0:
                 pl.when(under >= 0)(lambda: pass_b(under, up_b, high, up_b))
                 pl.when(over < LINE)(lambda: pass_b(over, down_b, low, down_b))
@@ -604,6 +622,7 @@
             for oy in range(2):
                 down_b(oz, oy).wait_send()
 
+    own.wait()
     for i in range(10):
         halves[i].wait()
         weight(0, i, x, core).wait_send()
@@ -625,9 +644,11 @@
         out_shape=shapes,
         in_specs=[pl.BlockSpec(memory_space=pl.ANY)] * 11,
         out_specs=[pl.BlockSpec(memory_space=pl.ANY)] * 11,
-        scratch_shapes=[dma, dma((10,)), dma((9, 16)), dma((9, 16)), dma((2, 10)), dma((2, 10))],
+        scratch_shapes=[pltpu.VMEM((rows, width), bf16)]
+        + [pltpu.VMEM(w.shape, bf16) for w in weights]
+        + [dma((11,)), dma, dma((10,)), dma((9, 16)), dma((9, 16)), dma((2, 10)), dma((2, 10))],
         compiler_params=pltpu.CompilerParams(
-            collective_id=0, has_side_effects=True, vmem_limit_bytes=4 << 20
+            collective_id=0, has_side_effects=True, vmem_limit_bytes=VMEM_LIMIT
         ),
         name="gather",
     )(encoded, *weights)
@@ -635,38 +656,51 @@
 
 
 TILE = 384
+HALF = TILE // 2
+PART = HALF // LINE
 UNITS = 16
-
-
-def share_of(refs, unit, core, plane):
-    narrow_units = (0, 1, 2, 4, 5, 6)
-    if unit < 6:
-        ref, row, column = refs[narrow_units[unit]], core * TILE, plane * TILE
-    elif unit < 8:
-        ref, row, column = refs[(3, 7)[unit - 6]], plane * TILE, core * TILE
-    elif unit < 12:
-        ref, row, column = refs[8], core * TILE, plane * 4 * TILE + (unit - 8) * TILE
-    else:
-        ref, row, column = refs[9], plane * 4 * TILE + (unit - 12) * TILE, core * TILE
-    return ref.at[
-        pl.ds(pl.multiple_of(row, 128), TILE), pl.ds(pl.multiple_of(column, 128), TILE)
-    ]
-
-
-def reduce_kernel(*refs):
-    grads = refs[:10]
-    theirs, mine, made, norms = refs[10:14]
-    sums_out, mine_out, theirs_out, made_out, norms_out = refs[14:19]
+SLOTS = 8
+UNIT_WEIGHTS = (8, 8, 8, 8, 9, 9, 9, 9, 7, 5, 6, 4, 3, 0, 1, 2)
+LAST_TICK = UNITS + 6
+
+
+def share_corner(unit, core, plane):
+    if unit < 4:
+        return core * TILE, (plane * 4 + unit) * TILE
+    if unit < 8:
+        return (plane * 4 + unit - 4) * TILE, core * TILE
+    if unit in (8, 12):
+        return plane * TILE, core * TILE
+    return core * TILE, plane * TILE
+
+
+def backward_kernel(*refs):
     (
-        own, from_core, from_x, from_y, from_z, total, rows_in, rows_got, norm_all, norm_in,
-        own_sem, core_send, core_recv, x_send, x_recv, y_send, y_recv, z_send, z_recv,
-        gz_send, gz_recv, gy_send, gy_recv, gc_send, gc_recv, out_sem,
-        extra_send, extra_recv, norm_send, norm_recv,
-    ) = refs[19:]
+        expand_grad, reduce_grad, cross_out_grad, picked_rows, keys_in, values_in, q_cross, a_cross,
+        g_cross, log_cross, first_low, cross_query, g_second, first_normal, first_inverse, first_gain,
+        a_self, self_out, q_self, k_self, v_self, log_self, hidden, self_query, self_key, self_value,
+        made, norms,
+    ) = refs[:28]
+    sums_out, mine_out, theirs_out, made_out, norms_out = refs[28:33]
+    (
+        own, from_core, from_a, from_b, from_z, summed, pool, pool32, both, staged, dq_cross, dk_sum,
+        dv_sum, theirs, rows_in, rows_got, norm_all, norm_in,
+        own_sem, core_send, core_recv, a_send, a_recv, b_send, b_recv, z_send, z_recv, gz_send, gz_recv,
+        gy_send, gy_recv, gc_send, gc_recv, keep_sem, load_sem, kv_sem, e_sem, extra_send, extra_recv,
+        norm_send, norm_recv,
+    ) = refs[33:]
     me = Place()
     x, y, z, core = me.x, me.y, me.z, me.core
-    half, part = TILE // 2, TILE // 2 // LINE
     sibling, beside, across = me.at(core=1 - core), me.at(y=1 - y), me.at(x=1 - x)
+    width = 2 * TILE
+    keys = RET_BLOCKS * BLOCK_ROWS
+    rows = q_cross.shape[0]
+    blocks = rows // BLOCK_ROWS
+    pairs = width // PAIR
+    chunk = rows // 2
+
+    def rem(u, n):
+        return u % n if isinstance(u, int) else lax.rem(u, n)
 
     def remote(src, dst, send, recv, target):
         return pltpu.make_async_remote_copy(
@@ -674,200 +708,456 @@
             device_id=target, device_id_type=MESH,
         )
 
-    def own_copy(unit, plane):
+
+    def share(ref, unit, of_core, plane, part):
+        row, column = share_corner(unit, of_core, plane)
+        return ref.at[
+            pl.ds(pl.multiple_of(row + part * HALF, 64), HALF),
+            pl.ds(pl.multiple_of(column, 128), TILE),
+        ]
+
+    def own_copy(ref, unit, plane, part):
         return pltpu.make_async_copy(
-            share_of(grads, unit, core, plane), own.at[unit, plane], own_sem.at[unit, plane]
-        )
-
-    def to_core(unit, plane):
+            share(ref, unit, core, plane, part),
+            own.at[unit % SLOTS, plane, part],
+            own_sem.at[unit % SLOTS, plane * 2 + part],
+        )
+
+    def core_copy(src, u, plane, part):
         return remote(
-            share_of(grads, unit, 1 - core, plane), from_core.at[unit, plane],
-            core_send.at[unit, plane], core_recv.at[unit, plane], sibling,
-        )
-
-    def to_x(u):
-        return remote(own.at[u, 1 - x], from_x.at[u], x_send.at[u], x_recv.at[u], across)
-
-    def to_y(u):
-        rows = pl.ds(pl.multiple_of((1 - y) * half, 16), half)
-        return remote(own.at[u, x, rows], from_y.at[u], y_send.at[u], y_recv.at[u], beside)
-
-    def to_z(u, d):
+            src, from_core.at[u, plane, part], core_send.at[u, plane * 2 + part],
+            core_recv.at[u, plane * 2 + part], sibling,
+        )
+
+    def to_core(ref, unit, plane, part):
+        return core_copy(share(ref, unit, 1 - core, plane, part), unit, plane, part)
+
+    def a_first(u, slot):
+        return remote(own.at[slot, 1 - x], from_a.at[u], a_send.at[u], a_recv.at[u], across)
+
+    def a_second(u, slot):
+        return remote(own.at[slot, :, 1 - y], from_a.at[u], a_send.at[u], a_recv.at[u], beside)
+
+    def b_first(u, slot):
+        return remote(own.at[slot, x, 1 - y], from_b.at[u], b_send.at[u], b_recv.at[u], beside)
+
+    def b_second(u, slot):
+        return remote(own.at[slot, 1 - x, y], from_b.at[u], b_send.at[u], b_recv.at[u], across)
+
+    def to_z(u, slot, d):
         other = lax.rem(z + d, LINE)
-        rows = pl.ds(pl.multiple_of(y * half + other * part, 16), part)
+        piece = own.at[slot, x, y, pl.ds(pl.multiple_of(other * PART, 16), PART)]
         return remote(
-            own.at[u, x, rows], from_z.at[u, d - 1], z_send.at[u, d - 1], z_recv.at[u, d - 1],
-            me.at(z=other),
-        )
+            piece, from_z.at[u, d - 1], z_send.at[u, d - 1], z_recv.at[u, d - 1], me.at(z=other)
+        )
+
+    def result(u, of_z):
+        return sums_out.at[u, core, pl.ds(pl.multiple_of(y * HALF + of_z * PART, 16), PART)]
+
+    def keep(u):
+        return pltpu.make_async_copy(summed.at[u], result(u, z), keep_sem.at[u])
 
     def gather_z(u, d):
-        rows = pl.ds(pl.multiple_of(y * half + z * part, 16), part)
-        piece = total.at[u, core, rows]
         return remote(
-            piece, piece, gz_send.at[u, d - 1], gz_recv.at[u, d - 1],
+            summed.at[u], result(u, z), gz_send.at[u, d - 1], gz_recv.at[u, d - 1],
             me.at(z=lax.rem(z + d, LINE)),
         )
 
     def gathered_z(u, d):
-        rows = pl.ds(pl.multiple_of(y * half + lax.rem(z + LINE - d, LINE) * part, 16), part)
-        piece = total.at[u, core, rows]
-        return remote(piece, piece, gz_send.at[u, d - 1], gz_recv.at[u, d - 1], beside)
+        return remote(
+            summed.at[u], result(u, lax.rem(z + LINE - d, LINE)), gz_send.at[u, d - 1],
+            gz_recv.at[u, d - 1], beside,
+        )
 
     def gather_y(u, at_y):
-        piece = total.at[u, core, pl.ds(pl.multiple_of(at_y * half, 16), half)]
+        piece = sums_out.at[u, core, pl.ds(pl.multiple_of(at_y * HALF, 16), HALF)]
         return remote(piece, piece, gy_send.at[u], gy_recv.at[u], beside)
 
     def gather_core(u, at_core):
-        piece = total.at[u, at_core]
+        piece = sums_out.at[u, at_core]
         return remote(piece, piece, gc_send.at[u], gc_recv.at[u], sibling)
-
-    def put_out(u):
-        return pltpu.make_async_copy(total.at[u], sums_out.at[u], out_sem.at[u])
-
-    rows_copy = remote(theirs, rows_in, extra_send.at[0], extra_recv.at[0], across)
-    made_copy = remote(made, made_out, extra_send.at[1], extra_recv.at[1], across)
-    got_copy = remote(rows_got, theirs_out, extra_send.at[2], extra_recv.at[2], across)
-
-    for unit in range(UNITS):
-        for plane in range(2):
-            own_copy(unit, plane).start()
-    me.greet()
-    rows_copy.start()
-    for unit in range(UNITS):
-        for plane in range(2):
-            to_core(unit, plane).start()
-
-    norm_all[...] = norms[...]
-    along_z = tuple(me.at(z=lax.rem(z + d, LINE)) for d in range(1, LINE))
-    slot = 0
-    for targets in ((sibling,), (across,), (beside,), along_z):
-        copies = []
-        for target in targets:
-            copies.append(
-                remote(norm_all, norm_in.at[slot], norm_send.at[slot], norm_recv.at[slot], target)
-            )
-            copies[-1].start()
-            slot += 1
-        for copy in copies:
-            copy.wait()
-        for k in range(slot - len(copies), slot):
-            norm_all[...] += norm_in[k]
-    norms_out[...] = norm_all[...]
-
-    for unit in range(UNITS):
-        for plane in range(2):
-            own_copy(unit, plane).wait()
 
     def plus(a, b):
         return (a.astype(f32) + b.astype(f32)).astype(bf16)
 
-    def step(t, carry):
-        def at(lag):
-            u = t - lag
-            return u, jnp.logical_and(u >= 0, u < UNITS)
-
-        u0, on0 = at(0)
-
-        @pl.when(on0)
+    def by_order(u, first, second):
+        if isinstance(u, int):
+            (first if u % 2 == 0 else second)()
+        else:
+            pl.when(lax.rem(u, 2) == 0)(first)
+            pl.when(lax.rem(u, 2) == 1)(second)
+
+    def stage_core(u):
+        slot = rem(u, SLOTS)
+        for plane in range(2):
+            for part in range(2):
+                core_copy(own.at[slot, plane, part], u, plane, part).wait_recv()
+        own[slot] = plus(own[slot], from_core[u])
+        by_order(u, lambda: a_first(u, slot).start(), lambda: a_second(u, slot).start())
+
+    def stage_a(u):
+        slot = rem(u, SLOTS)
+
+        def first():
+            a_first(u, slot).wait()
+            own[slot, x] = plus(own[slot, x], from_a[u])
+            b_first(u, slot).start()
+
+        def second():
+            a_second(u, slot).wait()
+            own[slot, :, y] = plus(own[slot, :, y], from_a[u])
+            b_second(u, slot).start()
+
+        by_order(u, first, second)
+
+    def stage_b(u):
+        slot = rem(u, SLOTS)
+        by_order(u, lambda: b_first(u, slot).wait(), lambda: b_second(u, slot).wait())
+        own[slot, x, y] = plus(own[slot, x, y], from_b[u])
+        for d in range(1, LINE):
+            to_z(u, slot, d).start()
+
+    def stage_z(u):
+        slot = rem(u, SLOTS)
+        for d in range(1, LINE):
+            to_z(u, slot, d).wait()
+        total = own[slot, x, y, pl.ds(pl.multiple_of(z * PART, 16), PART)].astype(f32)
+        for d in range(1, LINE):
+            total += from_z[u, d - 1].astype(f32)
+        summed[u] = total.astype(bf16)
+        keep(u).start()
+        for d in range(1, LINE):
+            gather_z(u, d).start()
+
+    def stage_gather_z(u):
+        keep(u).wait()
+        for d in range(1, LINE):
+            gathered_z(u, d).wait_recv()
+            gather_z(u, d).wait_send()
+        gather_y(u, y).start()
+
+    def stage_gather_y(u):
+        gather_y(u, 1 - y).wait_recv()
+        gather_y(u, y).wait_send()
+        gather_core(u, core).start()
+
+    def stage_gather_core(u):
+        gather_core(u, 1 - core).wait_recv()
+        gather_core(u, core).wait_send()
+
+    stages = (
+        (0, stage_core), (2, stage_a), (3, stage_b), (4, stage_z), (5, stage_gather_z),
+        (6, stage_gather_y), (7, stage_gather_core),
+    )
+
+    def tick(t):
+        for lag, stage in stages:
+            if isinstance(t, int):
+                if 0 <= t - lag < UNITS:
+                    stage(t - lag)
+            else:
+                u = t - lag
+                pl.when(jnp.logical_and(u >= 0, u < UNITS))(lambda stage=stage, u=u: stage(u))
+
+    KV, E, Q, O, G, FIRST, CROSS_Q, A_SELF, SELF_OUT = (
+        0, 4096, 5120, 5632, 6144, 6656, 7168, 7936, 8448
+    )
+    QS, KS, VS, DQ, DK, DV, HIDDEN, DA = 0, 512, 1536, 2560, 3072, 4096, 5120, 6144
+    WQ, WK, WV = 0, 768, 1536
+
+    def load(src, row, sem, into=pool):
+        return pltpu.make_async_copy(src, into.at[pl.ds(row, src.shape[0])], load_sem.at[sem])
+
+    def kv_copy(b, which):
+        src = (keys_in, values_in)[which].at[pl.ds(pl.multiple_of(b * keys, 128), keys)]
+        row = pl.multiple_of(lax.rem(b, 2) * (2 * keys) + which * keys, 128)
+        return pltpu.make_async_copy(src, pool.at[pl.ds(row, keys)], kv_sem.at[lax.rem(b, 2), which])
+
+    def e_copy(b):
+        src = picked_rows.at[pl.ds(pl.multiple_of(b * keys, 128), keys)]
+        return pltpu.make_async_copy(src, pool.at[pl.ds(E, keys)], e_sem)
+
+    early = [
+        load(q_cross, Q, 0), load(a_cross, O, 1), load(g_cross, G, 2), load(first_low, FIRST, 3),
+        load(cross_query, CROSS_Q, 4), load(a_self, A_SELF, 5), load(self_out, SELF_OUT, 6),
+    ]
+    for which in range(2):
+        kv_copy(jnp.int32(0), which).start()
+    for copy in early:
+        copy.start()
+    ready = [(expand_grad, u) for u in range(4)] + [(reduce_grad, u) for u in range(4, 8)]
+    corners = [(plane, part) for plane in range(2) for part in range(2)]
+    for ref, unit in ready:
+        for plane, part in corners:
+            own_copy(ref, unit, plane, part).start()
+    me.greet()
+    for ref, unit in ready + [(cross_out_grad, 8)]:
+        for plane, part in corners:
+            to_core(ref, unit, plane, part).start()
+    made_copy = remote(made, made_out, extra_send.at[1], extra_recv.at[1], across)
+    made_copy.start()
+    both_sums = pool32
+    both_sums[...] = jnp.zeros_like(both_sums)
+    for copy in early[:3]:
+        copy.wait()
+    for ref, unit in ready:
+        for plane, part in corners:
+            own_copy(ref, unit, plane, part).wait()
+
+    def at_row(row):
+        return pl.ds(pl.multiple_of(row, 128), BLOCK_ROWS)
+
+    def cross_step(i, carry):
+        b, g = lax.div(i, pairs), lax.rem(i, pairs)
+
+        @pl.when(g == 0)
         def _():
-            for plane in range(2):
-                to_core_wait(u0, plane)
-            own[u0] = plus(own[u0], from_core[u0])
-            to_x(u0).start()
-
-        u1, on1 = at(2)
-
-        @pl.when(on1)
+            for which in range(2):
+                kv_copy(b, which).wait()
+            e_copy(b).start()
+
+            @pl.when(b + 1 < blocks)
+            def _():
+                for which in range(2):
+                    kv_copy(b + 1, which).start()
+
+        lanes = pl.ds(pl.multiple_of(g * PAIR, PAIR), PAIR)
+        row = pl.multiple_of(b * BLOCK_ROWS, BLOCK_ROWS)
+        key_row = pl.multiple_of(lax.rem(b, 2) * (2 * keys), 128)
+        grad_q, grad_k, grad_v = pair_backward(
+            pool[at_row(Q + row), lanes],
+            pool[pl.ds(key_row, keys), lanes],
+            pool[pl.ds(pl.multiple_of(key_row + keys, 128), keys), lanes],
+            None,
+            log_cross[b, pl.ds(g, 1)],
+            pool[at_row(O + row), lanes],
+            pool[at_row(G + row), lanes],
+        )
+        dq_cross[pl.ds(row, BLOCK_ROWS), lanes] = grad_q.astype(bf16)
+        both[:, lanes] = grad_k.astype(bf16)
+        both[:, pl.ds(pl.multiple_of(width + g * PAIR, PAIR), PAIR)] = grad_v.astype(bf16)
+
+        @pl.when(g == pairs - 1)
         def _():
-            to_x(u1).wait()
-            own[u1, x] = plus(own[u1, x], from_x[u1])
-            to_y(u1).start()
-
-        u2, on2 = at(3)
-
-        @pl.when(on2)
-        def _():
-            to_y(u2).wait()
-            rows = pl.ds(pl.multiple_of(y * half, 16), half)
-            own[u2, x, rows] = plus(own[u2, x, rows], from_y[u2])
-            for d in range(1, LINE):
-                to_z(u2, d).start()
-
-        u3, on3 = at(4)
-
-        @pl.when(on3)
-        def _():
-            for d in range(1, LINE):
-                to_z(u3, d).wait()
-            rows = pl.ds(pl.multiple_of(y * half + z * part, 16), part)
-            summed = own[u3, x, rows].astype(f32)
-            for d in range(1, LINE):
-                summed += from_z[u3, d - 1].astype(f32)
-            total[u3, core, rows] = summed.astype(bf16)
-            for d in range(1, LINE):
-                gather_z(u3, d).start()
-
-        u4, on4 = at(5)
-
-        @pl.when(on4)
-        def _():
-            for d in range(1, LINE):
-                gathered_z(u4, d).wait_recv()
-                gather_z(u4, d).wait_send()
-            gather_y(u4, y).start()
-
-        u5, on5 = at(6)
-
-        @pl.when(on5)
-        def _():
-            gather_y(u5, 1 - y).wait_recv()
-            gather_y(u5, y).wait_send()
-            gather_core(u5, core).start()
-
-        u6, on6 = at(7)
-
-        @pl.when(on6)
-        def _():
-            gather_core(u6, 1 - core).wait_recv()
-            gather_core(u6, core).wait_send()
-            put_out(u6).start()
-
-        @pl.when(t == UNITS)
+            e_copy(b).wait()
+            both_sums[pl.ds(0, width)] += dot_tn(pool[pl.ds(E, keys)], both[:, :width])
+            both_sums[pl.ds(width, width)] += dot_tn(pool[pl.ds(E, keys)], both[:, width:])
+
+        pl.when(lax.rem(i, 4) == 3)(lambda: tick(lax.div(i, 4)))
+        return carry
+
+    lax.fori_loop(0, blocks * pairs, cross_step, 0)
+
+    def hand_over(unit):
+        ref = staged.at[unit % 2]
+        for plane, part in corners:
+            to_core(ref, unit, plane, part).start()
+            own_copy(ref, unit, plane, part).start()
+
+    def kept(unit):
+        for plane, part in corners:
+            own_copy(staged.at[unit % 2], unit, plane, part).wait()
+
+    def left(unit):
+        for plane, part in corners:
+            to_core(staged.at[unit % 2], unit, plane, part).wait_send()
+
+    def handed_over(unit):
+        kept(unit)
+        left(unit)
+
+    late = [load(q_self, QS, 7), load(k_self, KS, 8), load(v_self, VS, 9), load(hidden, HIDDEN, 10)]
+    for copy in late:
+        copy.start()
+    for plane, part in corners:
+        own_copy(cross_out_grad, 8, plane, part).start()
+    staged[1] = both_sums[pl.ds(0, width)].astype(bf16)
+    hand_over(9)
+    tick(6)
+    staged[0] = both_sums[pl.ds(width, width)].astype(bf16)
+    hand_over(10)
+    g_copy = load(g_second, 0, 11, pool32)
+    n_copy = load(first_normal, rows, 12, pool32)
+    g_copy.start()
+    n_copy.start()
+    for copy in early[3:]:
+        copy.wait()
+    tick(7)
+    handed_over(9)
+    staged[1] = dot_tn(pool[pl.ds(FIRST, rows)], dq_cross[...]).astype(bf16)
+    hand_over(11)
+
+    g_copy.wait()
+    n_copy.wait()
+    normal = pool32[pl.ds(rows, rows)]
+    grad_out = pool32[pl.ds(0, rows)] + dot_nt(dq_cross[...], pool[pl.ds(CROSS_Q, width)])
+    scaled = grad_out * first_gain[...]
+    grad_in = first_inverse[...] * (
+        scaled
+        - jnp.mean(scaled, axis=-1, keepdims=True)
+        - normal * jnp.mean(scaled * normal, axis=-1, keepdims=True)
+    )
+    norm_all[...] = norms[...]
+    norm_all[pl.ds(0, 1)] = jnp.sum(grad_out * normal, axis=0, keepdims=True)
+    norm_all[pl.ds(1, 1)] = jnp.sum(grad_out, axis=0, keepdims=True)
+    pool32[pl.ds(2 * rows, rows)] = grad_in
+    grad_low = grad_in.astype(bf16)
+    pool[pl.ds(DA, rows)] = dot_nt(grad_low, pool[pl.ds(SELF_OUT, width)]).astype(bf16)
+    for plane, part in corners:
+        own_copy(cross_out_grad, 8, plane, part).wait()
+    tick(8)
+    handed_over(10)
+    staged[0] = dot_tn(pool[pl.ds(A_SELF, rows)], grad_low).astype(bf16)
+    hand_over(12)
+
+    along_z = tuple(me.at(z=lax.rem(z + d, LINE)) for d in range(1, LINE))
+    rounds = ((sibling,), (across,), (beside,), along_z)
+
+    def norm_copies(which):
+        first = min(which, 3)
+        return [
+            remote(
+                norm_all, norm_in.at[first + k], norm_send.at[first + k], norm_recv.at[first + k], target
+            )
+            for k, target in enumerate(rounds[which])
+        ]
+
+    def norm_start(which):
+        for copy in norm_copies(which):
+            copy.start()
+
+    def norm_finish(which):
+        for copy in norm_copies(which):
+            copy.wait()
+        for k in range(len(rounds[which])):
+            norm_all[...] += norm_in[which + k]
+
+    norm_start(0)
+
+    for copy in late:
+        copy.wait()
+    kept(11)
+    kept(12)
+
+    def self_step(g, carry):
+        lanes = pl.ds(pl.multiple_of(g * PAIR, PAIR), PAIR)
+        dk_sum[...] = jnp.zeros_like(dk_sum)
+        dv_sum[...] = jnp.zeros_like(dv_sum)
+        for local_row, seen, taken in self_blocks(2, hidden.shape[0], x):
+
+            @pl.when(taken)
+            def _():
+                mine = pl.ds(local_row, BLOCK_ROWS)
+                grad_q, grad_k, grad_v = pair_backward(
+                    pool[pl.ds(QS + local_row, BLOCK_ROWS), lanes],
+                    pool[pl.ds(KS, seen), lanes],
+                    pool[pl.ds(VS, seen), lanes],
+                    causal_edge(BLOCK_ROWS),
+                    log_self[g, pl.ds(local_row // BLOCK_ROWS, 1)],
+                    a_self_rows(local_row, lanes),
+                    pool[pl.ds(DA + local_row, BLOCK_ROWS), lanes],
+                )
+                pool[pl.ds(DQ + local_row, BLOCK_ROWS), lanes] = grad_q.astype(bf16)
+                dk_sum[pl.ds(0, seen)] += grad_k
+                dv_sum[pl.ds(0, seen)] += grad_v
+
+        pool[pl.ds(DK, hidden.shape[0]), lanes] = dk_sum[...].astype(bf16)
+        pool[pl.ds(DV, hidden.shape[0]), lanes] = dv_sum[...].astype(bf16)
+        pl.when(lax.rem(g, 2) == 1)(lambda: tick(9 + lax.div(g, 2)))
+        return carry
+
+    def a_self_rows(local_row, lanes):
+        return pool[pl.ds(A_SELF + local_row, BLOCK_ROWS), lanes]
+
+    lax.fori_loop(0, pairs, self_step, 0)
+    norm_finish(0)
+    norm_start(1)
+    last_loads = [load(self_query, WQ, 13), load(self_key, WK, 14), load(self_value, WV, 15)]
+    for copy in last_loads:
+        copy.start()
+
+    left(11)
+    low_rows = pl.ds(pl.multiple_of(HIDDEN + x * chunk, 128), chunk)
+    high_rows = pl.ds(pl.multiple_of(HIDDEN + (3 - x) * chunk, 128), chunk)
+    all_rows = hidden.shape[0]
+    staged[1] = (
+        dot_tn(pool[low_rows], pool[pl.ds(DQ, chunk)])
+        + dot_tn(pool[high_rows], pool[pl.ds(DQ + chunk, chunk)])
+    ).astype(bf16)
+    hand_over(13)
+    norm_finish(1)
+    norm_start(2)
+    left(12)
+    staged[0] = dot_tn(pool[pl.ds(HIDDEN, all_rows)], pool[pl.ds(DK, all_rows)]).astype(bf16)
+    hand_over(14)
+    tick(12)
+    handed_over(13)
+    staged[1] = dot_tn(pool[pl.ds(HIDDEN, all_rows)], pool[pl.ds(DV, all_rows)]).astype(bf16)
+    hand_over(15)
+    norm_finish(2)
+    norm_start(3)
+    tick(13)
+    handed_over(14)
+    handed_over(15)
+
+    for copy in last_loads:
+        copy.wait()
+
+    def row_grads(at_chunk):
+        dk = pool[pl.ds(pl.multiple_of(DK + at_chunk * chunk, 128), chunk)]
+        dv = pool[pl.ds(pl.multiple_of(DV + at_chunk * chunk, 128), chunk)]
+        return dot_nt(dk, pool[pl.ds(WK, width)]) + dot_nt(dv, pool[pl.ds(WV, width)])
+
+    theirs[pl.ds(0, chunk)] = row_grads(1 - x).astype(bf16)
+    theirs[pl.ds(chunk, chunk)] = row_grads(2 + x).astype(bf16)
+    rows_copy = remote(theirs, rows_in, extra_send.at[0], extra_recv.at[0], across)
+    got_copy = remote(rows_got, theirs_out, extra_send.at[2], extra_recv.at[2], across)
+    rows_copy.start()
+    tick(14)
+    for k, at_chunk in enumerate((x, 3 - x)):
+        piece = pl.ds(k * chunk, chunk)
+        mine_out[piece] = (
+            row_grads(at_chunk)
+            + dot_nt(pool[pl.ds(DQ + k * chunk, chunk)], pool[pl.ds(WQ, width)])
+            + pool32[pl.ds(2 * rows + k * chunk, chunk)]
+        )
+    norm_finish(3)
+    norms_out[...] = norm_all[...]
+
+    def last_step(t, carry):
+        tick(t)
+
+        @pl.when(t == 17)
         def _():
             rows_copy.wait()
-            summed = mine[...] + rows_in[...].astype(f32)
-            mine_out[...] = summed
-            rows_got[...] = summed.astype(bf16)
+            whole = mine_out[...] + rows_in[...].astype(f32)
+            mine_out[...] = whole
+            rows_got[...] = whole.astype(bf16)
             got_copy.start()
-            made_copy.start()
 
         return carry
 
-    def to_core_wait(u, plane):
-        piece = remote(
-            own.at[u, plane], from_core.at[u, plane], core_send.at[u, plane],
-            core_recv.at[u, plane], sibling,
-        )
-        piece.wait_recv()
-
-    lax.fori_loop(0, UNITS + 7, step, 0)
+    lax.fori_loop(15, LAST_TICK + 1, last_step, 0)
     got_copy.wait()
     made_copy.wait()
-    for unit in range(UNITS):
-        put_out(unit).wait()
-        for plane in range(2):
-            to_core(unit, plane).wait_send()
-
-
-def reduce_by_kernel(grads, theirs, mine, made, norms):
-    rows, width = mine.shape
+    for ref, unit in ready + [(cross_out_grad, 8)]:
+        for plane, part in corners:
+            to_core(ref, unit, plane, part).wait_send()
+
+
+def backward_by_kernel(*args):
+    rows, width = args[6].shape
+    all_rows = args[22].shape[0]
+    norms = args[27]
     anywhere = pl.BlockSpec(memory_space=pl.ANY)
     vmem = pl.BlockSpec(memory_space=pltpu.VMEM)
+    in_specs = [anywhere] * 28
+    for i in (9, 14, 15, 21, 27):
+        in_specs[i] = vmem
     dma = pltpu.SemaphoreType.DMA
-    U, T = UNITS, TILE
-    z_only = LINE - 1
+    U, T, H, Z = UNITS, TILE, HALF, LINE - 1
     return pl.pallas_call(
-        reduce_kernel,
+        backward_kernel,
         out_shape=[
             jax.ShapeDtypeStruct((U, 2, T, T), bf16),
             jax.ShapeDtypeStruct((rows, width), f32),
@@ -875,40 +1165,95 @@
             jax.ShapeDtypeStruct((rows, width), bf16),
             jax.ShapeDtypeStruct(norms.shape, f32),
         ],
-        in_specs=[anywhere] * 10 + [anywhere, vmem, anywhere, vmem],
+        in_specs=in_specs,
         out_specs=[anywhere, vmem, anywhere, anywhere, vmem],
         scratch_shapes=[
-            pltpu.VMEM((U, 2, T, T), bf16),
-            pltpu.VMEM((U, 2, T, T), bf16),
-            pltpu.VMEM((U, T, T), bf16),
-            pltpu.VMEM((U, T // 2, T), bf16),
-            pltpu.VMEM((U, z_only, T // 2 // LINE, T), bf16),
-            pltpu.VMEM((U, 2, T, T), bf16),
+            pltpu.VMEM((SLOTS, 2, 2, H, T), bf16),
+            pltpu.VMEM((U, 2, 2, H, T), bf16),
+            pltpu.VMEM((U, 2, H, T), bf16),
+            pltpu.VMEM((U, H, T), bf16),
+            pltpu.VMEM((U, Z, PART, T), bf16),
+            pltpu.VMEM((U, PART, T), bf16),
+            pltpu.VMEM((9216, width), bf16),
+            pltpu.VMEM((2 * width, width), f32),
+            pltpu.VMEM((RET_BLOCKS * BLOCK_ROWS, 2 * width), bf16),
+            pltpu.VMEM((2, width, width), bf16),
+            pltpu.VMEM((rows, width), bf16),
+            pltpu.VMEM((all_rows, PAIR), f32),
+            pltpu.VMEM((all_rows, PAIR), f32),
+            pltpu.VMEM((rows, width), bf16),
             pltpu.VMEM((rows, width), bf16),
             pltpu.VMEM((rows, width), bf16),
             pltpu.VMEM(norms.shape, f32),
             pltpu.VMEM((6,) + norms.shape, f32),
-            dma((U, 2)), dma((U, 2)), dma((U, 2)), dma((U,)), dma((U,)), dma((U,)), dma((U,)),
-            dma((U, z_only)), dma((U, z_only)), dma((U, z_only)), dma((U, z_only)),
-            dma((U,)), dma((U,)), dma((U,)), dma((U,)), dma((U,)), dma((3,)), dma((3,)),
-            dma((6,)), dma((6,)),
+            dma((SLOTS, 4)), dma((U, 4)), dma((U, 4)), dma((U,)), dma((U,)), dma((U,)), dma((U,)),
+            dma((U, Z)), dma((U, Z)), dma((U, Z)), dma((U, Z)), dma((U,)), dma((U,)), dma((U,)),
+            dma((U,)), dma((U,)), dma((16,)), dma((2, 2)), dma, dma((3,)), dma((3,)), dma((6,)),
+            dma((6,)),
         ],
         compiler_params=pltpu.CompilerParams(
-            collective_id=1, has_side_effects=True, vmem_limit_bytes=VMEM_LIMIT
+            collective_id=1, has_side_effects=True, vmem_limit_bytes=BACKWARD_VMEM
         ),
-        name="reduce",
-    )(*grads, theirs, mine, made, norms)
+        name="backward",
+    )(*args)
+
+
+def output_place(unit, core):
+    row, column = share_corner(unit, core, 0)
+    return UNIT_WEIGHTS[unit], row, column
+
+
+def widen_kernel(sums, *refs):
+    outs, (taken, given, in_sem, out_sem) = refs[:10], refs[10:]
+    depth = taken.shape[0]
+    shares = [(unit, core) for unit in range(UNITS) for core in range(2)]
+
+    def fetch(i):
+        unit, core = shares[i]
+        return pltpu.make_async_copy(sums.at[unit, core], taken.at[i % depth], in_sem.at[i % depth])
+
+    def place(i):
+        weight, row, column = output_place(*shares[i])
+        return pltpu.make_async_copy(
+            given.at[i % depth],
+            outs[weight].at[pl.ds(row, TILE), pl.ds(column, TILE)],
+            out_sem.at[i % depth],
+        )
+
+    for i in range(depth - 1):
+        fetch(i).start()
+    for i in range(len(shares)):
+        if i + depth - 1 < len(shares):
+            fetch(i + depth - 1).start()
+        fetch(i).wait()
+        if i >= depth:
+            place(i - depth).wait()
+        given[i % depth] = taken[i % depth].astype(f32)
+        place(i).start()
+    for i in range(len(shares) - depth, len(shares)):
+        place(i).wait()
 
 
 def weight_outputs(sums):
-    narrow_ones = [sums[u].reshape(2 * TILE, TILE) for u in range(6)]
-    outs = [jnp.concatenate([sums[u, 0], sums[u, 1]], axis=1) for u in (6, 7)]
-    grow = jnp.concatenate([sums[u].reshape(2 * TILE, TILE) for u in range(8, 12)], axis=1)
-    shrink = jnp.concatenate(
-        [jnp.concatenate([sums[u, 0], sums[u, 1]], axis=1) for u in range(12, 16)], axis=0
-    )
-    ordered = narrow_ones[:3] + outs[:1] + narrow_ones[3:] + outs[1:] + [grow, shrink]
-    return tuple(piece.astype(f32) for piece in ordered)
+    shapes = [(2 * TILE, TILE)] * 3 + [(TILE, 2 * TILE)] + [(2 * TILE, TILE)] * 3
+    shapes += [(TILE, 2 * TILE), (2 * TILE, 4 * TILE), (4 * TILE, 2 * TILE)]
+    depth = 6
+    return (
+        tuple(pl.pallas_call(
+            widen_kernel,
+            out_shape=[jax.ShapeDtypeStruct(shape, f32) for shape in shapes],
+            in_specs=[pl.BlockSpec(memory_space=pl.ANY)],
+            out_specs=[pl.BlockSpec(memory_space=pl.ANY)] * 10,
+            scratch_shapes=[
+                pltpu.VMEM((depth, TILE, TILE), bf16),
+                pltpu.VMEM((depth, TILE, TILE), f32),
+                pltpu.SemaphoreType.DMA((depth,)),
+                pltpu.SemaphoreType.DMA((depth,)),
+            ],
+            compiler_params=pltpu.CompilerParams(vmem_limit_bytes=VMEM_LIMIT),
+            name="widen",
+        )(sums)),
+    )
 
 
 def by_kernels(narrow):
@@ -963,7 +1308,7 @@
     at = lax.axis_index("narrow").astype(jnp.int32)
     chunk = tok_rows // (2 * narrow)
 
-    def own(rows, size=chunk, at=at):
+    def own(rows, size=chunk):
         low = lax.dynamic_slice_in_dim(rows, at * size, size)
         high = lax.dynamic_slice_in_dim(rows, (2 * narrow - 1 - at) * size, size)
         return jnp.concatenate([low, high], axis=0)
@@ -1009,7 +1354,7 @@
     )
     first_low = first.astype(bf16)
     query_cross = project(first_low, cross_query).astype(bf16)
-    blend_cross, log_cross, key_cross, value_cross = cross_forward(
+    blend_cross, log_cross, key_cross, value_cross, picked_rows = cross_forward(
         picked, everything, cross_key, cross_value, query_cross
     )
     second, second_normal, second_inverse = norm_forward(
@@ -1037,62 +1382,38 @@
     grad_cross = grad_second_in.astype(bf16)
     cross_out_grad = grad_weight(blend_cross, grad_cross)
     grad_blend_cross = grad_input(grad_cross, cross_out).astype(bf16)
-    grad_query_cross, cross_key_grad, cross_value_grad = cross_backward(
-        picked,
-        everything,
-        key_cross,
-        value_cross,
-        query_cross,
-        log_cross,
-        blend_cross,
-        grad_blend_cross,
-    )
-    cross_query_grad = grad_weight(first_low, grad_query_cross)
-    grad_first = grad_second_in + grad_input(grad_query_cross, cross_query)
-    grad_first_in, first_gain_grad, first_shift_grad = norm_backward(
-        grad_first, first_normal, first_inverse, first_gain
-    )
-    grad_self = grad_first_in.astype(bf16)
-    self_out_grad = grad_weight(blend_self, grad_self)
-    grad_blend_self = grad_input(grad_self, self_out).astype(bf16)
-    grad_query_self, grad_key_self, grad_value_self = self_backward(
-        narrow, where_at, query_self, key_self, value_self, log_self, blend_self, grad_blend_self
-    )
-    self_query_grad = grad_weight(mine, grad_query_self)
-    self_key_grad = grad_weight(hidden, grad_key_self)
-    self_value_grad = grad_weight(hidden, grad_value_self)
-    grad_rows = grad_input(grad_key_self, self_key) + grad_input(grad_value_self, self_value)
-    grad_own = grad_first_in + grad_input(grad_query_self, self_query)
-    weight_grads = (
-        self_query_grad,
-        self_key_grad,
-        self_value_grad,
-        self_out_grad,
-        cross_query_grad,
-        cross_key_grad,
-        cross_value_grad,
-        cross_out_grad,
-        expand_grad,
-        reduce_grad,
-    )
-    norm_grads = (
-        first_gain_grad,
-        first_shift_grad,
-        second_gain_grad,
-        second_shift_grad,
-        third_gain_grad,
-        third_shift_grad,
-    )
-
     if by_kernels(narrow):
-        zero = jnp.zeros_like(first_gain_grad)
-        theirs = own(grad_rows, at=1 - at).astype(bf16)
-        sums, grad_mine, grad_theirs, made_theirs, norm_sums = reduce_by_kernel(
-            tuple(g.astype(bf16) for g in weight_grads),
-            theirs,
-            own(grad_rows) + grad_own,
+        zero = jnp.zeros_like(second_gain_grad)
+        norm_grads = (zero, zero, second_gain_grad, second_shift_grad, third_gain_grad)
+        sums, grad_mine, grad_theirs, made_theirs, norm_sums = backward_by_kernel(
+            expand_grad.astype(bf16),
+            reduce_grad.astype(bf16),
+            cross_out_grad.astype(bf16),
+            picked_rows,
+            key_cross,
+            value_cross,
+            query_cross,
+            blend_cross,
+            grad_blend_cross,
+            log_cross,
+            first_low,
+            cross_query,
+            grad_second_in,
+            first_normal,
+            first_inverse,
+            first_gain.reshape(1, width),
+            blend_self,
+            self_out,
+            query_self,
+            key_self,
+            value_self,
+            log_self,
+            hidden,
+            self_query,
+            self_key,
+            self_value,
             output,
-            jnp.stack(norm_grads + (zero, zero)),
+            jnp.stack(norm_grads + (third_shift_grad, zero, zero)),
         )
 
         def ordered(ours, others):
@@ -1109,23 +1430,76 @@
                 axis=0,
             )
 
-        output = ordered(output, made_theirs)
-        grad_hidden = ordered(grad_mine, grad_theirs.astype(f32))
-        weight_sums = weight_outputs(sums)
-    else:
-
-        def spread(rows):
-            empty = jnp.zeros((tok_rows, width), rows.dtype)
-            placed = lax.dynamic_update_slice_in_dim(empty, rows[:chunk], at * chunk, 0)
-            return lax.dynamic_update_slice_in_dim(
-                placed, rows[chunk:], (2 * narrow - 1 - at) * chunk, 0
-            )
-
-        grad_hidden = lax.psum((grad_rows + spread(grad_own)).astype(bf16), "narrow").astype(f32)
-        output = lax.psum(spread(output), "narrow")
-        weight_sums = reduce_all(weight_grads)
-        norm_sums = lax.psum(jnp.stack(norm_grads), ("wide", "narrow"))
-    return (output, grad_hidden) + weight_sums + tuple(norm_sums[i] for i in range(6))
+        return (
+            (ordered(output, made_theirs), ordered(grad_mine, grad_theirs.astype(f32)))
+            + weight_outputs(sums)[0]
+            + tuple(norm_sums[i] for i in range(6))
+        )
+
+    grad_query_cross, cross_key_grad, cross_value_grad = cross_backward(
+        picked,
+        everything,
+        key_cross,
+        value_cross,
+        query_cross,
+        log_cross,
+        blend_cross,
+        grad_blend_cross,
+    )
+    cross_query_grad = grad_weight(first_low, grad_query_cross)
+    grad_first = grad_second_in + grad_input(grad_query_cross, cross_query)
+    grad_first_in, first_gain_grad, first_shift_grad = norm_backward(
+        grad_first, first_normal, first_inverse, first_gain
+    )
+    grad_self = grad_first_in.astype(bf16)
+    self_out_grad = grad_weight(blend_self, grad_self)
+    grad_blend_self = grad_input(grad_self, self_out).astype(bf16)
+    grad_query_self, grad_key_self, grad_value_self = self_backward(
+        narrow, where_at, query_self, key_self, value_self, log_self, blend_self, grad_blend_self
+    )
+    self_query_grad = grad_weight(mine, grad_query_self)
+    self_key_grad = grad_weight(hidden, grad_key_self)
+    self_value_grad = grad_weight(hidden, grad_value_self)
+    grad_rows = grad_input(grad_key_self, self_key) + grad_input(grad_value_self, self_value)
+    grad_own = grad_first_in + grad_input(grad_query_self, self_query)
+
+    def spread(rows):
+        empty = jnp.zeros((tok_rows, width), rows.dtype)
+        placed = lax.dynamic_update_slice_in_dim(empty, rows[:chunk], at * chunk, 0)
+        return lax.dynamic_update_slice_in_dim(
+            placed, rows[chunk:], (2 * narrow - 1 - at) * chunk, 0
+        )
+
+    grad_hidden = lax.psum((grad_rows + spread(grad_own)).astype(bf16), "narrow").astype(f32)
+    output = lax.psum(spread(output), "narrow")
+    weight_grads = reduce_all(
+        (
+            self_query_grad,
+            self_key_grad,
+            self_value_grad,
+            self_out_grad,
+            cross_query_grad,
+            cross_key_grad,
+            cross_value_grad,
+            cross_out_grad,
+            expand_grad,
+            reduce_grad,
+        )
+    )
+    norm_grads = lax.psum(
+        jnp.stack(
+            [
+                first_gain_grad,
+                first_shift_grad,
+                second_gain_grad,
+                second_shift_grad,
+                third_gain_grad,
+                third_shift_grad,
+            ]
+        ),
+        ("wide", "narrow"),
+    )
+    return (output, grad_hidden) + weight_grads + tuple(norm_grads[i] for i in range(6))
 
 
 def solution(mesh):

time: 604 us -> 513 us (0.85)
  other arithmetic: 37.5 us -> 11.3 us
  Pallas kernels: 445 us -> 420 us
  local copies, waits for them, and re-layouts: 34.3 us -> 11.8 us
  matrix products: 79.8 us -> 63.9 us
    pallas_call x3 -> x2, Pallas kernels: 216 us -> 185 us  [the longest x1 174 us: backward_by_kernel(): pl.pallas_call(backward_kernel, out_shape=[jax.ShapeDtypeStruct((U, 2, T,...]
    convert_element_type x11 -> x2, other arithmetic: 26.1 us -> 1.7 us  [the longest x1 1.36 us: local(): grad_theirs.astype(f32)]
    unnamed x158 -> x88, local copies, waits for them, and re-layouts: 24.1 us -> 3.08 us
    dot_general x8 -> x3, matrix products: 24.7 us -> 11.8 us  [grad_weight(): return jnp.einsum('ti,to->io', left, right, preferred_element_type=f32)]
    dot_general x8 -> x3, matrix products: 24 us -> 13.4 us  [grad_input(): jnp.einsum('to,io->ti', grad_rows, weight, preferred_element_type=f32)]
    dot_general x8, matrix products: 31.1 us -> 38.7 us  [project(): return jnp.dot(rows_in, weight, preferred_element_type=f32)]
where the time goes in v2:
time: 513 us; the launch traced here: 509 us
  Pallas kernels  420 us (82%)
  matrix products  63.9 us (12%)
  local copies, waits for them, and re-layouts  11.8 us (2%)
  other arithmetic  11.3 us (2%)
    pallas_call x1, Pallas kernels, gather_by_kernel(): pl.pallas_call(functools.partial(gather_kernel, a_rows, b_rows), out_shap...  187 us
    pallas_call x1, Pallas kernels, backward_by_kernel(): pl.pallas_call(backward_kernel, out_shape=[jax.ShapeDtypeStruct((U, 2, T,...  174 us
    dot_general x8, matrix products, project(): return jnp.dot(rows_in, weight, preferred_element_type=f32)  38.7 us
    pallas_call x1, Pallas kernels, cross_forward(): pl.pallas_call(cross_forward_kernel, grid_spec=pltpu.PrefetchScalarGridSp...  33.2 us
    pallas_call x1, Pallas kernels, self_forward(): pl.pallas_call(functools.partial(self_forward_kernel, narrow), grid_spec=...  15.7 us
    dot_general x3, matrix products, grad_input(): jnp.einsum('to,io->ti', grad_rows, weight, preferred_element_type=f32)  13.4 us
    dot_general x3, matrix products, grad_weight(): return jnp.einsum('ti,to->io', left, right, preferred_element_type=f32)  11.8 us
    pallas_call x1, Pallas kernels, weight_outputs(): pl.pallas_call(widen_kernel, out_shape=[jax.ShapeDtypeStruct(shape, f32)...  10.6 us

profile of v2, /device:TPU:0, one launch (start us, length us, event | category | flops | bytes accessed | tf_op | source)
XLA Modules:
  0.0 508.5 jit_solution(1138855901107290066)
XLA Ops:
  0.7 2.3 constant_dynamic-slice_fusion.1
  3.0 186.5 %gather.1 = (bf16[24576,768]{1,0:T(8,128)(2,1)}, bf16[768,768]{1,0:T(8,128)(2,1)}, bf16[768,768]{1,0:T(8,128)(2,1)}, bf16[768,768]{1,0:T(8,128)(2,1)}, bf16[768,...) custom-call(bf16[1536,768]{1,0:T(8,128)(2,1)} %refs_0_.1, ...), custom_call_target="tpu_custom_call" | custom-call | tf_op jit(solution)/shard_map/gather/pallas_call | solution.py:642
  189.6 3.1 convolution_convert_fusion.7.q_ref.refs_18_
  192.7 2.5 fusion.23.k_ref.refs_19_
  195.2 2.6 fusion.24.v_ref.refs_20_
  197.8 15.7 %self_forward.1 = (bf16[512,768]{1,0:T(8,128)(2,1)}, f32[6,4,256]{2,1,0:T(4,128)}) custom-call(s32[1]{0:T(128)} %bitcast.at_ref, bf16[512,768]{1,0:T(8,128)(2,1)} %convolution_convert_fusion.7.q_ref.refs_18_, bf16[1024,768]{1,0:T(8,128)(2,1)} %fusion.23.k_ref.refs_19_, bf16[1024,768]{1,0:T(8,128)(2,1)} %fusion.24.v_ref.refs_20_), custom_call_target="tpu_custom_call" | custom-call | tf_op jit(solution)/shard_map/self_forward/pallas_call | solution.py:170
  213.5 2.0 fusion.37
  217.6 1.7 convolution_convert_fusion.6.refs_10_.refs_6_
  219.9 33.2 %cross_forward.1 = (bf16[512,768]{1,0:T(8,128)(2,1)}, f32[4,6,256]{2,1,0:T(8,128)}, bf16[4096,768]{1,0:T(8,128)(2,1)}, bf16[4096,768]{1,0:T(8,128)(2,1)}, bf16[4096,768]{1,0:T(8,128)(2,1)}) custom-call(s32[32]{0:T(128)} %reshape.115.picked_ref, bf16[24576,768]{1,0:T(8,128)(2,1)} %get-tuple-element.56.refs_0_.refs_1_.refs_2_.refs_3_.refs_4_.refs_5_.refs_6_.refs_7_, ...), custom_call_target="tpu_custom_call" | custom-call | tf_op jit(solution)/shard_map/cross_forward/pallas_call | solution.py:276
  253.1 2.4 fusion.38
  256.2 18.3 %fusion.2 = (bf16[512,3072]{1,0:T(8,128)(2,1)S(1)}, f32[512,3072]{1,0:T(8,128)S(1)}) fusion(bf16[768,3072]{1,0:T(8,128)(2,1)} %get-tuple-element.62, f32[512,768]{1,0:T(8,128)S(1)} %get-tuple-element.118, f32[768]{0:T(1024)S(1)} %copy-done.36, f32[768]{0:T(1024)S(1)} %copy-done.28, f32[512]{0:T(512)S(1)} %add_rsqrt_fusion.1, f32[512]{0:T(512)S(1)} %broadcast_multiply_fusion.5), kind=kOutput, calls=%fused_computation.4 | convolution fusion | flops 2520121344 | bytes 15738880 | tf_op jit(solution)/shard_map/dot_general | solution.py:49
  274.5 6.2 %fusion.39 = (f32[512]{0:T(512)S(1)}, f32[512,768]{1,0:T(8,128)S(1)}) fusion(bf16[512,3072]{1,0:T(8,128)(2,1)S(1)} %get-tuple-element.119, bf16[3072,768]{1,0:T(8,128)(2,1)} %get-tuple-element.63, f32[768]{0:T(1024)S(1)} %copy-done.36, f32[768]{0:T(1024)S(1)} %copy-done.28, f32[512]{0:T(512)S(1)} %add_rsqrt_fusion.1, ...), kind=kOutput, calls=%fused_computation.108 | convolution fusion | flops 2418277888 | bytes 11022336 | tf_op jit(solution)/shard_map/dot_general | solution.py:49
  281.8 1.8 fusion.22
  283.7 6.7 %fusion.8 = bf16[512,3072]{1,0:T(8,128)(2,1)S(1)} fusion(f32[512,3072]{1,0:T(8,128)S(1)} %get-tuple-element.120, bf16[3072,768]{1,0:T(8,128)(2,1)} %get-tuple-element.63, f32[512,768]{1,0:T(8,128)S(1)} %get-tuple-element.122, f32[512]{0:T(512)S(1)} %broadcast_multiply_fusion.2, f32[512]{0:T(512)S(1)} %broadcast_multiply_fusion.3, f32[768]{0:T(1024)S(1)} %copy-done.26, ...), kind=kOutput, calls=%fused_computation.10 | convolution fusion | flops 2436366336 | bytes 16526336 | tf_op jit(solution)/shard_map/to,io->ti/dot_general | solution.py:57
  290.5 5.0 multiply_reduce_fusion
  297.8 1.4 stack.19.refs_27_
  300.6 2.0 subtract_multiply_fusion.refs_12_
  302.6 1.7 convolution_convert_fusion.5.refs_8_
  304.3 1.8 convolution_convert_fusion.4.refs_2_
  306.2 5.2 %convolution_convert_fusion.refs_1_ = bf16[3072,768]{1,0:T(8,128)(2,1)} fusion(bf16[512,3072]{1,0:T(8,128)(2,1)S(1)} %copy-done.41, f32[512,768]{1,0:T(8,128)S(1)} %get-tuple-element.122, f32[512]{0:T(512)S(1)} %copy-done.31, f32[512]{0:T(512)S(1)} %copy-done.33, f32[768]{0:T(1024)S(1)} %copy-done.27, f32[512]{0:T(512)S(1)} %copy-done.23, ...), kind=kOutput, calls=%fused_computation.26 | convolution fusion | flops 2422996992 | bytes 10234880 | tf_op jit(solution)/shard_map/ti,to->io/dot_general | solution.py:53
  311.5 4.8 convolution_convert_fusion.1.refs_0_
  317.7 174.0 %backward.1 = (bf16[16,2,384,384]{3,2,1,0:T(8,128)(2,1)}, f32[512,768]{1,0:T(8,128)}, bf16[512,768]{1,0:T(8,128)(2,1)}, bf16[512,768]{1,0:T(8,128)(2,1)}, f32[8,768]{1,0:T(8,128)}) custom-call(bf16[768,3072]{1,0:T(8,128)(2,1)} %convolution_convert_fusion.1.refs_0_, bf16[3072,768]{1,0:T(8,128)(2,1)} %convolution_convert_fusion.refs_1_, ...), custom_call_target="tpu_custom_call" | custom-call | tf_op jit(solution)/shard_map/backward/pallas_call | solution.py:1159
  491.7 10.6 %widen.1 = (f32[768,384]{1,0:T(8,128)}, f32[768,384]{1,0:T(8,128)}, f32[768,384]{1,0:T(8,128)}, f32[384,768]{1,0:T(8,128)}, f32[768,384]{1,0:T(8,128)}, /*index=...) custom-call(bf16[16,2,384,384]{3,2,1,0:T(8,128)(2,1)} %get-tuple-element, ...), custom_call_target="tpu_custom_call" | custom-call | tf_op jit(solution)/shard_map/widen/pallas_call | solution.py:1242
  504.2 1.9 pad_maximum_fusion
  (118 shorter events, 13.7 us)
Async XLA Ops:
  189.5 3.1 copy-start.3
  189.6 3.1 copy-start.10
  192.7 2.5 copy-start.11
  197.8 15.7 %copy-start.12 = (bf16[768,768]{1,0:T(8,128)(2,1)S(1)}, bf16[768,768]{1,0:T(8,128)(2,1)}, u32[]{:S(2)}) copy-start(bf16[768,768]{1,0:T(8,128)(2,1)} %get-tuple-element.55.refs_17_) | copy-start | bytes 3538948
  216.8 36.4 %copy-start.2 = (f32[512,768]{1,0:T(8,128)}, f32[512,768]{1,0:T(8,128)S(1)}, u32[]{:S(2)}) copy-start(f32[512,768]{1,0:T(8,128)S(1)} %get-tuple-element.99.refs_13_) | copy-start | bytes 4718596
  255.9 34.6 %copy-start.20 = (f32[512]{0:T(512)}, f32[512]{0:T(512)S(1)}, u32[]{:S(2)}) copy-start(f32[512]{0:T(512)S(1)} %add_rsqrt_fusion.1) | copy-start | bytes 6148
  274.5 6.2 %copy-start.40 = (bf16[512,3072]{1,0:T(8,128)(2,1)}, bf16[512,3072]{1,0:T(8,128)(2,1)S(1)}, u32[]{:S(2)}) copy-start(bf16[512,3072]{1,0:T(8,128)(2,1)S(1)} %get-tuple-element.119) | copy-start | bytes 9437188
  281.1 9.4 %copy-start.22 = (f32[512]{0:T(512)}, f32[512]{0:T(512)S(1)}, u32[]{:S(2)}) copy-start(f32[512]{0:T(512)S(1)} %add_rsqrt_fusion) | copy-start | bytes 6148
  281.8 8.6 %slice-start = ((s8[4718592]{0:T(1024)(128)(4,1)}), s8[4194304]{0:T(1024)(128)(4,1)S(1)}, s32[]{:S(2)}) async-start(s8[4718592]{0:T(1024)(128)(4,1)} %bitcast.28), calls=%async_computation | async-start | bytes 8388608
  283.7 6.8 %copy-start.30 = (f32[512]{0:T(512)}, f32[512]{0:T(512)S(1)}, u32[]{:S(2)}) copy-start(f32[512]{0:T(512)S(1)} %broadcast_multiply_fusion.2) | copy-start | bytes 6148
  283.7 6.8 %copy-start.32 = (f32[512]{0:T(512)}, f32[512]{0:T(512)S(1)}, u32[]{:S(2)}) copy-start(f32[512]{0:T(512)S(1)} %broadcast_multiply_fusion.3) | copy-start | bytes 6148
  283.7 6.8 %slice-start.1 = ((s8[4718592]{0:T(1024)(128)(4,1)}), s8[524288]{0:T(1024)(128)(4,1)S(1)}, s32[]{:S(2)}) async-start(s8[4718592]{0:T(1024)(128)(4,1)} %bitcast.28), calls=%async_computation.1 | async-start | bytes 1048576
  290.5 5.0 copy-start.38
  300.6 2.0 copy-start.35
  302.6 3.6 copy-start.41
  304.3 1.9 copy-start.23
  306.2 5.2 %copy-start.21 = (f32[512]{0:T(512)S(1)}, f32[512]{0:T(512)}, u32[]{:S(2)}) copy-start(f32[512]{0:T(512)} %copy-done.20) | copy-start | bytes 6148
  306.2 5.2 %copy-start.29 = (f32[768]{0:T(1024)S(1)}, f32[768]{0:T(1024)}, u32[]{:S(2)}) copy-start(f32[768]{0:T(1024)} %param.35) | copy-start | bytes 9220
  306.2 5.2 %copy-start.37 = (f32[768]{0:T(1024)S(1)}, f32[768]{0:T(1024)}, u32[]{:S(2)}) copy-start(f32[768]{0:T(1024)} %param.36) | copy-start | bytes 9220
  306.2 5.2 %copy-start.39 = (bf16[512,3072]{1,0:T(8,128)(2,1)S(1)}, bf16[512,3072]{1,0:T(8,128)(2,1)}, u32[]{:S(2)}) copy-start(bf16[512,3072]{1,0:T(8,128)(2,1)} %copy-done.38) | copy-start | bytes 9437188
  311.4 4.8 copy-start.16
  311.5 5.7 %copy-start.18 = (f32[768]{0:T(1024)S(1)}, f32[768]{0:T(1024)}, u32[]{:S(2)}) copy-start(f32[768]{0:T(1024)} %param.33) | copy-start | bytes 9220
  504.1 1.9 copy-start.1
  504.2 1.9 copy-start.14
  (20 other events, 25.6 us)

commit v3 on v2

--- a/solution.py
+++ b/solution.py
@@ -387,6 +387,7 @@
 
 
 LINE = 4
+HELD = 5
 
 
 class Place:
@@ -412,22 +413,22 @@
         pl.semaphore_wait(barrier, len(targets))
 
 
-def gather_kernel(a_rows, b_rows, *refs):
+def forward_kernel(a_rows, b_rows, *refs):
     encoded_in, weights_in = refs[0], refs[1:11]
-    everything, full = refs[11], refs[12:22]
-    encoded, weights = refs[22], refs[23:33]
-    load_sem, own_sem, half_sem, flow_send, flow_recv, weight_send, weight_recv = refs[33:]
+    hidden_in, first_gain, first_shift = refs[11:14]
+    everything, full_out = refs[14], refs[15:25]
+    kept_out, (log_self, inverse_out) = refs[25:33], refs[33:35]
+    encoded, weights, kept = refs[35], refs[36:46], refs[46:54]
+    hidden = refs[54]
+    load_sem, own_sem, half_sem, kept_sem, flow_send, flow_recv, weight_send, weight_recv = refs[55:]
+    q_self, k_self, v_self, a_self, first, first_normal, first_low, q_cross = kept
+    full = weights[:HELD] + full_out[HELD:]
     me = Place()
     rows = encoded.shape[0]
     x, y, z, core = me.x, me.y, me.z, me.core
     low, high = z > 0, z < LINE - 1
     UP_A, DOWN_A, Y_A, UP_B, DOWN_B, Y_B, X_B, CORE_A, CORE_B = range(9)
 
-    loads = [pltpu.make_async_copy(encoded_in, encoded, load_sem.at[10])]
-    for i in range(10):
-        loads.append(pltpu.make_async_copy(weights_in[i], weights[i], load_sem.at[i]))
-    for load in loads:
-        load.start()
     own = pltpu.make_async_copy(
         encoded, everything.at[pl.ds(pl.multiple_of(me.wide * rows, 128), rows)], own_sem
     )
@@ -446,15 +447,24 @@
         first = pl.multiple_of(plane * count + part * (count // 2), 16)
         return ref.at[pl.ds(first, count // 2)]
 
-    halves = []
+    loads, halves = [], []
     for i in range(10):
-        halves.append(
-            pltpu.make_async_copy(weights[i], region(i, full[i], x, None), half_sem.at[i])
-        )
-
+        into = region(i, weights[i], x, None) if i < HELD else weights[i]
+        loads.append(pltpu.make_async_copy(weights_in[i], into, load_sem.at[i]))
+        if i < HELD:
+            halves.append(pltpu.make_async_copy(weights[i], full_out[i], half_sem.at[i]))
+        else:
+            halves.append(
+                pltpu.make_async_copy(weights[i], region(i, full[i], x, None), half_sem.at[i])
+            )
+    loads.append(pltpu.make_async_copy(encoded_in, encoded, load_sem.at[10]))
+    loads.append(pltpu.make_async_copy(hidden_in, hidden, load_sem.at[11]))
+    loads[10].start()
+    for i in range(10):
+        loads[i].start()
+    loads[11].start()
     me.greet()
-    for load in loads:
-        load.wait()
+    loads[10].wait()
 
     def flow(kind, owner_z, owner_y, plane, target, from_core=None, held=False):
         owner = owner_z * 2 + owner_y
@@ -512,7 +522,7 @@
 
     def weight(way, i, plane, part):
         piece = region(i, full[i], plane, part)
-        if way == 0:
+        if way == 0 and i >= HELD:
             piece_in = weights[i]
             count = piece_in.shape[0] // 2
             piece_in = piece_in.at[pl.ds(pl.multiple_of(part * count, 16), count)]
@@ -531,18 +541,71 @@
     y_a(z, y, True).start()
     pl.when(high)(lambda: up_a(z, True).start())
     pl.when(low)(lambda: down_a(z, True).start())
-    for i in range(10):
-        weight(0, i, x, core).start()
+
+    def weights_go(some):
+        for i in some:
+            weight(0, i, x, core).start()
+
+    def weights_come(some):
+        for i in some:
+            weight(0, i, 1 - x, core).wait_recv()
+            weight(1, i, 1 - x, core).start()
+
+    for i in range(3):
+        loads[i].wait()
+    weights_go(range(3))
     core_a(z, y, held=True).start()
     core_b(z, y, 0, held=True).start()
     core_b(z, y, 1, held=True).start()
     own.start()
-    for i in range(10):
+    for i in range(3, 12):
+        if i != 10:
+            loads[i].wait()
+    for i in range(HELD, 10):
         halves[i].start()
 
     y_b(1 - y).wait_recv()
     core_b(z, 1 - y, x).start()
-    x_b(z, 1 - y, x).start()
+    weights_come(range(3))
+    weights_go(range(3, 8))
+    for i in range(3):
+        weight(1, i, 1 - x, 1 - core).wait_recv()
+
+    total_rows = hidden.shape[0]
+    chunk = total_rows // 4
+    mine = (
+        pl.ds(pl.multiple_of(x * chunk, 128), chunk),
+        pl.ds(pl.multiple_of((3 - x) * chunk, 128), chunk),
+    )
+    places = (pl.ds(0, chunk), pl.ds(chunk, chunk))
+    for piece, place in zip(mine, places):
+        q_self[place] = dot_nn(hidden[piece], weights[0][...]).astype(bf16)
+    k_self[...] = dot_nn(hidden[...], weights[1][...]).astype(bf16)
+    v_self[...] = dot_nn(hidden[...], weights[2][...]).astype(bf16)
+    put = [pltpu.make_async_copy(kept[i], kept_out[i], kept_sem.at[i]) for i in range(8)]
+    for i in range(3):
+        put[i].start()
+
+    def self_step(g, carry):
+        lanes = pl.ds(pl.multiple_of(g * PAIR, PAIR), PAIR)
+        for local_row, seen, taken in self_blocks(2, total_rows, x):
+
+            @pl.when(taken)
+            def _():
+                some = pl.ds(local_row, BLOCK_ROWS)
+                blended, log_total = pair_forward(
+                    q_self[some, lanes],
+                    k_self[pl.ds(0, seen), lanes],
+                    v_self[pl.ds(0, seen), lanes],
+                    causal_edge(BLOCK_ROWS),
+                )
+                a_self[some, lanes] = blended
+                log_self[g, pl.ds(local_row // BLOCK_ROWS, 1)] = log_total
+
+        return carry
+
+    pairs = q_self.shape[1] // PAIR
+    lax.fori_loop(0, pairs // 2, self_step, 0)
 
     def beside_arrives(oz):
         y_a(oz, 1 - y).wait_recv()
@@ -561,22 +624,50 @@
             x_b(oz, oy, x).start()
             core_b(oz, oy, x).start()
 
-    for step in range(LINE):
-        for kind, back in ((0, 1), (1, 0)):
-            under, over = z - back - step, z + back + step
-            if kind == 0 and step < LINE - 1:
-                pl.when(under >= 0)(lambda: pass_a(under, up_a, high, up_a))
-                pl.when(over < LINE)(lambda: pass_a(over, down_a, low, down_a))
-            if kind == 1 and step == 0:
-                for oy, held in ((y, True), (1 - y, False)):
-                    pl.when(high)(lambda oy=oy, held=held: up_b(z, oy, held).start())
-                    pl.when(low)(lambda oy=oy, held=held: down_b(z, oy, held).start())
-            if kind == 1 and step > 0:
-                pl.when(under >= 0)(lambda: pass_b(under, up_b, high, up_b))
-                pl.when(over < LINE)(lambda: pass_b(over, down_b, low, down_b))
-    for i in range(10):
-        weight(0, i, 1 - x, core).wait_recv()
-        weight(1, i, 1 - x, core).start()
+    def step_a(step):
+        under, over = z - 1 - step, z + 1 + step
+        pl.when(under >= 0)(lambda: pass_a(under, up_a, high, up_a))
+        pl.when(over < LINE)(lambda: pass_a(over, down_a, low, down_a))
+
+    def step_b(step):
+        under, over = z - 1 - step, z + 1 + step
+        pl.when(under >= 0)(lambda: pass_b(under, up_b, high, up_b))
+        pl.when(over < LINE)(lambda: pass_b(over, down_b, low, down_b))
+
+    step_a(0)
+    for oy, held in ((y, True), (1 - y, False)):
+        pl.when(high)(lambda oy=oy, held=held: up_b(z, oy, held).start())
+        pl.when(low)(lambda oy=oy, held=held: down_b(z, oy, held).start())
+    weights_go(range(8, 10))
+    x_b(z, 1 - y, x).start()
+    lax.fori_loop(pairs // 2, pairs, self_step, 0)
+    put[3].start()
+    weights_come(range(3, 5))
+    for i in range(3, 5):
+        weight(1, i, 1 - x, 1 - core).wait_recv()
+    for i in range(HELD):
+        halves[i].start()
+
+    for piece, place in zip(mine, places):
+        summed = hidden[piece].astype(f32) + dot_nn(a_self[place], weights[3][...])
+        centred = summed - jnp.mean(summed, axis=-1, keepdims=True)
+        inverse = lax.rsqrt(jnp.mean(centred * centred, axis=-1, keepdims=True) + epsilon)
+        normal = centred * inverse
+        result = normal * first_gain[...] + first_shift[...]
+        first_normal[place] = normal
+        inverse_out[place] = inverse
+        first[place] = result
+        first_low[place] = result.astype(bf16)
+        q_cross[place] = dot_nn(result.astype(bf16), weights[4][...]).astype(bf16)
+    for i in range(4, 8):
+        put[i].start()
+
+    step_a(1)
+    step_b(0)
+    step_a(2)
+    step_b(1)
+    step_b(2)
+    weights_come(range(5, 10))
     beside_arrives(z)
     for step in range(1, LINE):
         pl.when(z - step >= 0)(lambda: beside_arrives(z - step))
@@ -627,10 +718,13 @@
         halves[i].wait()
         weight(0, i, x, core).wait_send()
         weight(1, i, 1 - x, core).wait_send()
-        weight(1, i, 1 - x, 1 - core).wait_recv()
-
-
-def gather_by_kernel(encoded, weights):
+        if i >= HELD:
+            weight(1, i, 1 - x, 1 - core).wait_recv()
+    for copy in put:
+        copy.wait()
+
+
+def forward_by_kernel(encoded, weights, hidden, first_gain, first_shift):
     rows, width = encoded.shape
     a_rows = rows * 17 // 24 // 16 * 16
     b_rows = (rows - a_rows) // 2
@@ -638,21 +732,35 @@
     for i, w in enumerate(weights):
         doubled = (w.shape[0], 2 * w.shape[1]) if i in COLUMNS else (2 * w.shape[0], w.shape[1])
         shapes.append(jax.ShapeDtypeStruct(doubled, bf16))
+    total_rows = hidden.shape[0]
+    mine, pairs = total_rows // 2, width // PAIR
+    kept = [(mine, bf16), (total_rows, bf16), (total_rows, bf16), (mine, bf16)]
+    kept += [(mine, f32), (mine, f32), (mine, bf16), (mine, bf16)]
+    held = [s.shape if i < HELD else w.shape for i, (s, w) in enumerate(zip(shapes[1:], weights))]
+    small = [
+        jax.ShapeDtypeStruct((pairs, mine // BLOCK_ROWS, 2 * BLOCK_ROWS), f32),
+        jax.ShapeDtypeStruct((mine, 1), f32),
+    ]
     dma = pltpu.SemaphoreType.DMA
+    anywhere = pl.BlockSpec(memory_space=pl.ANY)
+    vmem = pl.BlockSpec(memory_space=pltpu.VMEM)
     out = pl.pallas_call(
-        functools.partial(gather_kernel, a_rows, b_rows),
-        out_shape=shapes,
-        in_specs=[pl.BlockSpec(memory_space=pl.ANY)] * 11,
-        out_specs=[pl.BlockSpec(memory_space=pl.ANY)] * 11,
+        functools.partial(forward_kernel, a_rows, b_rows),
+        out_shape=shapes + [jax.ShapeDtypeStruct((n, width), dtype) for n, dtype in kept] + small,
+        in_specs=[anywhere] * 12 + [vmem] * 2,
+        out_specs=[anywhere] * 19 + [vmem] * 2,
         scratch_shapes=[pltpu.VMEM((rows, width), bf16)]
-        + [pltpu.VMEM(w.shape, bf16) for w in weights]
-        + [dma((11,)), dma, dma((10,)), dma((9, 16)), dma((9, 16)), dma((2, 10)), dma((2, 10))],
+        + [pltpu.VMEM(shape, bf16) for shape in held]
+        + [pltpu.VMEM((n, width), dtype) for n, dtype in kept]
+        + [pltpu.VMEM((total_rows, width), bf16)]
+        + [dma((12,)), dma, dma((10,)), dma((8,))]
+        + [dma((9, 16)), dma((9, 16)), dma((2, 10)), dma((2, 10))],
         compiler_params=pltpu.CompilerParams(
             collective_id=0, has_side_effects=True, vmem_limit_bytes=VMEM_LIMIT
         ),
-        name="gather",
-    )(encoded, *weights)
-    return out[0], tuple(out[1:])
+        name="forward",
+    )(encoded, *weights, hidden, first_gain.reshape(1, width), first_shift.reshape(1, width))
+    return out[0], tuple(out[1:11]), tuple(out[11:])
 
 
 TILE = 384
@@ -1256,13 +1364,140 @@
     )
 
 
+FF_COLUMNS = 512
+
+
+def layer_norm(summed, norm_gain, norm_shift):
+    centred = summed - jnp.mean(summed, axis=-1, keepdims=True)
+    inverse = lax.rsqrt(jnp.mean(centred * centred, axis=-1, keepdims=True) + epsilon)
+    normal = centred * inverse
+    return normal * norm_gain + norm_shift, normal, inverse
+
+
+def dense_kernel(
+    a_cross, first, cotangent, cross_out, gain_two, shift_two, gain_three, shift_three, expand_in, reduce_in,
+    out_ref, g_second, g_across, cross_out_grad, norms, expand_grad, reduce_grad,
+    expand, reduce, activated, slope, expand_staged, reduce_staged,
+    expand_sem, reduce_sem, expand_out_sem, reduce_out_sem,
+):
+    count = expand.shape[1] // FF_COLUMNS
+
+    def piece(c):
+        return pl.ds(c * FF_COLUMNS, FF_COLUMNS)
+
+    def fetch_expand(c):
+        return pltpu.make_async_copy(
+            expand_in.at[:, piece(c)], expand.at[:, piece(c)], expand_sem.at[c]
+        )
+
+    def fetch_reduce(c):
+        return pltpu.make_async_copy(reduce_in.at[piece(c)], reduce.at[piece(c)], reduce_sem.at[c])
+
+    def put_expand(c):
+        return pltpu.make_async_copy(
+            expand_staged.at[c % 2], expand_grad.at[:, piece(c)], expand_out_sem.at[c % 2]
+        )
+
+    def put_reduce(c):
+        return pltpu.make_async_copy(
+            reduce_staged.at[c % 2], reduce_grad.at[piece(c)], reduce_out_sem.at[c % 2]
+        )
+
+    for c in range(count):
+        fetch_expand(c).start()
+        fetch_reduce(c).start()
+    second, normal_two, inverse_two = layer_norm(
+        first[...] + dot_nn(a_cross[...], cross_out[...]), gain_two[...], shift_two[...]
+    )
+    second_low = second.astype(bf16)
+    total = second
+    for c in range(count):
+        fetch_expand(c).wait()
+        pre = dot_nn(second_low, expand[:, piece(c)])
+        phi = 0.5 * (1.0 + lax.erf(pre * 0.7071067811865476))
+        slope[:, piece(c)] = phi + pre * jnp.exp(-0.5 * pre * pre) * 0.3989422804014327
+        activated[:, piece(c)] = (pre * phi).astype(bf16)
+        fetch_reduce(c).wait()
+        total = total + dot_nn(activated[:, piece(c)], reduce[piece(c)])
+    final, normal, inverse = layer_norm(total, gain_three[...], shift_three[...])
+    out_ref[...] = final.astype(bf16)
+    grad = cotangent[...].astype(f32)
+    norms[...] = jnp.zeros_like(norms)
+
+    def back(grad, normal, inverse, gain, row):
+        norms[pl.ds(row, 1)] = jnp.sum(grad * normal, axis=0, keepdims=True)
+        norms[pl.ds(row + 1, 1)] = jnp.sum(grad, axis=0, keepdims=True)
+        scaled = grad * gain
+        return inverse * (
+            scaled
+            - jnp.mean(scaled, axis=-1, keepdims=True)
+            - normal * jnp.mean(scaled * normal, axis=-1, keepdims=True)
+        )
+
+    grad = back(grad, normal, inverse, gain_three[...], 4)
+    grad_low = grad.astype(bf16)
+    for c in range(count):
+        if c >= 2:
+            put_reduce(c - 2).wait()
+            put_expand(c - 2).wait()
+        reduce_staged[c % 2] = dot_tn(activated[:, piece(c)], grad_low).astype(bf16)
+        put_reduce(c).start()
+        grad_pre = (dot_nt(grad_low, reduce[piece(c)]) * slope[:, piece(c)]).astype(bf16)
+        expand_staged[c % 2] = dot_tn(second_low, grad_pre).astype(bf16)
+        put_expand(c).start()
+        grad = grad + dot_nt(grad_pre, expand[:, piece(c)])
+    grad = back(grad, normal_two, inverse_two, gain_two[...], 2)
+    g_second[...] = grad
+    grad_low = grad.astype(bf16)
+    cross_out_grad[...] = dot_tn(a_cross[...], grad_low).astype(bf16)
+    g_across[...] = dot_nt(grad_low, cross_out[...]).astype(bf16)
+    for c in range(count - 2, count):
+        put_reduce(c).wait()
+        put_expand(c).wait()
+
+
+def dense_by_kernel(a_cross, first, cotangent, cross_out, norm_params, expand, reduce):
+    rows, width = first.shape
+    hidden_units = expand.shape[1]
+    count = hidden_units // FF_COLUMNS
+    anywhere = pl.BlockSpec(memory_space=pl.ANY)
+    vmem = pl.BlockSpec(memory_space=pltpu.VMEM)
+    dma = pltpu.SemaphoreType.DMA
+    return pl.pallas_call(
+        dense_kernel,
+        out_shape=[
+            jax.ShapeDtypeStruct((rows, width), bf16),
+            jax.ShapeDtypeStruct((rows, width), f32),
+            jax.ShapeDtypeStruct((rows, width), bf16),
+            jax.ShapeDtypeStruct((width, width), bf16),
+            jax.ShapeDtypeStruct((8, width), f32),
+            jax.ShapeDtypeStruct(expand.shape, bf16),
+            jax.ShapeDtypeStruct(reduce.shape, bf16),
+        ],
+        in_specs=[vmem] * 8 + [anywhere] * 2,
+        out_specs=[vmem] * 5 + [anywhere] * 2,
+        scratch_shapes=[
+            pltpu.VMEM(expand.shape, bf16),
+            pltpu.VMEM(reduce.shape, bf16),
+            pltpu.VMEM((rows, hidden_units), bf16),
+            pltpu.VMEM((rows, hidden_units), f32),
+            pltpu.VMEM((2, width, FF_COLUMNS), bf16),
+            pltpu.VMEM((2, FF_COLUMNS, width), bf16),
+            dma((count,)),
+            dma((count,)),
+            dma((2,)),
+            dma((2,)),
+        ],
+        compiler_params=pltpu.CompilerParams(vmem_limit_bytes=VMEM_LIMIT),
+        name="dense",
+    )(a_cross, first, cotangent, cross_out, *[p.reshape(1, width) for p in norm_params], expand, reduce)
+
+
 def by_kernels(narrow):
     return lax.axis_size("wide") == 4 * LINE and narrow == 2
 
 
 def gather_all(encoded, weights):
-    if by_kernels(lax.axis_size("narrow")):
-        return gather_by_kernel(encoded, weights)
     everything = lax.all_gather(encoded, "wide", tiled=True)
     full = tuple(
         lax.all_gather(w, "narrow", axis=1 if i in COLUMNS else 0, tiled=True)
@@ -1313,82 +1548,49 @@
         high = lax.dynamic_slice_in_dim(rows, (2 * narrow - 1 - at) * size, size)
         return jnp.concatenate([low, high], axis=0)
 
-    everything, full = gather_all(
-        encoded,
-        (
-            self_query,
-            self_key,
-            self_value,
-            self_out,
-            cross_query,
-            cross_key,
-            cross_value,
-            cross_out,
-            expand_weight,
-            reduce_weight,
-        ),
-    )
-    (
-        self_query,
-        self_key,
-        self_value,
-        self_out,
-        cross_query,
-        cross_key,
-        cross_value,
-        cross_out,
-        expand_weight,
-        reduce_weight,
-    ) = full
     where_at = at.reshape(1)
     picked = own(retrieved, chunk // BLOCK_ROWS).reshape(-1)
-    mine = own(hidden)
-    grad_final = own(cotangent).astype(f32)
-
-    query_self = project(mine, self_query).astype(bf16)
-    key_self = project(hidden, self_key).astype(bf16)
-    value_self = project(hidden, self_value).astype(bf16)
-    blend_self, log_self = self_forward(narrow, where_at, query_self, key_self, value_self)
-    first, first_normal, first_inverse = norm_forward(
-        mine.astype(f32) + project(blend_self, self_out), first_gain, first_shift
-    )
-    first_low = first.astype(bf16)
-    query_cross = project(first_low, cross_query).astype(bf16)
-    blend_cross, log_cross, key_cross, value_cross, picked_rows = cross_forward(
-        picked, everything, cross_key, cross_value, query_cross
-    )
-    second, second_normal, second_inverse = norm_forward(
-        first + project(blend_cross, cross_out), second_gain, second_shift
-    )
-    second_low = second.astype(bf16)
-    pre_act = project(second_low, expand_weight)
-    activated = jax.nn.gelu(pre_act, approximate=False).astype(bf16)
-    final, third_normal, third_inverse = norm_forward(
-        second + project(activated, reduce_weight), third_gain, third_shift
-    )
-    output = final.astype(bf16)
-
-    grad_third, third_gain_grad, third_shift_grad = norm_backward(
-        grad_final, third_normal, third_inverse, third_gain
-    )
-    grad_ffn = grad_third.astype(bf16)
-    reduce_grad = grad_weight(activated, grad_ffn)
-    grad_pre = (grad_input(grad_ffn, reduce_weight) * gelu_slope(pre_act)).astype(bf16)
-    expand_grad = grad_weight(second_low, grad_pre)
-    grad_second = grad_third + grad_input(grad_pre, expand_weight)
-    grad_second_in, second_gain_grad, second_shift_grad = norm_backward(
-        grad_second, second_normal, second_inverse, second_gain
-    )
-    grad_cross = grad_second_in.astype(bf16)
-    cross_out_grad = grad_weight(blend_cross, grad_cross)
-    grad_blend_cross = grad_input(grad_cross, cross_out).astype(bf16)
     if by_kernels(narrow):
-        zero = jnp.zeros_like(second_gain_grad)
-        norm_grads = (zero, zero, second_gain_grad, second_shift_grad, third_gain_grad)
+        everything, full, kept = forward_by_kernel(
+            encoded,
+            (
+                self_query,
+                self_key,
+                self_value,
+                self_out,
+                cross_query,
+                cross_key,
+                cross_value,
+                cross_out,
+                expand_weight,
+                reduce_weight,
+            ),
+            hidden,
+            first_gain,
+            first_shift,
+        )
+        query_self, key_self, value_self, blend_self, first, first_normal, first_low = kept[:7]
+        query_cross, log_self, first_inverse = kept[7:]
+        (self_query, self_key, self_value, self_out, cross_query, cross_key, cross_value) = full[:7]
+        (cross_out, expand_weight, reduce_weight) = full[7:]
+        blend_cross, log_cross, key_cross, value_cross, picked_rows = cross_forward(
+            picked, everything, cross_key, cross_value, query_cross
+        )
+        output, grad_second_in, grad_blend_cross, cross_out_grad, norms, expand_grad, reduce_grad = (
+            dense_by_kernel(
+                blend_cross,
+                first,
+                own(cotangent),
+                cross_out,
+                (second_gain, second_shift, third_gain, third_shift),
+                expand_weight,
+                reduce_weight,
+            )
+        )
         sums, grad_mine, grad_theirs, made_theirs, norm_sums = backward_by_kernel(
-            expand_grad.astype(bf16),
-            reduce_grad.astype(bf16),
-            cross_out_grad.astype(bf16),
+            expand_grad,
+            reduce_grad,
+            cross_out_grad,
             picked_rows,
             key_cross,
             value_cross,
@@ -1413,7 +1615,7 @@
             self_key,
             self_value,
             output,
-            jnp.stack(norm_grads + (third_shift_grad, zero, zero)),
+            norms,
         )
 
         def ordered(ours, others):
@@ -1436,6 +1638,73 @@
             + tuple(norm_sums[i] for i in range(6))
         )
 
+    everything, full = gather_all(
+        encoded,
+        (
+            self_query,
+            self_key,
+            self_value,
+            self_out,
+            cross_query,
+            cross_key,
+            cross_value,
+            cross_out,
+            expand_weight,
+            reduce_weight,
+        ),
+    )
+    (
+        self_query,
+        self_key,
+        self_value,
+        self_out,
+        cross_query,
+        cross_key,
+        cross_value,
+        cross_out,
+        expand_weight,
+        reduce_weight,
+    ) = full
+    mine = own(hidden)
+    grad_final = own(cotangent).astype(f32)
+
+    query_self = project(mine, self_query).astype(bf16)
+    key_self = project(hidden, self_key).astype(bf16)
+    value_self = project(hidden, self_value).astype(bf16)
+    blend_self, log_self = self_forward(narrow, where_at, query_self, key_self, value_self)
+    first, first_normal, first_inverse = norm_forward(
+        mine.astype(f32) + project(blend_self, self_out), first_gain, first_shift
+    )
+    first_low = first.astype(bf16)
+    query_cross = project(first_low, cross_query).astype(bf16)
+    blend_cross, log_cross, key_cross, value_cross, picked_rows = cross_forward(
+        picked, everything, cross_key, cross_value, query_cross
+    )
+    second, second_normal, second_inverse = norm_forward(
+        first + project(blend_cross, cross_out), second_gain, second_shift
+    )
+    second_low = second.astype(bf16)
+    pre_act = project(second_low, expand_weight)
+    activated = jax.nn.gelu(pre_act, approximate=False).astype(bf16)
+    final, third_normal, third_inverse = norm_forward(
+        second + project(activated, reduce_weight), third_gain, third_shift
+    )
+    output = final.astype(bf16)
+
+    grad_third, third_gain_grad, third_shift_grad = norm_backward(
+        grad_final, third_normal, third_inverse, third_gain
+    )
+    grad_ffn = grad_third.astype(bf16)
+    reduce_grad = grad_weight(activated, grad_ffn)
+    grad_pre = (grad_input(grad_ffn, reduce_weight) * gelu_slope(pre_act)).astype(bf16)
+    expand_grad = grad_weight(second_low, grad_pre)
+    grad_second = grad_third + grad_input(grad_pre, expand_weight)
+    grad_second_in, second_gain_grad, second_shift_grad = norm_backward(
+        grad_second, second_normal, second_inverse, second_gain
+    )
+    grad_cross = grad_second_in.astype(bf16)
+    cross_out_grad = grad_weight(blend_cross, grad_cross)
+    grad_blend_cross = grad_input(grad_cross, cross_out).astype(bf16)
     grad_query_cross, cross_key_grad, cross_value_grad = cross_backward(
         picked,
         everything,

time: 513 us -> 454 us (0.88)
  matrix products: 63.9 us -> 0 us
  Pallas kernels: 420 us -> 431 us
  other arithmetic: 11.3 us -> 5.76 us
    dot_general x14 -> x0, matrix products: 63.9 us -> none  [the longest x8 38.7 us: project(): return jnp.dot(rows_in, weight, preferred_element_type=f32)]
    pallas_call x2, Pallas kernels: 202 us -> 213 us  [the longest x1 183 us: forward_by_kernel(): pl.pallas_call(functools.partial(forward_kernel, a_rows, b_rows), out_sha...]
where the time goes in v3:
time: 454 us; the launch traced here: 446 us
  Pallas kernels  431 us (95%)
  local copies, waits for them, and re-layouts  7.28 us (2%)
  other arithmetic  5.76 us (1%)
    pallas_call x1, Pallas kernels, forward_by_kernel(): pl.pallas_call(functools.partial(forward_kernel, a_rows, b_rows), out_sha...  183 us
    pallas_call x1, Pallas kernels, backward_by_kernel(): pl.pallas_call(backward_kernel, out_shape=[jax.ShapeDtypeStruct((U, 2, T,...  174 us
    pallas_call x1, Pallas kernels, cross_forward(): pl.pallas_call(cross_forward_kernel, grid_spec=pltpu.PrefetchScalarGridSp...  33.5 us
    pallas_call x1, Pallas kernels, dense_by_kernel(): pl.pallas_call(dense_kernel, out_shape=[jax.ShapeDtypeStruct((rows, width...  29.8 us
    pallas_call x1, Pallas kernels, weight_outputs(): pl.pallas_call(widen_kernel, out_shape=[jax.ShapeDtypeStruct(shape, f32)...  10.6 us

profile of v3, /device:TPU:0, one launch (start us, length us, event | category | flops | bytes accessed | tf_op | source)
XLA Modules:
  0.0 445.6 jit_solution(12775673297888390134)
XLA Ops:
  0.7 0.8 constant_dynamic-slice_fusion.3
  1.4 0.6 reshape.58.picked_ref
  2.0 1.3 reshape.59.refs_12_.refs_15_
  3.3 1.3 reshape.60.refs_13_
  4.6 183.4 %forward.1 = (bf16[24576,768]{1,0:T(8,128)(2,1)}, bf16[768,768]{1,0:T(8,128)(2,1)}, bf16[768,768]{1,0:T(8,128)(2,1)}, bf16[768,768]{1,0:T(8,128)(2,1)}, bf16[768...) custom-call(bf16[1536,768]{1,0:T(8,128)(2,1)} %refs_0_.1, ...), custom_call_target="tpu_custom_call" | custom-call | tf_op jit(solution)/shard_map/forward/pallas_call | solution.py:747
  188.0 33.5 %cross_forward.1 = (bf16[512,768]{1,0:T(8,128)(2,1)}, f32[4,6,256]{2,1,0:T(8,128)}, bf16[4096,768]{1,0:T(8,128)(2,1)}, bf16[4096,768]{1,0:T(8,128)(2,1)}, bf16[4096,768]{1,0:T(8,128)(2,1)}) custom-call(s32[32]{0:T(128)} %reshape.58.picked_ref, bf16[24576,768]{1,0:T(8,128)(2,1)} %get-tuple-element.66.refs_0_.refs_1_.refs_2_.refs_3_.refs_4_.refs_5_.refs_6_.refs_7_, ...), custom_call_target="tpu_custom_call" | custom-call | tf_op jit(solution)/shard_map/cross_forward/pallas_call | solution.py:276
  221.5 0.0 copy-start.6
  221.5 0.1 constant_dynamic-slice_fusion.1
  221.6 0.9 pad_maximum_fusion.2.cotangent
  222.5 0.6 reshape.61.gain_two
  223.1 0.6 reshape.62.shift_two
  223.7 0.6 reshape.63.gain_three
  224.3 0.6 reshape.64.shift_three
  224.9 29.8 %dense.1 = (bf16[512,768]{1,0:T(8,128)(2,1)}, f32[512,768]{1,0:T(8,128)}, bf16[512,768]{1,0:T(8,128)(2,1)}, bf16[768,768]{1,0:T(8,128)(2,1)}, f32[8,768]{1,0:T(8...) custom-call(bf16[512,768]{1,0:T(8,128)(2,1)} %get-tuple-element.70.a_cross.refs_7_, ...), custom_call_target="tpu_custom_call" | custom-call | tf_op jit(solution)/shard_map/dense/pallas_call | solution.py:1466
  254.7 174.1 %backward.1 = (bf16[16,2,384,384]{3,2,1,0:T(8,128)(2,1)}, f32[512,768]{1,0:T(8,128)}, bf16[512,768]{1,0:T(8,128)(2,1)}, bf16[512,768]{1,0:T(8,128)(2,1)}, f32[8,768]{1,0:T(8,128)}) custom-call(bf16[768,3072]{1,0:T(8,128)(2,1)} %get-tuple-element.76.refs_0_, bf16[3072,768]{1,0:T(8,128)(2,1)} %get-tuple-element.77.refs_1_, ...), custom_call_target="tpu_custom_call" | custom-call | tf_op jit(solution)/shard_map/backward/pallas_call | solution.py:1267
  428.8 10.6 %widen.1 = (f32[768,384]{1,0:T(8,128)}, f32[768,384]{1,0:T(8,128)}, f32[768,384]{1,0:T(8,128)}, f32[384,768]{1,0:T(8,128)}, f32[768,384]{1,0:T(8,128)}, /*index=...) custom-call(bf16[16,2,384,384]{3,2,1,0:T(8,128)(2,1)} %get-tuple-element, ...), custom_call_target="tpu_custom_call" | custom-call | tf_op jit(solution)/shard_map/widen/pallas_call | solution.py:1350
  439.4 1.4 convert_element_type.3
  440.7 0.3 copy-done.1
  441.0 0.2 slice_select_fusion.3
  441.3 1.9 pad_maximum_fusion
  443.1 0.0 copy-done.2
  443.2 0.1 broadcast_select_fusion.3
  443.3 1.2 pad_maximum_fusion.1
  444.5 0.6 slice_reduce_fusion
  (16 shorter events, 0.1 us)
Async XLA Ops:
  188.0 33.5 %copy-start.3 = (bf16[1024,768]{1,0:T(8,128)(2,1)S(1)}, bf16[1024,768]{1,0:T(8,128)(2,1)}, u32[]{:S(2)}) copy-start(bf16[1024,768]{1,0:T(8,128)(2,1)} %param.39) | copy-start | bytes 4718596
  221.5 1.0 copy-start.5
  221.5 1.6 copy-start.6
  221.5 2.2 copy-start.7
  221.5 2.8 copy-start.8
  439.3 1.6 copy-start.1
  441.2 1.9 copy-start
  441.2 1.9 copy-start.2
  443.3 1.3 copy-start.4

commit v4 on v3

--- a/solution.py
+++ b/solution.py
@@ -390,6 +390,10 @@
 HELD = 5
 
 
+def as_row(ref):
+    return ref[...].reshape(1, ref.shape[0])
+
+
 class Place:
     def __init__(self):
         wide = lax.axis_index("wide")
@@ -653,7 +657,7 @@
         centred = summed - jnp.mean(summed, axis=-1, keepdims=True)
         inverse = lax.rsqrt(jnp.mean(centred * centred, axis=-1, keepdims=True) + epsilon)
         normal = centred * inverse
-        result = normal * first_gain[...] + first_shift[...]
+        result = normal * as_row(first_gain) + as_row(first_shift)
         first_normal[place] = normal
         inverse_out[place] = inverse
         first[place] = result
@@ -759,7 +763,7 @@
             collective_id=0, has_side_effects=True, vmem_limit_bytes=VMEM_LIMIT
         ),
         name="forward",
-    )(encoded, *weights, hidden, first_gain.reshape(1, width), first_shift.reshape(1, width))
+    )(encoded, *weights, hidden, first_gain, first_shift)
     return out[0], tuple(out[1:11]), tuple(out[11:])
 
 
@@ -767,9 +771,9 @@
 HALF = TILE // 2
 PART = HALF // LINE
 UNITS = 16
-SLOTS = 8
+SLOTS = 12
 UNIT_WEIGHTS = (8, 8, 8, 8, 9, 9, 9, 9, 7, 5, 6, 4, 3, 0, 1, 2)
-LAST_TICK = UNITS + 6
+LAST_TICK = UNITS + 11
 
 
 def share_corner(unit, core, plane):
@@ -787,16 +791,16 @@
         expand_grad, reduce_grad, cross_out_grad, picked_rows, keys_in, values_in, q_cross, a_cross,
         g_cross, log_cross, first_low, cross_query, g_second, first_normal, first_inverse, first_gain,
         a_self, self_out, q_self, k_self, v_self, log_self, hidden, self_query, self_key, self_value,
-        made, norms,
-    ) = refs[:28]
-    sums_out, mine_out, theirs_out, made_out, norms_out = refs[28:33]
+        norms,
+    ) = refs[:27]
+    sums_out, mine_out, theirs_out, norms_out = refs[27:31]
     (
         own, from_core, from_a, from_b, from_z, summed, pool, pool32, both, staged, dq_cross, dk_sum,
         dv_sum, theirs, rows_in, rows_got, norm_all, norm_in,
         own_sem, core_send, core_recv, a_send, a_recv, b_send, b_recv, z_send, z_recv, gz_send, gz_recv,
         gy_send, gy_recv, gc_send, gc_recv, keep_sem, load_sem, kv_sem, e_sem, extra_send, extra_recv,
         norm_send, norm_recv,
-    ) = refs[33:]
+    ) = refs[31:]
     me = Place()
     x, y, z, core = me.x, me.y, me.z, me.core
     sibling, beside, across = me.at(core=1 - core), me.at(y=1 - y), me.at(x=1 - x)
@@ -954,8 +958,8 @@
         gather_core(u, core).wait_send()
 
     stages = (
-        (0, stage_core), (2, stage_a), (3, stage_b), (4, stage_z), (5, stage_gather_z),
-        (6, stage_gather_y), (7, stage_gather_core),
+        (0, stage_core), (2, stage_a), (4, stage_b), (6, stage_z), (8, stage_gather_z),
+        (10, stage_gather_y), (12, stage_gather_core),
     )
 
     def tick(t):
@@ -1002,8 +1006,6 @@
     for ref, unit in ready + [(cross_out_grad, 8)]:
         for plane, part in corners:
             to_core(ref, unit, plane, part).start()
-    made_copy = remote(made, made_out, extra_send.at[1], extra_recv.at[1], across)
-    made_copy.start()
     both_sums = pool32
     both_sums[...] = jnp.zeros_like(both_sums)
     for copy in early[:3]:
@@ -1099,7 +1101,7 @@
     n_copy.wait()
     normal = pool32[pl.ds(rows, rows)]
     grad_out = pool32[pl.ds(0, rows)] + dot_nt(dq_cross[...], pool[pl.ds(CROSS_Q, width)])
-    scaled = grad_out * first_gain[...]
+    scaled = grad_out * as_row(first_gain)
     grad_in = first_inverse[...] * (
         scaled
         - jnp.mean(scaled, axis=-1, keepdims=True)
@@ -1219,7 +1221,7 @@
     theirs[pl.ds(0, chunk)] = row_grads(1 - x).astype(bf16)
     theirs[pl.ds(chunk, chunk)] = row_grads(2 + x).astype(bf16)
     rows_copy = remote(theirs, rows_in, extra_send.at[0], extra_recv.at[0], across)
-    got_copy = remote(rows_got, theirs_out, extra_send.at[2], extra_recv.at[2], across)
+    got_copy = remote(rows_got, theirs_out, extra_send.at[1], extra_recv.at[1], across)
     rows_copy.start()
     tick(14)
     for k, at_chunk in enumerate((x, 3 - x)):
@@ -1247,7 +1249,6 @@
 
     lax.fori_loop(15, LAST_TICK + 1, last_step, 0)
     got_copy.wait()
-    made_copy.wait()
     for ref, unit in ready + [(cross_out_grad, 8)]:
         for plane, part in corners:
             to_core(ref, unit, plane, part).wait_send()
@@ -1256,11 +1257,11 @@
 def backward_by_kernel(*args):
     rows, width = args[6].shape
     all_rows = args[22].shape[0]
-    norms = args[27]
+    norms = args[26]
     anywhere = pl.BlockSpec(memory_space=pl.ANY)
     vmem = pl.BlockSpec(memory_space=pltpu.VMEM)
-    in_specs = [anywhere] * 28
-    for i in (9, 14, 15, 21, 27):
+    in_specs = [anywhere] * 27
+    for i in (9, 14, 15, 21, 26):
         in_specs[i] = vmem
     dma = pltpu.SemaphoreType.DMA
     U, T, H, Z = UNITS, TILE, HALF, LINE - 1
@@ -1270,11 +1271,10 @@
             jax.ShapeDtypeStruct((U, 2, T, T), bf16),
             jax.ShapeDtypeStruct((rows, width), f32),
             jax.ShapeDtypeStruct((rows, width), bf16),
-            jax.ShapeDtypeStruct((rows, width), bf16),
             jax.ShapeDtypeStruct(norms.shape, f32),
         ],
         in_specs=in_specs,
-        out_specs=[anywhere, vmem, anywhere, anywhere, vmem],
+        out_specs=[anywhere, vmem, anywhere, vmem],
         scratch_shapes=[
             pltpu.VMEM((SLOTS, 2, 2, H, T), bf16),
             pltpu.VMEM((U, 2, 2, H, T), bf16),
@@ -1296,7 +1296,7 @@
             pltpu.VMEM((6,) + norms.shape, f32),
             dma((SLOTS, 4)), dma((U, 4)), dma((U, 4)), dma((U,)), dma((U,)), dma((U,)), dma((U,)),
             dma((U, Z)), dma((U, Z)), dma((U, Z)), dma((U, Z)), dma((U,)), dma((U,)), dma((U,)),
-            dma((U,)), dma((U,)), dma((16,)), dma((2, 2)), dma, dma((3,)), dma((3,)), dma((6,)),
+            dma((U,)), dma((U,)), dma((16,)), dma((2, 2)), dma, dma((2,)), dma((2,)), dma((6,)),
             dma((6,)),
         ],
         compiler_params=pltpu.CompilerParams(
@@ -1311,10 +1311,15 @@
     return UNIT_WEIGHTS[unit], row, column
 
 
-def widen_kernel(sums, *refs):
-    outs, (taken, given, in_sem, out_sem) = refs[:10], refs[10:]
+def finish_kernel(*refs):
+    sums, ours_in, theirs_in, made_in, made_theirs_in, norms = refs[:6]
+    output, grad_hidden, outs, norm_outs = refs[6], refs[7], refs[8:18], refs[18:24]
+    taken, given, ours, theirs, made, made_theirs, theirs_wide = refs[24:31]
+    in_sem, out_sem, row_sem, row_out_sem = refs[31:]
     depth = taken.shape[0]
     shares = [(unit, core) for unit in range(UNITS) for core in range(2)]
+    x = lax.axis_index("narrow")
+    chunk = ours.shape[0] // 2
 
     def fetch(i):
         unit, core = shares[i]
@@ -1328,8 +1333,35 @@
             out_sem.at[i % depth],
         )
 
+    pairs_in = ((ours_in, ours), (theirs_in, theirs), (made_in, made), (made_theirs_in, made_theirs))
+    rows_in = [pltpu.make_async_copy(a, b, row_sem.at[k]) for k, (a, b) in enumerate(pairs_in)]
+
+    def rows_out(src, dst, which, k, at):
+        start = (at if k == 0 else 3 - at) * chunk
+        return pltpu.make_async_copy(
+            src.at[pl.ds(k * chunk, chunk)],
+            dst.at[pl.ds(pl.multiple_of(start, 128), chunk)],
+            row_out_sem.at[which, k],
+        )
+
+    moves = [
+        rows_out(src, dst, which, k, at)
+        for which, (src, dst, at) in enumerate(
+            (
+                (ours, grad_hidden, x),
+                (theirs_wide, grad_hidden, 1 - x),
+                (made, output, x),
+                (made_theirs, output, 1 - x),
+            )
+        )
+        for k in range(2)
+    ]
     for i in range(depth - 1):
         fetch(i).start()
+    for copy in rows_in:
+        copy.start()
+    for i in range(6):
+        norm_outs[i][...] = norms[i]
     for i in range(len(shares)):
         if i + depth - 1 < len(shares):
             fetch(i + depth - 1).start()
@@ -1338,29 +1370,52 @@
             place(i - depth).wait()
         given[i % depth] = taken[i % depth].astype(f32)
         place(i).start()
+        if i == depth:
+            for copy in rows_in:
+                copy.wait()
+            theirs_wide[...] = theirs[...].astype(f32)
+            for copy in moves:
+                copy.start()
     for i in range(len(shares) - depth, len(shares)):
         place(i).wait()
-
-
-def weight_outputs(sums):
+    for copy in moves:
+        copy.wait()
+
+
+def finish(sums, ours, theirs, made, made_theirs, norms):
+    rows, width = ours.shape
     shapes = [(2 * TILE, TILE)] * 3 + [(TILE, 2 * TILE)] + [(2 * TILE, TILE)] * 3
     shapes += [(TILE, 2 * TILE), (2 * TILE, 4 * TILE), (4 * TILE, 2 * TILE)]
     depth = 6
-    return (
-        tuple(pl.pallas_call(
-            widen_kernel,
-            out_shape=[jax.ShapeDtypeStruct(shape, f32) for shape in shapes],
-            in_specs=[pl.BlockSpec(memory_space=pl.ANY)],
-            out_specs=[pl.BlockSpec(memory_space=pl.ANY)] * 10,
+    anywhere = pl.BlockSpec(memory_space=pl.ANY)
+    vmem = pl.BlockSpec(memory_space=pltpu.VMEM)
+    return tuple(
+        pl.pallas_call(
+            finish_kernel,
+            out_shape=[
+                jax.ShapeDtypeStruct((2 * rows, width), bf16),
+                jax.ShapeDtypeStruct((2 * rows, width), f32),
+            ]
+            + [jax.ShapeDtypeStruct(shape, f32) for shape in shapes]
+            + [jax.ShapeDtypeStruct((width,), f32)] * 6,
+            in_specs=[anywhere] * 5 + [vmem],
+            out_specs=[anywhere] * 12 + [vmem] * 6,
             scratch_shapes=[
                 pltpu.VMEM((depth, TILE, TILE), bf16),
                 pltpu.VMEM((depth, TILE, TILE), f32),
+                pltpu.VMEM((rows, width), f32),
+                pltpu.VMEM((rows, width), bf16),
+                pltpu.VMEM((rows, width), bf16),
+                pltpu.VMEM((rows, width), bf16),
+                pltpu.VMEM((rows, width), f32),
                 pltpu.SemaphoreType.DMA((depth,)),
                 pltpu.SemaphoreType.DMA((depth,)),
+                pltpu.SemaphoreType.DMA((4,)),
+                pltpu.SemaphoreType.DMA((4, 2)),
             ],
             compiler_params=pltpu.CompilerParams(vmem_limit_bytes=VMEM_LIMIT),
-            name="widen",
-        )(sums)),
+            name="finish",
+        )(sums, ours, theirs, made, made_theirs, norms)
     )
 
 
@@ -1376,10 +1431,15 @@
 
 def dense_kernel(
     a_cross, first, cotangent, cross_out, gain_two, shift_two, gain_three, shift_three, expand_in, reduce_in,
-    out_ref, g_second, g_across, cross_out_grad, norms, expand_grad, reduce_grad,
+    out_ref, g_second, g_across, cross_out_grad, norms, expand_grad, reduce_grad, made_out,
     expand, reduce, activated, slope, expand_staged, reduce_staged,
-    expand_sem, reduce_sem, expand_out_sem, reduce_out_sem,
+    expand_sem, reduce_sem, expand_out_sem, reduce_out_sem, made_send, made_recv,
 ):
+    me = Place()
+    across = me.at(x=1 - me.x)
+    gain_two, shift_two = as_row(gain_two), as_row(shift_two)
+    gain_three, shift_three = as_row(gain_three), as_row(shift_three)
+    chunk = cotangent.shape[0] // 4
     count = expand.shape[1] // FF_COLUMNS
 
     def piece(c):
@@ -1406,8 +1466,10 @@
     for c in range(count):
         fetch_expand(c).start()
         fetch_reduce(c).start()
+    barrier = pltpu.get_barrier_semaphore()
+    pl.semaphore_signal(barrier, inc=1, device_id=across, device_id_type=MESH)
     second, normal_two, inverse_two = layer_norm(
-        first[...] + dot_nn(a_cross[...], cross_out[...]), gain_two[...], shift_two[...]
+        first[...] + dot_nn(a_cross[...], cross_out[...]), gain_two, shift_two
     )
     second_low = second.astype(bf16)
     total = second
@@ -1419,9 +1481,21 @@
         activated[:, piece(c)] = (pre * phi).astype(bf16)
         fetch_reduce(c).wait()
         total = total + dot_nn(activated[:, piece(c)], reduce[piece(c)])
-    final, normal, inverse = layer_norm(total, gain_three[...], shift_three[...])
+    final, normal, inverse = layer_norm(total, gain_three, shift_three)
     out_ref[...] = final.astype(bf16)
-    grad = cotangent[...].astype(f32)
+    pl.semaphore_wait(barrier, 1)
+    made_copy = pltpu.make_async_remote_copy(
+        src_ref=out_ref, dst_ref=made_out, send_sem=made_send, recv_sem=made_recv,
+        device_id=across, device_id_type=MESH,
+    )
+    made_copy.start()
+    grad = jnp.concatenate(
+        [
+            cotangent[pl.ds(pl.multiple_of(me.x * chunk, 128), chunk)],
+            cotangent[pl.ds(pl.multiple_of((3 - me.x) * chunk, 128), chunk)],
+        ],
+        axis=0,
+    ).astype(f32)
     norms[...] = jnp.zeros_like(norms)
 
     def back(grad, normal, inverse, gain, row):
@@ -1434,7 +1508,7 @@
             - normal * jnp.mean(scaled * normal, axis=-1, keepdims=True)
         )
 
-    grad = back(grad, normal, inverse, gain_three[...], 4)
+    grad = back(grad, normal, inverse, gain_three, 4)
     grad_low = grad.astype(bf16)
     for c in range(count):
         if c >= 2:
@@ -1446,7 +1520,7 @@
         expand_staged[c % 2] = dot_tn(second_low, grad_pre).astype(bf16)
         put_expand(c).start()
         grad = grad + dot_nt(grad_pre, expand[:, piece(c)])
-    grad = back(grad, normal_two, inverse_two, gain_two[...], 2)
+    grad = back(grad, normal_two, inverse_two, gain_two, 2)
     g_second[...] = grad
     grad_low = grad.astype(bf16)
     cross_out_grad[...] = dot_tn(a_cross[...], grad_low).astype(bf16)
@@ -1454,6 +1528,7 @@
     for c in range(count - 2, count):
         put_reduce(c).wait()
         put_expand(c).wait()
+    made_copy.wait()
 
 
 def dense_by_kernel(a_cross, first, cotangent, cross_out, norm_params, expand, reduce):
@@ -1473,9 +1548,10 @@
             jax.ShapeDtypeStruct((8, width), f32),
             jax.ShapeDtypeStruct(expand.shape, bf16),
             jax.ShapeDtypeStruct(reduce.shape, bf16),
+            jax.ShapeDtypeStruct((rows, width), bf16),
         ],
         in_specs=[vmem] * 8 + [anywhere] * 2,
-        out_specs=[vmem] * 5 + [anywhere] * 2,
+        out_specs=[vmem] * 5 + [anywhere] * 3,
         scratch_shapes=[
             pltpu.VMEM(expand.shape, bf16),
             pltpu.VMEM(reduce.shape, bf16),
@@ -1487,10 +1563,14 @@
             dma((count,)),
             dma((2,)),
             dma((2,)),
+            dma,
+            dma,
         ],
-        compiler_params=pltpu.CompilerParams(vmem_limit_bytes=VMEM_LIMIT),
+        compiler_params=pltpu.CompilerParams(
+            collective_id=2, has_side_effects=True, vmem_limit_bytes=VMEM_LIMIT
+        ),
         name="dense",
-    )(a_cross, first, cotangent, cross_out, *[p.reshape(1, width) for p in norm_params], expand, reduce)
+    )(a_cross, first, cotangent, cross_out, *norm_params, expand, reduce)
 
 
 def by_kernels(narrow):
@@ -1576,18 +1656,18 @@
         blend_cross, log_cross, key_cross, value_cross, picked_rows = cross_forward(
             picked, everything, cross_key, cross_value, query_cross
         )
-        output, grad_second_in, grad_blend_cross, cross_out_grad, norms, expand_grad, reduce_grad = (
-            dense_by_kernel(
-                blend_cross,
-                first,
-                own(cotangent),
-                cross_out,
-                (second_gain, second_shift, third_gain, third_shift),
-                expand_weight,
-                reduce_weight,
-            )
-        )
-        sums, grad_mine, grad_theirs, made_theirs, norm_sums = backward_by_kernel(
+        made = dense_by_kernel(
+            blend_cross,
+            first,
+            cotangent,
+            cross_out,
+            (second_gain, second_shift, third_gain, third_shift),
+            expand_weight,
+            reduce_weight,
+        )
+        output, grad_second_in, grad_blend_cross, cross_out_grad, norms = made[:5]
+        expand_grad, reduce_grad, made_theirs = made[5:]
+        sums, grad_mine, grad_theirs, norm_sums = backward_by_kernel(
             expand_grad,
             reduce_grad,
             cross_out_grad,
@@ -1603,7 +1683,7 @@
             grad_second_in,
             first_normal,
             first_inverse,
-            first_gain.reshape(1, width),
+            first_gain,
             blend_self,
             self_out,
             query_self,
@@ -1614,29 +1694,10 @@
             self_query,
             self_key,
             self_value,
-            output,
             norms,
         )
 
-        def ordered(ours, others):
-            a, b = ours[:chunk], ours[chunk:]
-            c, d = others[:chunk], others[chunk:]
-            first_one = at == 0
-            return jnp.concatenate(
-                [
-                    jnp.where(first_one, a, c),
-                    jnp.where(first_one, c, a),
-                    jnp.where(first_one, d, b),
-                    jnp.where(first_one, b, d),
-                ],
-                axis=0,
-            )
-
-        return (
-            (ordered(output, made_theirs), ordered(grad_mine, grad_theirs.astype(f32)))
-            + weight_outputs(sums)[0]
-            + tuple(norm_sums[i] for i in range(6))
-        )
+        return finish(sums, grad_mine, grad_theirs, output, made_theirs, norm_sums)
 
     everything, full = gather_all(
         encoded,

time: 454 us -> 438 us (0.965)
  local copies, waits for them, and re-layouts: 7.28 us -> 1.37 us
  other arithmetic: 5.76 us -> 0.01 us
    pallas_call x1, Pallas kernels: 174 us -> 160 us  [backward_by_kernel(): pl.pallas_call(backward_kernel, out_shape=[jax.ShapeDtypeStruct((U, 2, T,...]
    pallas_call x1, Pallas kernels: 29.8 us -> 35.9 us  [dense_by_kernel(): pl.pallas_call(dense_kernel, out_shape=[jax.ShapeDtypeStruct((rows, width...]
    reshape x6 -> x0, local copies, waits for them, and re-layouts: 4.85 us -> none  [the longest x4 2.32 us: dense_by_kernel(): p.reshape(1, width)]
where the time goes in v4:
time: 438 us; the launch traced here: 430 us
  Pallas kernels  427 us (97%)
    pallas_call x1, Pallas kernels, forward_by_kernel(): pl.pallas_call(functools.partial(forward_kernel, a_rows, b_rows), out_sha...  183 us
    pallas_call x1, Pallas kernels, backward_by_kernel(): pl.pallas_call(backward_kernel, out_shape=[jax.ShapeDtypeStruct((U, 2, T,...  160 us
    pallas_call x1, Pallas kernels, dense_by_kernel(): pl.pallas_call(dense_kernel, out_shape=[jax.ShapeDtypeStruct((rows, width...  35.9 us
    pallas_call x1, Pallas kernels, cross_forward(): pl.pallas_call(cross_forward_kernel, grid_spec=pltpu.PrefetchScalarGridSp...  33.4 us
    pallas_call x1, Pallas kernels, finish(): pl.pallas_call(finish_kernel, out_shape=[jax.ShapeDtypeStruct((2 * rows,...  14.1 us

profile of v4, /device:TPU:0, one launch (start us, length us, event | category | flops | bytes accessed | tf_op | source)
XLA Modules:
  0.0 429.7 jit_solution(13225059310385074940)
XLA Ops:
  0.7 0.8 constant_dynamic-slice_fusion.1
  1.4 0.6 reshape.39.picked_ref
  2.0 183.4 %forward.1 = (bf16[24576,768]{1,0:T(8,128)(2,1)}, bf16[768,768]{1,0:T(8,128)(2,1)}, bf16[768,768]{1,0:T(8,128)(2,1)}, bf16[768,768]{1,0:T(8,128)(2,1)}, bf16[768...) custom-call(bf16[1536,768]{1,0:T(8,128)(2,1)} %refs_0_.1, ...), custom_call_target="tpu_custom_call" | custom-call | tf_op jit(solution)/shard_map/forward/pallas_call | solution.py:751
  185.4 33.4 %cross_forward.1 = (bf16[512,768]{1,0:T(8,128)(2,1)}, f32[4,6,256]{2,1,0:T(8,128)}, bf16[4096,768]{1,0:T(8,128)(2,1)}, bf16[4096,768]{1,0:T(8,128)(2,1)}, bf16[4096,768]{1,0:T(8,128)(2,1)}) custom-call(s32[32]{0:T(128)} %reshape.39.picked_ref, bf16[24576,768]{1,0:T(8,128)(2,1)} %get-tuple-element.56.refs_0_.refs_1_.refs_2_.refs_3_.refs_4_.refs_5_.refs_6_.refs_7_, ...), custom_call_target="tpu_custom_call" | custom-call | tf_op jit(solution)/shard_map/cross_forward/pallas_call | solution.py:276
  218.8 35.9 %dense.1 = (bf16[512,768]{1,0:T(8,128)(2,1)}, f32[512,768]{1,0:T(8,128)}, bf16[512,768]{1,0:T(8,128)(2,1)}, bf16[768,768]{1,0:T(8,128)(2,1)}, f32[8,768]{1,0:T(8...) custom-call(bf16[512,768]{1,0:T(8,128)(2,1)} %get-tuple-element.60.a_cross.refs_7_, ...), custom_call_target="tpu_custom_call" | custom-call | tf_op jit(solution)/shard_map/dense/pallas_call | solution.py:1541
  254.7 160.4 %backward.1 = (bf16[16,2,384,384]{3,2,1,0:T(8,128)(2,1)}, f32[512,768]{1,0:T(8,128)}, bf16[512,768]{1,0:T(8,128)(2,1)}, f32[8,768]{1,0:T(8,128)}) custom-call(bf16[768,3072]{1,0:T(8,128)(2,1)} %get-tuple-element.65.refs_0_, bf16[3072,768]{1,0:T(8,128)(2,1)} %get-tuple-element.66.refs_1_, bf16[768,768]{1,0:T(8,128)(2,1)} %get-tuple-element.67.refs_2_, ...), custom_call_target="tpu_custom_call" | custom-call | tf_op jit(solution)/shard_map/backward/pallas_call | solution.py:1268
  415.1 14.1 %finish.1 = (bf16[1024,768]{1,0:T(8,128)(2,1)}, f32[1024,768]{1,0:T(8,128)}, f32[768,384]{1,0:T(8,128)}, f32[768,384]{1,0:T(8,128)}, f32[768,384]{1,0:T(8,128)},...) custom-call(bf16[16,2,384,384]{3,2,1,0:T(8,128)(2,1)} %get-tuple-ele, ...), custom_call_target="tpu_custom_call" | custom-call | tf_op jit(solution)/shard_map/finish/pallas_call | solution.py:1393
  (1 shorter events, 0.0 us)

commit v5 on v4

--- a/solution.py
+++ b/solution.py
@@ -98,18 +98,35 @@
     return stack_heads(pair_rows.astype(f32) * HEAD_DIM**-0.5)
 
 
+KEY_ROWS = 128
+
+
+def scores_of(keys, stacked, start, edge):
+    part = dot_nt(keys[start : start + KEY_ROWS], stacked)
+    if edge is not None and start + KEY_ROWS == keys.shape[0]:
+        part = jnp.where(edge, part, -1e30)
+    return part
+
+
+def by_rows(part, reduce):
+    return reduce(part.reshape(KEY_ROWS // 8, 8, part.shape[1]), axis=0)
+
+
 def pair_forward(queries, keys, values, edge):
     stacked = scaled_heads(queries)
-    scores = dot_nt(keys, stacked)
-    if edge is not None:
-        split = keys.shape[0] - edge.shape[0]
-        last = jnp.where(edge, scores[split:], -1e30)
-        scores = jnp.concatenate([scores[:split], last], axis=0) if split else last
-    top = jnp.max(scores, axis=0, keepdims=True)
-    raised = jnp.exp(scores - top)
-    total = jnp.sum(raised, axis=0, keepdims=True)
-    blended = dot_tn(values, raised.astype(bf16)) / total
-    return merge_heads(blended).astype(bf16), top + jnp.log(total)
+    starts = range(0, keys.shape[0], KEY_ROWS)
+    scores = [scores_of(keys, stacked, start, edge) for start in starts]
+    top = by_rows(scores[0], jnp.max)
+    for part in scores[1:]:
+        top = jnp.maximum(top, by_rows(part, jnp.max))
+    top = jnp.max(top, axis=0, keepdims=True)
+    total, blended = 0.0, 0.0
+    for start, part in zip(starts, scores):
+        raised = jnp.exp(part - top)
+        total = total + by_rows(raised, jnp.sum)
+        blended = blended + dot_tn(values[start : start + KEY_ROWS], raised.astype(bf16))
+    total = jnp.sum(total, axis=0, keepdims=True)
+    return merge_heads(blended / total).astype(bf16), top + jnp.log(total)
 
 
 def pair_backward(queries, keys, values, edge, log_total, blended, grad_blend):
@@ -890,7 +907,7 @@
         return remote(piece, piece, gc_send.at[u], gc_recv.at[u], sibling)
 
     def plus(a, b):
-        return (a.astype(f32) + b.astype(f32)).astype(bf16)
+        return a + b
 
     def by_order(u, first, second):
         if isinstance(u, int):
@@ -901,9 +918,20 @@
 
     def stage_core(u):
         slot = rem(u, SLOTS)
-        for plane in range(2):
-            for part in range(2):
-                core_copy(own.at[slot, plane, part], u, plane, part).wait_recv()
+        early_one = u < len(ready)
+
+        def arrived():
+            for plane, part in corners:
+                piece = own.at[slot, plane, part]
+                pltpu.make_async_copy(piece, piece, own_sem.at[slot, plane * 2 + part]).wait()
+
+        if isinstance(u, int):
+            if early_one:
+                arrived()
+        else:
+            pl.when(early_one)(arrived)
+        for plane, part in corners:
+            core_copy(own.at[slot, plane, part], u, plane, part).wait_recv()
         own[slot] = plus(own[slot], from_core[u])
         by_order(u, lambda: a_first(u, slot).start(), lambda: a_second(u, slot).start())
 
@@ -998,21 +1026,19 @@
     for copy in early:
         copy.start()
     ready = [(expand_grad, u) for u in range(4)] + [(reduce_grad, u) for u in range(4, 8)]
+    ready.append((cross_out_grad, 8))
     corners = [(plane, part) for plane in range(2) for part in range(2)]
     for ref, unit in ready:
         for plane, part in corners:
             own_copy(ref, unit, plane, part).start()
     me.greet()
-    for ref, unit in ready + [(cross_out_grad, 8)]:
+    for ref, unit in ready:
         for plane, part in corners:
             to_core(ref, unit, plane, part).start()
     both_sums = pool32
     both_sums[...] = jnp.zeros_like(both_sums)
     for copy in early[:3]:
         copy.wait()
-    for ref, unit in ready:
-        for plane, part in corners:
-            own_copy(ref, unit, plane, part).wait()
 
     def at_row(row):
         return pl.ds(pl.multiple_of(row, 128), BLOCK_ROWS)
@@ -1079,8 +1105,6 @@
     late = [load(q_self, QS, 7), load(k_self, KS, 8), load(v_self, VS, 9), load(hidden, HIDDEN, 10)]
     for copy in late:
         copy.start()
-    for plane, part in corners:
-        own_copy(cross_out_grad, 8, plane, part).start()
     staged[1] = both_sums[pl.ds(0, width)].astype(bf16)
     hand_over(9)
     tick(6)
@@ -1113,8 +1137,6 @@
     pool32[pl.ds(2 * rows, rows)] = grad_in
     grad_low = grad_in.astype(bf16)
     pool[pl.ds(DA, rows)] = dot_nt(grad_low, pool[pl.ds(SELF_OUT, width)]).astype(bf16)
-    for plane, part in corners:
-        own_copy(cross_out_grad, 8, plane, part).wait()
     tick(8)
     handed_over(10)
     staged[0] = dot_tn(pool[pl.ds(A_SELF, rows)], grad_low).astype(bf16)
@@ -1187,6 +1209,19 @@
         copy.start()
 
     left(11)
+    for copy in last_loads:
+        copy.wait()
+
+    def row_grads(at_chunk):
+        dk = pool[pl.ds(pl.multiple_of(DK + at_chunk * chunk, 128), chunk)]
+        dv = pool[pl.ds(pl.multiple_of(DV + at_chunk * chunk, 128), chunk)]
+        return dot_nt(dk, pool[pl.ds(WK, width)]) + dot_nt(dv, pool[pl.ds(WV, width)])
+
+    theirs[pl.ds(0, chunk)] = row_grads(1 - x).astype(bf16)
+    theirs[pl.ds(chunk, chunk)] = row_grads(2 + x).astype(bf16)
+    rows_copy = remote(theirs, rows_in, extra_send.at[0], extra_recv.at[0], across)
+    got_copy = remote(rows_got, theirs_out, extra_send.at[1], extra_recv.at[1], across)
+    rows_copy.start()
     low_rows = pl.ds(pl.multiple_of(HIDDEN + x * chunk, 128), chunk)
     high_rows = pl.ds(pl.multiple_of(HIDDEN + (3 - x) * chunk, 128), chunk)
     all_rows = hidden.shape[0]
@@ -1210,19 +1245,6 @@
     handed_over(14)
     handed_over(15)
 
-    for copy in last_loads:
-        copy.wait()
-
-    def row_grads(at_chunk):
-        dk = pool[pl.ds(pl.multiple_of(DK + at_chunk * chunk, 128), chunk)]
-        dv = pool[pl.ds(pl.multiple_of(DV + at_chunk * chunk, 128), chunk)]
-        return dot_nt(dk, pool[pl.ds(WK, width)]) + dot_nt(dv, pool[pl.ds(WV, width)])
-
-    theirs[pl.ds(0, chunk)] = row_grads(1 - x).astype(bf16)
-    theirs[pl.ds(chunk, chunk)] = row_grads(2 + x).astype(bf16)
-    rows_copy = remote(theirs, rows_in, extra_send.at[0], extra_recv.at[0], across)
-    got_copy = remote(rows_got, theirs_out, extra_send.at[1], extra_recv.at[1], across)
-    rows_copy.start()
     tick(14)
     for k, at_chunk in enumerate((x, 3 - x)):
         piece = pl.ds(k * chunk, chunk)
@@ -1249,7 +1271,7 @@
 
     lax.fori_loop(15, LAST_TICK + 1, last_step, 0)
     got_copy.wait()
-    for ref, unit in ready + [(cross_out_grad, 8)]:
+    for ref, unit in ready:
         for plane, part in corners:
             to_core(ref, unit, plane, part).wait_send()
 

time: 438 us -> 432 us (0.986)
  Pallas kernels: 427 us -> 422 us
    pallas_call x1, Pallas kernels: 33.4 us -> 27 us  [cross_forward(): pl.pallas_call(cross_forward_kernel, grid_spec=pltpu.PrefetchScalarGridSp...]
where the time goes in v5:
time: 432 us; the launch traced here: 424 us
  Pallas kernels  422 us (98%)
    pallas_call x1, Pallas kernels, forward_by_kernel(): pl.pallas_call(functools.partial(forward_kernel, a_rows, b_rows), out_sha...  183 us
    pallas_call x1, Pallas kernels, backward_by_kernel(): pl.pallas_call(backward_kernel, out_shape=[jax.ShapeDtypeStruct((U, 2, T,...  158 us
    pallas_call x1, Pallas kernels, dense_by_kernel(): pl.pallas_call(dense_kernel, out_shape=[jax.ShapeDtypeStruct((rows, width...  38.8 us
    pallas_call x1, Pallas kernels, cross_forward(): pl.pallas_call(cross_forward_kernel, grid_spec=pltpu.PrefetchScalarGridSp...  27 us
    pallas_call x1, Pallas kernels, finish(): pl.pallas_call(finish_kernel, out_shape=[jax.ShapeDtypeStruct((2 * rows,...  14.1 us

profile of v5, /device:TPU:0, one launch (start us, length us, event | category | flops | bytes accessed | tf_op | source)
XLA Modules:
  0.0 424.2 jit_solution(2935859164154702166)
XLA Ops:
  0.7 0.8 constant_dynamic-slice_fusion.1
  1.4 0.6 reshape.39.picked_ref
  2.0 183.4 %forward.1 = (bf16[24576,768]{1,0:T(8,128)(2,1)}, bf16[768,768]{1,0:T(8,128)(2,1)}, bf16[768,768]{1,0:T(8,128)(2,1)}, bf16[768,768]{1,0:T(8,128)(2,1)}, bf16[768...) custom-call(bf16[1536,768]{1,0:T(8,128)(2,1)} %refs_0_.1, ...), custom_call_target="tpu_custom_call" | custom-call | tf_op jit(solution)/shard_map/forward/pallas_call | solution.py:768
  185.4 27.0 %cross_forward.1 = (bf16[512,768]{1,0:T(8,128)(2,1)}, f32[4,6,256]{2,1,0:T(8,128)}, bf16[4096,768]{1,0:T(8,128)(2,1)}, bf16[4096,768]{1,0:T(8,128)(2,1)}, bf16[4096,768]{1,0:T(8,128)(2,1)}) custom-call(s32[32]{0:T(128)} %reshape.39.picked_ref, bf16[24576,768]{1,0:T(8,128)(2,1)} %get-tuple-element.56.refs_0_.refs_1_.refs_2_.refs_3_.refs_4_.refs_5_.refs_6_.refs_7_, ...), custom_call_target="tpu_custom_call" | custom-call | tf_op jit(solution)/shard_map/cross_forward/pallas_call | solution.py:293
  212.4 38.8 %dense.1 = (bf16[512,768]{1,0:T(8,128)(2,1)}, f32[512,768]{1,0:T(8,128)}, bf16[512,768]{1,0:T(8,128)(2,1)}, bf16[768,768]{1,0:T(8,128)(2,1)}, f32[8,768]{1,0:T(8...) custom-call(bf16[512,768]{1,0:T(8,128)(2,1)} %get-tuple-element.60.a_cross.refs_7_, ...), custom_call_target="tpu_custom_call" | custom-call | tf_op jit(solution)/shard_map/dense/pallas_call | solution.py:1563
  251.2 158.4 %backward.1 = (bf16[16,2,384,384]{3,2,1,0:T(8,128)(2,1)}, f32[512,768]{1,0:T(8,128)}, bf16[512,768]{1,0:T(8,128)(2,1)}, f32[8,768]{1,0:T(8,128)}) custom-call(bf16[768,3072]{1,0:T(8,128)(2,1)} %get-tuple-element.65.refs_0_, bf16[3072,768]{1,0:T(8,128)(2,1)} %get-tuple-element.66.refs_1_, bf16[768,768]{1,0:T(8,128)(2,1)} %get-tuple-element.67.refs_2_, ...), custom_call_target="tpu_custom_call" | custom-call | tf_op jit(solution)/shard_map/backward/pallas_call | solution.py:1290
  409.7 14.1 %finish.1 = (bf16[1024,768]{1,0:T(8,128)(2,1)}, f32[1024,768]{1,0:T(8,128)}, f32[768,384]{1,0:T(8,128)}, f32[768,384]{1,0:T(8,128)}, f32[768,384]{1,0:T(8,128)},...) custom-call(bf16[16,2,384,384]{3,2,1,0:T(8,128)(2,1)} %get-tuple-ele, ...), custom_call_target="tpu_custom_call" | custom-call | tf_op jit(solution)/shard_map/finish/pallas_call | solution.py:1415
  (1 shorter events, 0.0 us)

commit v6 on v5

--- a/solution.py
+++ b/solution.py
@@ -1079,7 +1079,7 @@
             both_sums[pl.ds(0, width)] += dot_tn(pool[pl.ds(E, keys)], both[:, :width])
             both_sums[pl.ds(width, width)] += dot_tn(pool[pl.ds(E, keys)], both[:, width:])
 
-        pl.when(lax.rem(i, 4) == 3)(lambda: tick(lax.div(i, 4)))
+        pl.when(lax.rem(i, 4) == 1)(lambda: tick(lax.div(i, 4)))
         return carry
 
     lax.fori_loop(0, blocks * pairs, cross_step, 0)
@@ -1441,7 +1441,7 @@
     )
 
 
-FF_COLUMNS = 512
+FF_COLUMNS = 1024
 
 
 def layer_norm(summed, norm_gain, norm_shift):

time: 432 us -> 428 us (level)
  no operation moved by 1% of the time
where the time goes in v6:
time: 428 us; the launch traced here: 420 us
  Pallas kernels  418 us (98%)
    pallas_call x1, Pallas kernels, forward_by_kernel(): pl.pallas_call(functools.partial(forward_kernel, a_rows, b_rows), out_sha...  183 us
    pallas_call x1, Pallas kernels, backward_by_kernel(): pl.pallas_call(backward_kernel, out_shape=[jax.ShapeDtypeStruct((U, 2, T,...  157 us
    pallas_call x1, Pallas kernels, dense_by_kernel(): pl.pallas_call(dense_kernel, out_shape=[jax.ShapeDtypeStruct((rows, width...  36.5 us
    pallas_call x1, Pallas kernels, cross_forward(): pl.pallas_call(cross_forward_kernel, grid_spec=pltpu.PrefetchScalarGridSp...  27 us
    pallas_call x1, Pallas kernels, finish(): pl.pallas_call(finish_kernel, out_shape=[jax.ShapeDtypeStruct((2 * rows,...  14.1 us

profile of v6, /device:TPU:0, one launch (start us, length us, event | category | flops | bytes accessed | tf_op | source)
XLA Modules:
  0.0 420.2 jit_solution(12244335206310238086)
XLA Ops:
  0.7 0.8 constant_dynamic-slice_fusion.1
  1.4 0.6 reshape.39.picked_ref
  2.0 183.4 %forward.1 = (bf16[24576,768]{1,0:T(8,128)(2,1)}, bf16[768,768]{1,0:T(8,128)(2,1)}, bf16[768,768]{1,0:T(8,128)(2,1)}, bf16[768,768]{1,0:T(8,128)(2,1)}, bf16[768...) custom-call(bf16[1536,768]{1,0:T(8,128)(2,1)} %refs_0_.1, ...), custom_call_target="tpu_custom_call" | custom-call | tf_op jit(solution)/shard_map/forward/pallas_call | solution.py:768
  185.4 27.0 %cross_forward.1 = (bf16[512,768]{1,0:T(8,128)(2,1)}, f32[4,6,256]{2,1,0:T(8,128)}, bf16[4096,768]{1,0:T(8,128)(2,1)}, bf16[4096,768]{1,0:T(8,128)(2,1)}, bf16[4096,768]{1,0:T(8,128)(2,1)}) custom-call(s32[32]{0:T(128)} %reshape.39.picked_ref, bf16[24576,768]{1,0:T(8,128)(2,1)} %get-tuple-element.56.refs_0_.refs_1_.refs_2_.refs_3_.refs_4_.refs_5_.refs_6_.refs_7_, ...), custom_call_target="tpu_custom_call" | custom-call | tf_op jit(solution)/shard_map/cross_forward/pallas_call | solution.py:293
  212.4 36.5 %dense.1 = (bf16[512,768]{1,0:T(8,128)(2,1)}, f32[512,768]{1,0:T(8,128)}, bf16[512,768]{1,0:T(8,128)(2,1)}, bf16[768,768]{1,0:T(8,128)(2,1)}, f32[8,768]{1,0:T(8...) custom-call(bf16[512,768]{1,0:T(8,128)(2,1)} %get-tuple-element.60.a_cross.refs_7_, ...), custom_call_target="tpu_custom_call" | custom-call | tf_op jit(solution)/shard_map/dense/pallas_call | solution.py:1563
  248.9 156.7 %backward.1 = (bf16[16,2,384,384]{3,2,1,0:T(8,128)(2,1)}, f32[512,768]{1,0:T(8,128)}, bf16[512,768]{1,0:T(8,128)(2,1)}, f32[8,768]{1,0:T(8,128)}) custom-call(bf16[768,3072]{1,0:T(8,128)(2,1)} %get-tuple-element.65.refs_0_, bf16[3072,768]{1,0:T(8,128)(2,1)} %get-tuple-element.66.refs_1_, bf16[768,768]{1,0:T(8,128)(2,1)} %get-tuple-element.67.refs_2_, ...), custom_call_target="tpu_custom_call" | custom-call | tf_op jit(solution)/shard_map/backward/pallas_call | solution.py:1290
  405.6 14.1 %finish.1 = (bf16[1024,768]{1,0:T(8,128)(2,1)}, f32[1024,768]{1,0:T(8,128)}, f32[768,384]{1,0:T(8,128)}, f32[768,384]{1,0:T(8,128)}, f32[768,384]{1,0:T(8,128)},...) custom-call(bf16[16,2,384,384]{3,2,1,0:T(8,128)(2,1)} %get-tuple-ele, ...), custom_call_target="tpu_custom_call" | custom-call | tf_op jit(solution)/shard_map/finish/pallas_call | solution.py:1415
  (1 shorter events, 0.0 us)

commit v7 on v6

--- a/solution.py
+++ b/solution.py
@@ -1079,7 +1079,7 @@
             both_sums[pl.ds(0, width)] += dot_tn(pool[pl.ds(E, keys)], both[:, :width])
             both_sums[pl.ds(width, width)] += dot_tn(pool[pl.ds(E, keys)], both[:, width:])
 
-        pl.when(lax.rem(i, 4) == 1)(lambda: tick(lax.div(i, 4)))
+        pl.when(lax.rem(i, 4) == 0)(lambda: tick(lax.div(i, 4)))
         return carry
 
     lax.fori_loop(0, blocks * pairs, cross_step, 0)
@@ -1408,7 +1408,7 @@
     rows, width = ours.shape
     shapes = [(2 * TILE, TILE)] * 3 + [(TILE, 2 * TILE)] + [(2 * TILE, TILE)] * 3
     shapes += [(TILE, 2 * TILE), (2 * TILE, 4 * TILE), (4 * TILE, 2 * TILE)]
-    depth = 6
+    depth = 8
     anywhere = pl.BlockSpec(memory_space=pl.ANY)
     vmem = pl.BlockSpec(memory_space=pltpu.VMEM)
     return tuple(

time: 428 us -> 427 us (level)
  the two profiles are of different devices: /device:TPU:0 before, /device:TPU:27 now
where the time goes in v7:
time: 427 us; the launch traced here: 420 us
  Pallas kernels  417 us (98%)
    pallas_call x1, Pallas kernels, forward_by_kernel(): pl.pallas_call(functools.partial(forward_kernel, a_rows, b_rows), out_sha...  180 us
    pallas_call x1, Pallas kernels, backward_by_kernel(): pl.pallas_call(backward_kernel, out_shape=[jax.ShapeDtypeStruct((U, 2, T,...  159 us
    pallas_call x1, Pallas kernels, dense_by_kernel(): pl.pallas_call(dense_kernel, out_shape=[jax.ShapeDtypeStruct((rows, width...  36.5 us
    pallas_call x1, Pallas kernels, cross_forward(): pl.pallas_call(cross_forward_kernel, grid_spec=pltpu.PrefetchScalarGridSp...  27 us
    pallas_call x1, Pallas kernels, finish(): pl.pallas_call(finish_kernel, out_shape=[jax.ShapeDtypeStruct((2 * rows,...  13.7 us

profile of v7, /device:TPU:27, one launch (start us, length us, event | category | flops | bytes accessed | tf_op | source)
XLA Modules:
  0.0 419.5 jit_solution(17127672404606671754)
XLA Ops:
  0.7 0.8 constant_dynamic-slice_fusion.1
  1.4 0.6 reshape.39.picked_ref
  2.0 180.4 %forward.1 = (bf16[24576,768]{1,0:T(8,128)(2,1)}, bf16[768,768]{1,0:T(8,128)(2,1)}, bf16[768,768]{1,0:T(8,128)(2,1)}, bf16[768,768]{1,0:T(8,128)(2,1)}, bf16[768...) custom-call(bf16[1536,768]{1,0:T(8,128)(2,1)} %refs_0_.1, ...), custom_call_target="tpu_custom_call" | custom-call | tf_op jit(solution)/shard_map/forward/pallas_call | solution.py:768
  182.4 27.0 %cross_forward.1 = (bf16[512,768]{1,0:T(8,128)(2,1)}, f32[4,6,256]{2,1,0:T(8,128)}, bf16[4096,768]{1,0:T(8,128)(2,1)}, bf16[4096,768]{1,0:T(8,128)(2,1)}, bf16[4096,768]{1,0:T(8,128)(2,1)}) custom-call(s32[32]{0:T(128)} %reshape.39.picked_ref, bf16[24576,768]{1,0:T(8,128)(2,1)} %get-tuple-element.56.refs_0_.refs_1_.refs_2_.refs_3_.refs_4_.refs_5_.refs_6_.refs_7_, ...), custom_call_target="tpu_custom_call" | custom-call | tf_op jit(solution)/shard_map/cross_forward/pallas_call | solution.py:293
  209.4 36.5 %dense.1 = (bf16[512,768]{1,0:T(8,128)(2,1)}, f32[512,768]{1,0:T(8,128)}, bf16[512,768]{1,0:T(8,128)(2,1)}, bf16[768,768]{1,0:T(8,128)(2,1)}, f32[8,768]{1,0:T(8...) custom-call(bf16[512,768]{1,0:T(8,128)(2,1)} %get-tuple-element.60.a_cross.refs_7_, ...), custom_call_target="tpu_custom_call" | custom-call | tf_op jit(solution)/shard_map/dense/pallas_call | solution.py:1563
  245.9 159.4 %backward.1 = (bf16[16,2,384,384]{3,2,1,0:T(8,128)(2,1)}, f32[512,768]{1,0:T(8,128)}, bf16[512,768]{1,0:T(8,128)(2,1)}, f32[8,768]{1,0:T(8,128)}) custom-call(bf16[768,3072]{1,0:T(8,128)(2,1)} %get-tuple-element.65.refs_0_, bf16[3072,768]{1,0:T(8,128)(2,1)} %get-tuple-element.66.refs_1_, bf16[768,768]{1,0:T(8,128)(2,1)} %get-tuple-element.67.refs_2_, ...), custom_call_target="tpu_custom_call" | custom-call | tf_op jit(solution)/shard_map/backward/pallas_call | solution.py:1290
  405.4 13.7 %finish.1 = (bf16[1024,768]{1,0:T(8,128)(2,1)}, f32[1024,768]{1,0:T(8,128)}, f32[768,384]{1,0:T(8,128)}, f32[768,384]{1,0:T(8,128)}, f32[768,384]{1,0:T(8,128)},...) custom-call(bf16[16,2,384,384]{3,2,1,0:T(8,128)(2,1)} %get-tuple-ele, ...), custom_call_target="tpu_custom_call" | custom-call | tf_op jit(solution)/shard_map/finish/pallas_call | solution.py:1415
  (1 shorter events, 0.0 us)
